TPU v7x, 32 devices: a whole 2x2x4 slice. The times are simulated.
32 devices in a mesh: gx: 4 (over z), gy: 4 (over y, x), gz: 2 (over core).
Axes of the slice: x: 2, y: 2, z: 4, core: 2. Of those that a mesh axis runs over, the one named last changes fastest.
Arguments:
- fine_residual: bfloat16 [4, 4, 2, 2, 2, 12, 32, 256], P('gx', 'gy', 'gz'), may hold values from -6 to 6
- candidates: bfloat16 [4, 4, 2, 2, 48, 2, 12, 256], P('gx', 'gy', 'gz'), may hold values from -0.29882812 to 0.29882812
- vector_pick: int32 [32], replicated, may hold values from 0 to 47, as said below
- coarse_links: float32 [4, 4, 2, 2, 9, 64, 128], P(None, 'gy', 'gz'), may hold values from -0.1875 to 0.1875
Outputs:
- correction: bfloat16 [4, 4, 2, 2, 2, 12, 32, 256], P('gx', 'gy', 'gz')
- coarse_error: float32 [4, 4, 2, 2, 2, 64, 32], P('gx', 'gy', 'gz')
Inputs may be any that keep to these rules, and one draw needn't show every extreme that they name: `vector_pick`: 32 distinct indices of candidate vectors.
All inputs are finite; a program needn't handle non-finite values.
Results may differ from a plain program's by a relative error of at most 0.0049.
Values sent between devices are 32-bit elements; how exact they have to be, the bound alone decides.
No kernel may reach another device: no remote copies, remote signals or barrier semaphores. Data moves between devices by JAX's collectives and lax.ppermute only.
A program may use at most 64 MiB of HBM per device.

v0:
```python
import jax
import jax.numpy as jnp
from jax import lax
from jax.sharding import PartitionSpec as P

APPLIES = 2


def extended(shard, sides, width):
    for axis, dim in sides:
        devices, length = (lax.axis_size(axis), shard.shape[dim])
        up = [(i, (i + 1) % devices) for i in range(devices)]
        down = [(j, i) for i, j in up]
        last = lax.slice_in_dim(shard, length - width, length, axis=dim)
        initial = lax.slice_in_dim(shard, 0, width, axis=dim)
        before = lax.ppermute(last, axis, up)
        after = lax.ppermute(initial, axis, down)
        shard = jnp.concatenate([before, shard, after], axis=dim)
    return shard


def restrict_local(chosen, fine_part):
    shaped = chosen.reshape(
        (chosen.shape[0], chosen.shape[1], 2, 2, chosen.shape[3] // 2, chosen.shape[4])
    )
    source = fine_part.reshape(
        (fine_part.shape[0], 2, 2, fine_part.shape[2] // 2, fine_part.shape[3], fine_part.shape[4])
    )
    partial_terms = jnp.einsum(
        "tkqhcs,tphcrs->thkqpr", shaped, source, preferred_element_type=jnp.float32
    )
    real_part = partial_terms[:, :, :, 0, 0] + partial_terms[:, :, :, 1, 1]
    imag_part = partial_terms[:, :, :, 0, 1] - partial_terms[:, :, :, 1, 0]
    merged_shape = (real_part.shape[0], real_part.shape[1] * real_part.shape[2], real_part.shape[3])
    return jnp.stack([real_part.reshape(merged_shape), imag_part.reshape(merged_shape)], axis=1)


def prolong_local(chosen, error_half):
    shaped = chosen.reshape(
        (chosen.shape[0], chosen.shape[1], 2, 2, chosen.shape[3] // 2, chosen.shape[4])
    )
    coarse = error_half.reshape(
        (error_half.shape[0], 2, 2, error_half.shape[2] // 2, error_half.shape[3])
    )
    grid = jnp.einsum("tkqhcs,tphkr->tqphcrs", shaped, coarse, preferred_element_type=jnp.float32)
    real_part = grid[:, 0, 0] - grid[:, 1, 1]
    imag_part = grid[:, 0, 1] + grid[:, 1, 0]
    merged_shape = (real_part.shape[0], chosen.shape[3], real_part.shape[3], real_part.shape[4])
    stacked = jnp.stack([real_part.reshape(merged_shape), imag_part.reshape(merged_shape)], axis=1)
    return stacked.astype(jnp.bfloat16)


def neighbours(iterate, padded):
    shifted = [iterate, jnp.roll(iterate, -1, 0), jnp.roll(iterate, 1, 0)]
    shifted = shifted + [
        padded[:, 2:, 1:-1],
        padded[:, :-2, 1:-1],
        padded[:, 1:-1, 2:],
        padded[:, 1:-1, :-2],
    ]
    shifted = shifted + [jnp.roll(iterate, -1, 3), jnp.roll(iterate, 1, 3)]
    return shifted


def apply_operator(local_links, shifted):
    stacked = jnp.stack([shifted[0]] + [-vector for vector in shifted[1:]], axis=4)
    real_part = stacked[:, :, :, :, :, 0]
    imag_part = stacked[:, :, :, :, :, 1]
    columns = jnp.concatenate(
        [
            jnp.concatenate([real_part, -imag_part], axis=-2),
            jnp.concatenate([imag_part, real_part], axis=-2),
        ],
        axis=-1,
    )
    product = jnp.einsum(
        "abcdeij,abcdejr->abcdir",
        local_links,
        columns,
        precision=lax.Precision.HIGHEST,
        preferred_element_type=jnp.float32,
    )
    split_at = real_part.shape[-1]
    return shifted[0] + jnp.stack([product[..., :split_at], product[..., split_at:]], axis=4)


def on_device(fine_residual, candidates, vector_pick, coarse_links):
    chosen = jnp.take(candidates[0, 0, 0], vector_pick, axis=1)
    restricted = restrict_local(chosen, fine_residual[0, 0, 0])[None, None, None]
    line_source = lax.all_to_all(restricted, "gx", split_axis=6, concat_axis=0, tiled=True)
    iterate = 0.5 * line_source
    for repeat in range(APPLIES):
        padded = extended(iterate, (("gy", 1), ("gz", 2)), 1)
        image = apply_operator(coarse_links, neighbours(iterate, padded))
        iterate = iterate + 0.5 * (line_source - image)
    coarse_error = lax.all_to_all(iterate, "gx", split_axis=0, concat_axis=6, tiled=True)
    error_half = coarse_error[0, 0, 0].astype(jnp.bfloat16)
    correction = prolong_local(chosen, error_half)[None, None, None]
    return (correction, coarse_error)


def solution(mesh):
    placed = (
        P("gx", "gy", "gz", None, None, None, None, None),
        P("gx", "gy", "gz", None, None, None, None, None),
        P(),
        P(None, "gy", "gz", None, None, None, None),
    )
    return jax.shard_map(
        on_device,
        mesh=mesh,
        in_specs=placed,
        out_specs=(
            P("gx", "gy", "gz", None, None, None, None, None),
            P("gx", "gy", "gz", None, None, None, None),
        ),
        check_vma=False,
    )
```

profile of v0, /device:TPU:0, one launch (start us, length us, event | category | flops | bytes accessed | tf_op | source)
XLA Modules:
  0.0 54.9 jit_solution(17053101549682431291)
XLA Ops:
  0.6 0.8 %compare_and_fusion = pred[32]{0:T(512)(128)(4,1)S(1)} fusion(s32[32]{0:T(128)} %param.6), kind=kLoop, calls=%fused_computation.111 | loop fusion | flops 192 | bytes 160 | tf_op jit(solution)/shard_map/jit(_take)/and | solution.py:88
  1.5 0.7 %compare_select_fusion = s32[32]{0:T(128)S(1)} fusion(s32[32]{0:T(128)} %param.6), kind=kLoop, calls=%fused_computation.110 | loop fusion | flops 96 | bytes 256 | tf_op jit(solution)/shard_map/jit(_take)/jit(_where)/select_n | solution.py:88
  2.1 3.4 %gather_fusion = bf16[32,2,2,12,256]{4,2,3,1,0:T(2,128)(2,1)S(1)} fusion(bf16[2,48,2,12,256]{4,2,3,1,0:T(2,128)(2,1)} %bitcast.201, s32[1024]{0:T(1024)S(1)} %pad_clamp_fusion), kind=kCustom, calls=%fused_computation | custom fusion | bytes 1572992 | tf_op jit(solution)/shard_map/jit(_take)/gather | solution.py:88
  5.5 1.9 %convolution_bitcast_fusion.1 = f32[2,2,32,2,2,32]{5,2,4,3,1,0:T(8,128)S(1)} fusion(bf16[2,2,2,6,32,256,1]{5,4,3,2,1,0,6:T(8,128)(2,1)} %bitcast.210, bf16[2,32,2,2,6,256]{5,2,4,3,0,1:T(2,128)(2,1)S(1)} %bitcast.190, pred[32]{0:T(512)(128)(4,1)S(1)} %compare_and_fusion), kind=kOutput, calls=%fused_computation.6 | convolution fusion | flops 50724864 | bytes 1638432 | tf_op jit(solution)/shard_map/tkqhcs,tphcrs->thkqpr/dot_general | solution.py:29
  7.9 11.8 %all_to_all.39 = f32[4,1,2048]{2,1,0:T(1,128)S(1)} all-to-all(f32[4,1,2048]{2,1,0:T(1,128)S(1)} %reshape.628), channel_id=1, replica_groups=mesh['gx'=4,'gy'=4,'gz'=2] {'gx'}, dimensions={0} | all-to-all | bytes 65536 | tf_op jit(solution)/shard_map/all_to_all | solution.py:90
  19.6 0.5 broadcast.83
  20.2 0.7 %reduce = f32[4,2048]{1,0:T(4,128)S(1)} reduce(f32[4,1,2048]{2,1,0:T(1,128)S(1)} %all_to_all.39, f32[]{:T(128)} %broadcast.83), dimensions={1}, to_apply=%all_to_all.28.reduce_sub_computation | reduce | bytes 65540 | tf_op jit(solution)/shard_map/all_to_all | solution.py:90
  21.0 1.5 %collective-permute-start.1 = (f32[4,1,1,2,2,64,8]{5,6,0,4,3,2,1:T(8,128)S(1)}, f32[4,1,1,2,2,64,8]{5,6,0,4,3,2,1:T(8,128)S(1)}, u32[]{:S(2)}, u32[]{:S(2)}) collective-permute-start(f32[4,1,1,2,2,64,8]{5,6,0,4,3,2,1:T(8,128)S(1)} %copy_multiply_fusion.1), channel_id=1, source_target_pairs={{0,2},{2,4},{4,6},{6,0},{1,3},{3,5},{5,7},{7,1},{8,10},{10,12},{12... | collective-permute-start | bytes 98312 | tf_op jit(solution)/shard_map/ppermute | solution.py:16
  22.6 1.4 %collective-permute-start = (f32[4,1,1,2,2,64,8]{5,6,0,4,3,2,1:T(8,128)S(1)}, f32[4,1,1,2,2,64,8]{5,6,0,4,3,2,1:T(8,128)S(1)}, u32[]{:S(2)}, u32[]{:S(2)}) collective-permute-start(f32[4,1,1,2,2,64,8]{5,6,0,4,3,2,1:T(8,128)S(1)} %copy_multiply_fusion.1), channel_id=1, source_target_pairs={{2,0},{4,2},{6,4},{0,6},{3,1},{5,3},{7,5},{1,7},{10,8},{12,10},{14... | collective-permute-start | bytes 98312 | tf_op jit(solution)/shard_map/ppermute | solution.py:17
  24.1 2.2 %collective-permute-done.1 = f32[4,1,1,2,2,64,8]{5,6,0,4,3,2,1:T(8,128)S(1)} collective-permute-done((f32[4,1,1,2,2,64,8]{5,6,0,4,3,2,1:T(8,128)S(1)}, f32[4,1,1,2,2,64,8]{5,6,0,4,3,2,1:T(8,128)S(1)}, u32[]{:S(2)}, u32[]{:S(2)}) %collective-permute-start.1) | collective-permute-done | bytes 32800 | tf_op jit(solution)/shard_map/ppermute | solution.py:16
  26.3 0.8 %collective-permute-done = f32[4,1,1,2,2,64,8]{5,6,0,4,3,2,1:T(8,128)S(1)} collective-permute-done((f32[4,1,1,2,2,64,8]{5,6,0,4,3,2,1:T(8,128)S(1)}, f32[4,1,1,2,2,64,8]{5,6,0,4,3,2,1:T(8,128)S(1)}, u32[]{:S(2)}, u32[]{:S(2)}) %collective-permute-start) | collective-permute-done | bytes 32800 | tf_op jit(solution)/shard_map/ppermute | solution.py:17
  27.1 0.5 collective-permute-start.2
  27.6 1.2 %collective-permute-done.2 = f32[4,3,1,2,2,64,8]{5,6,0,4,3,2,1:T(8,128)S(1)} collective-permute-done((f32[4,3,1,2,2,64,8]{5,6,0,4,3,2,1:T(8,128)S(1)}, f32[4,3,1,2,2,64,8]{5,6,0,4,3,2,1:T(8,128)S(1)}, u32[]{:S(2)}, u32[]{:S(2)}) %collective-permute-start.2) | collective-permute-done | bytes 98336 | tf_op jit(solution)/shard_map/ppermute | solution.py:17
  29.0 2.4 %fusion.4 = f32[4,1,1,2,64,16]{4,5,0,3,2,1:T(8,128)S(1)} fusion(f32[4,1,1,2,9,64,8]{5,6,4,0,3,2,1:T(8,128)S(1)} %get-tuple-element.7, f32[4,1,1,2,9,64,8]{5,6,4,0,3,2,1:T(8,128)S(1)} %get-tuple-element.6, f32[4,1,1,2,9,64,8]{5,6,4,0,3,2,1:T(8,128)S(1)} %fusion.48, f32[4,1,1,2,9,64,128]{6,5,4,3,2,1,0:T(8,128)S(1)} %copy-done), kind=kOutput, calls=%fused_computation.7 | convolution fusion | flops 113688576 | bytes 2834432 | tf_op jit(solution)/shard_map/abcdeij,abcdejr->abcdir/dot_general | solution.py:76
  31.4 2.2 %collective-permute-start.4 = (f32[4,1,1,2,2,64,8]{5,6,0,3,4,2,1:T(8,128)S(1)}, f32[4,1,1,2,2,64,8]{5,6,0,3,4,2,1:T(8,128)S(1)}, u32[]{:S(2)}, u32[]{:S(2)}) collective-permute-start(f32[4,1,1,2,2,64,8]{5,6,0,3,4,2,1:T(8,128)S(1)} %copy.102), channel_id=1, source_target_pairs={{2,0},{4,2},{6,4},{0,6},{3,1},{5,3},{7,5},{1,7},{10,8},{12,10},{14... | collective-permute-start | bytes 98312 | tf_op jit(solution)/shard_map/ppermute | solution.py:17
  33.9 5.0 %collective-permute-done.5 = f32[4,1,1,2,2,64,8]{5,6,0,3,4,2,1:T(8,128)S(1)} collective-permute-done((f32[4,1,1,2,2,64,8]{5,6,0,3,4,2,1:T(8,128)S(1)}, f32[4,1,1,2,2,64,8]{5,6,0,3,4,2,1:T(8,128)S(1)}, u32[]{:S(2)}, u32[]{:S(2)}) %collective-permute-start.5) | collective-permute-done | bytes 32800 | tf_op jit(solution)/shard_map/ppermute | solution.py:16
  39.0 0.5 collective-permute-start.6
  39.5 1.2 %collective-permute-done.6 = f32[4,3,1,2,2,64,8]{5,6,0,3,4,2,1:T(8,128)S(1)} collective-permute-done((f32[4,3,1,2,2,64,8]{5,6,0,3,4,2,1:T(8,128)S(1)}, f32[4,3,1,2,2,64,8]{5,6,0,3,4,2,1:T(8,128)S(1)}, u32[]{:S(2)}, u32[]{:S(2)}) %collective-permute-start.6) | collective-permute-done | bytes 98336 | tf_op jit(solution)/shard_map/ppermute | solution.py:17
  40.8 2.3 %fusion.7 = f32[4,2,16,64]{3,2,1,0:T(8,128)S(1)} fusion(f32[4,1,1,2,9,64,128]{6,5,4,3,2,1,0:T(8,128)S(1)} %copy-done, f32[4,1,1,2,9,64,8]{5,6,0,3,4,2,1:T(8,128)S(1)} %get-tuple-element.5, f32[4,1,1,2,9,64,8]{5,6,0,3,4,2,1:T(8,128)S(1)} %get-tuple-element.4, f32[4,1,1,2,9,64,8]{5,6,0,3,4,2,1:T(8,128)S(1)} %fusion.49), kind=kOutput, calls=%fused_computation.8 | convolution fusion | flops 113688576 | bytes 2834432 | tf_op jit(solution)/shard_map/abcdeij,abcdejr->abcdir/dot_general | solution.py:76
  43.4 8.0 %all_to_all.40 = f32[4,1,2048]{2,1,0:T(1,128)S(1)} all-to-all(f32[4,1,2048]{2,1,0:T(1,128)S(1)} %reshape.630), channel_id=1, replica_groups=mesh['gx'=4,'gy'=4,'gz'=2] {'gx'}, dimensions={0} | all-to-all | bytes 65536 | tf_op jit(solution)/shard_map/all_to_all | solution.py:96
  51.4 0.7 %reduce.1 = f32[4,2048]{1,0:T(4,128)S(1)} reduce(f32[4,1,2048]{2,1,0:T(1,128)S(1)} %all_to_all.40, f32[]{:T(128)} %broadcast.83), dimensions={1}, to_apply=%all_to_all.33.reduce_sub_computation | reduce | bytes 65540 | tf_op jit(solution)/shard_map/all_to_all | solution.py:96
  52.2 0.6 %copy_bitcast_fusion.1 = f32[1,1,1,2,2,64,32]{5,6,4,3,2,1,0:T(8,128)} fusion(f32[4,1,1,2,2,8,64]{6,5,4,3,2,1,0:T(8,128)S(1)} %reshape.631), kind=kLoop, calls=%fused_computation.81 | loop fusion | bytes 65536 | tf_op jit(solution)/shard_map/all_to_all | solution.py:96
  52.9 0.7 %convolution_bitcast_fusion = f32[2,2,2,2,6,32,256]{6,5,4,1,2,3,0:T(8,128)S(1)} fusion(bf16[2,32,2,2,6,256]{5,2,4,3,0,1:T(2,128)(2,1)S(1)} %bitcast.191, pred[32]{0:T(512)(128)(4,1)S(1)} %compare_and_fusion, bf16[2,2,2,32,32,1,1]{3,2,4,1,0,6,5:T(2,128)(2,1)S(1)} %bitcast.204), kind=kOutput, calls=%fused_computation.5 | convolution fusion | flops 50724864 | bytes 3948576 | tf_op jit(solution)/shard_map/tkqhcs,tphkr->tqphcrs/dot_general | solution.py:45
  54.0 1.0 %pad_maximum_fusion = bf16[1,1,1,2,2,12,32,256]{7,6,5,4,3,2,1,0:T(8,128)(2,1)} fusion(bf16[1,1,1,2,1,12,32,256]{7,6,5,4,3,2,1,0:T(8,128)(2,1)S(1)} %bitcast.200, bf16[1,1,1,2,1,12,32,256]{7,6,5,4,3,2,1,0:T(8,128)(2,1)S(1)} %bitcast.199), kind=kLoop, calls=%fused_computation.13 | loop fusion | flops 393216 | bytes 1572864 | tf_op jit(solution)/shard_map/stack | solution.py:49
  (62 shorter events, 1.9 us)
Async XLA Ops:
  0.6 28.3 %copy-start = (f32[4,1,1,2,9,64,128]{6,5,4,3,2,1,0:T(8,128)S(1)}, f32[4,1,1,2,9,64,128]{6,5,4,3,2,1,0:T(8,128)}, u32[]{:S(2)}) copy-start(f32[4,1,1,2,9,64,128]{6,5,4,3,2,1,0:T(8,128)} %param.7) | copy-start | bytes 7077892
  21.0 5.2 %collective-permute-start.1 = (f32[4,1,1,2,2,64,8]{5,6,0,4,3,2,1:T(8,128)S(1)}, f32[4,1,1,2,2,64,8]{5,6,0,4,3,2,1:T(8,128)S(1)}, u32[]{:S(2)}, u32[]{:S(2)}) collective-permute-start(f32[4,1,1,2,2,64,8]{5,6,0,4,3,2,1:T(8,128)S(1)} %copy_multiply_fusion.1), channel_id=1, source_target_pairs={{0,2},{2,4},{4,6},{6,0},{1,3},{3,5},{5,7},{7,1},{8,10},{10,12},{12... | collective-permute-start | bytes 98312 | tf_op jit(solution)/shard_map/ppermute | solution.py:16
  22.6 4.4 %collective-permute-start = (f32[4,1,1,2,2,64,8]{5,6,0,4,3,2,1:T(8,128)S(1)}, f32[4,1,1,2,2,64,8]{5,6,0,4,3,2,1:T(8,128)S(1)}, u32[]{:S(2)}, u32[]{:S(2)}) collective-permute-start(f32[4,1,1,2,2,64,8]{5,6,0,4,3,2,1:T(8,128)S(1)} %copy_multiply_fusion.1), channel_id=1, source_target_pairs={{2,0},{4,2},{6,4},{0,6},{3,1},{5,3},{7,5},{1,7},{10,8},{12,10},{14... | collective-permute-start | bytes 98312 | tf_op jit(solution)/shard_map/ppermute | solution.py:17
  27.0 1.8 %collective-permute-start.3 = (f32[4,3,1,2,2,64,8]{5,6,0,4,3,2,1:T(8,128)S(1)}, f32[4,3,1,2,2,64,8]{5,6,0,4,3,2,1:T(8,128)S(1)}, u32[]{:S(2)}, u32[]{:S(2)}) collective-permute-start(f32[4,3,1,2,2,64,8]{5,6,0,4,3,2,1:T(8,128)S(1)} %pad_maximum_fusion.1), channel_id=1, source_target_pairs={{0,1},{1,0},{2,3},{3,2},{4,5},{5,4},{6,7},{7,6},{8,9},{9,8},{10,11... | collective-permute-start | bytes 294920 | tf_op jit(solution)/shard_map/ppermute | solution.py:16
  27.1 1.7 %collective-permute-start.2 = (f32[4,3,1,2,2,64,8]{5,6,0,4,3,2,1:T(8,128)S(1)}, f32[4,3,1,2,2,64,8]{5,6,0,4,3,2,1:T(8,128)S(1)}, u32[]{:S(2)}, u32[]{:S(2)}) collective-permute-start(f32[4,3,1,2,2,64,8]{5,6,0,4,3,2,1:T(8,128)S(1)} %pad_maximum_fusion.1), channel_id=1, source_target_pairs={{1,0},{0,1},{3,2},{2,3},{5,4},{4,5},{7,6},{6,7},{9,8},{8,9},{11,10... | collective-permute-start | bytes 294920 | tf_op jit(solution)/shard_map/ppermute | solution.py:17
  31.4 7.4 %collective-permute-start.4 = (f32[4,1,1,2,2,64,8]{5,6,0,3,4,2,1:T(8,128)S(1)}, f32[4,1,1,2,2,64,8]{5,6,0,3,4,2,1:T(8,128)S(1)}, u32[]{:S(2)}, u32[]{:S(2)}) collective-permute-start(f32[4,1,1,2,2,64,8]{5,6,0,3,4,2,1:T(8,128)S(1)} %copy.102), channel_id=1, source_target_pairs={{2,0},{4,2},{6,4},{0,6},{3,1},{5,3},{7,5},{1,7},{10,8},{12,10},{14... | collective-permute-start | bytes 98312 | tf_op jit(solution)/shard_map/ppermute | solution.py:17
  33.7 5.2 %collective-permute-start.5 = (f32[4,1,1,2,2,64,8]{5,6,0,3,4,2,1:T(8,128)S(1)}, f32[4,1,1,2,2,64,8]{5,6,0,3,4,2,1:T(8,128)S(1)}, u32[]{:S(2)}, u32[]{:S(2)}) collective-permute-start(f32[4,1,1,2,2,64,8]{5,6,0,3,4,2,1:T(8,128)S(1)} %copy.102), channel_id=1, source_target_pairs={{0,2},{2,4},{4,6},{6,0},{1,3},{3,5},{5,7},{7,1},{8,10},{10,12},{12... | collective-permute-start | bytes 98312 | tf_op jit(solution)/shard_map/ppermute | solution.py:16
  38.9 1.8 %collective-permute-start.7 = (f32[4,3,1,2,2,64,8]{5,6,0,3,4,2,1:T(8,128)S(1)}, f32[4,3,1,2,2,64,8]{5,6,0,3,4,2,1:T(8,128)S(1)}, u32[]{:S(2)}, u32[]{:S(2)}) collective-permute-start(f32[4,3,1,2,2,64,8]{5,6,0,3,4,2,1:T(8,128)S(1)} %constant_dynamic-update-slice_fusion), channel_id=1, source_target_pairs={{0,1},{1,0},{2,3},{3,2},{4,5},{5,4},{6,7},{7,6},{8,9},{9,8},{10,11... | collective-permute-start | bytes 294920 | tf_op jit(solution)/shard_map/ppermute | solution.py:16
  39.0 1.7 %collective-permute-start.6 = (f32[4,3,1,2,2,64,8]{5,6,0,3,4,2,1:T(8,128)S(1)}, f32[4,3,1,2,2,64,8]{5,6,0,3,4,2,1:T(8,128)S(1)}, u32[]{:S(2)}, u32[]{:S(2)}) collective-permute-start(f32[4,3,1,2,2,64,8]{5,6,0,3,4,2,1:T(8,128)S(1)} %constant_dynamic-update-slice_fusion), channel_id=1, source_target_pairs={{1,0},{0,1},{3,2},{2,3},{5,4},{4,5},{7,6},{6,7},{9,8},{8,9},{11,10... | collective-permute-start | bytes 294920 | tf_op jit(solution)/shard_map/ppermute | solution.py:17
where the time goes:
time: 55.2 us; the launch traced here: 54.9 us
  blocking collectives  19.8 us (36%)
  waiting for transfers between devices  10.3 us (19%)
  matrix products  7.38 us (13%)
  starting transfers between devices  6.45 us (12%)
  local copies, waits for them, and re-layouts  5.43 us (10%)
  other arithmetic  4.6 us (8%)
  between operations  0.99 us (2%)
    all_to_all x1, blocking collectives, on_device(): lax.all_to_all(restricted, 'gx', split_axis=6, concat_axis=0, tiled=True)  11.8 us
    all_to_all x1, blocking collectives, on_device(): lax.all_to_all(iterate, 'gx', split_axis=0, concat_axis=6, tiled=True)  8.01 us
    ppermute x4, waiting for transfers between devices, extended(): before = lax.ppermute(last, axis, up)  7.13 us
    dot_general x2, matrix products, apply_operator(): jnp.einsum('abcdeij,abcdejr->abcdir', local_links, columns, precision=lax...  4.69 us
    ppermute x4, starting transfers between devices, extended(): after = lax.ppermute(initial, axis, down)  4.65 us
    gather x1, local copies, waits for them, and re-layouts, on_device(): chosen = jnp.take(candidates[0, 0, 0], vector_pick, axis=1)  3.4 us
    ppermute x4, waiting for transfers between devices, extended(): after = lax.ppermute(initial, axis, down)  3.15 us
    dot_general x1, matrix products, restrict_local(): jnp.einsum('tkqhcs,tphcrs->thkqpr', shaped, source, preferred_element_typ...  1.94 us
  transfers between devices with their start and end apart: 8, of which 5 were waited for; matrix products, arithmetic and copies ran while one was open for 0% of the time, Pallas kernels for 0%

commit v1 on v0

v1 whole, which is shorter than its diff:
```python
import functools

import jax
import jax.numpy as jnp
from jax import lax
from jax.experimental import pallas as pl
from jax.experimental.pallas import tpu as pltpu
from jax.sharding import PartitionSpec as P

F32 = jnp.float32
BF16 = jnp.bfloat16
VMEM = pl.BlockSpec(memory_space=pltpu.VMEM)
SMEM = pl.BlockSpec(memory_space=pltpu.SMEM)
HBM = pl.BlockSpec(memory_space=pltpu.HBM)
MIB = 1 << 20


def matchings(axis):
    size = lax.axis_size(axis)
    first = [(i, i ^ 1) for i in range(size)]
    if size == 2:
        return [first]
    second = [(i, (i + 1) % size if i % 2 else (i - 1) % size) for i in range(size)]
    return [first, second]


def turned(value):
    lanes = value.shape[-1]
    lane = lax.broadcasted_iota(jnp.int32, value.shape, value.ndim - 1)
    from_imag = pltpu.roll(value, lanes - 32, value.ndim - 1)
    from_real = pltpu.roll(value, 32, value.ndim - 1)
    return jnp.where((lane // 32) % 2 == 0, -from_imag, from_real)


def restrict_kernel(
    pick_ref, pool_ref, source_ref, out_ref, matrix_ref, pick, pool, source, rows, pick_sem, pool_sems, source_sems
):
    def copies(t, h):
        part = pl.ds(6 * h, 6)
        return (
            pltpu.make_async_copy(pool_ref.at[t, :, part], pool.at[t, :, part], pool_sems.at[t, h]),
            pltpu.make_async_copy(source_ref.at[t, :, part], source.at[t, :, part], source_sems.at[t, h]),
        )

    chunks = [(t, h) for t in range(2) for h in range(2)]
    picked = pltpu.make_async_copy(pick_ref, pick, pick_sem)
    picked.start()
    for chunk in chunks:
        for copy in copies(*chunk):
            copy.start()
    picked.wait()
    index = [pick[k] for k in range(32)]
    for t, h in chunks:
        for copy in copies(t, h):
            copy.wait()
        total = None
        for a in range(6 * h, 6 * h + 6):
            matrix = jnp.stack([pool[t, index[k], a] for k in range(32)], axis=0).reshape(64, 256)
            matrix_ref[t, a] = matrix
            term = lax.dot_general(
                matrix, source[t, :, a].reshape(64, 256), (((1,), (1,)), ((), ())), preferred_element_type=F32
            )
            total = term if total is None else total + term
        rows[h, :, 64 * t : 64 * t + 64] = total
    for h in range(2):
        plain = rows[h, pl.ds(0, 32, stride=2), :]
        crossed = rows[h, pl.ds(1, 32, stride=2), :]
        out_ref[pl.ds(32 * h, 32), :] = plain - turned(crossed)


def operator_kernel(links_ref, out_ref, held, sems, *, plan):
    line = lax.axis_index("gx")
    copies = [pltpu.make_async_copy(links_ref.at[line, t], held.at[t], sems.at[t]) for t in range(2)]
    for copy in copies:
        copy.start()
    for t in range(2):
        copies[t].wait()
        rows = pl.ds(64 * t, 64)
        out_ref[rows, 0:128] = (-held[t, 0]).astype(BF16)
        out_ref[rows, 128:256] = (held[t, 7] + held[t, 8]).astype(BF16)
        column = 256
        for axis, direction, order in plan:
            if order is None:
                block = held[t, direction] + held[t, direction + 1]
            else:
                odd = lax.rem(lax.axis_index(axis), 2)
                block = held[t, direction + (odd if order == 0 else 1 - odd)]
            out_ref[rows, column : column + 128] = block.astype(BF16)
            column += 128


def summed(operator_ref, own, others):
    pieces = []
    for value in [own, pltpu.roll(own, 64, 1)] + others:
        pieces += [value, turned(value)]
    columns = jnp.concatenate(pieces, axis=0).astype(BF16)
    product = jnp.dot(operator_ref[...], columns, preferred_element_type=F32)
    lane = lax.broadcasted_iota(jnp.int32, own.shape, 1)
    return jnp.where(lane < 64, product[:64], product[64:])


def first_kernel(operator_ref, own_ref, *refs):
    others, out_ref = refs[:-1], refs[-1]
    own = own_ref[...]
    out_ref[...] = 0.75 * own + 0.25 * summed(operator_ref, own, [ref[...] for ref in others])


def second_kernel(operator_ref, matrix_ref, source_ref, own_ref, *refs):
    others, (error_ref, out_ref, error, result, rows, error_sem, sems) = refs[:-7], refs[-7:]
    own = own_ref[...]
    image = summed(operator_ref, own, [ref[...] for ref in others])
    final = 0.5 * (own + source_ref[...] + image)
    error[...] = final.T
    copies = [pltpu.make_async_copy(error, error_ref, error_sem)]
    copies[0].start()
    half = final.astype(BF16).astype(F32)
    crossed = turned(half)
    for h in range(2):
        rows[h, pl.ds(0, 32, stride=2), :] = half[32 * h : 32 * h + 32]
        rows[h, pl.ds(1, 32, stride=2), :] = crossed[32 * h : 32 * h + 32]
        spread = rows[h].T.astype(BF16)
        for t in range(2):
            for start in (6 * h, 6 * h + 3):
                for a in range(start, start + 3):
                    product = jnp.dot(spread[64 * t : 64 * t + 64], matrix_ref[t, a], preferred_element_type=F32)
                    result[t, :, a] = product.astype(BF16).reshape(2, 32, 256)
                part = (t, slice(None), pl.ds(start, 3))
                copy = pltpu.make_async_copy(result.at[part], out_ref.at[part], sems.at[t, start // 3])
                copy.start()
                copies.append(copy)
    for copy in copies:
        copy.wait()


def limit(mib):
    return pltpu.CompilerParams(vmem_limit_bytes=mib * MIB)


def on_device(fine_residual, candidates, vector_pick, coarse_links):
    vector = jax.ShapeDtypeStruct((64, 128), F32)
    hbm = functools.partial(pltpu.with_memory_space_constraint, memory_space=pltpu.HBM)
    restricted, matrix = pl.pallas_call(
        restrict_kernel,
        out_shape=(vector, jax.ShapeDtypeStruct((2, 12, 64, 256), BF16)),
        in_specs=[HBM, HBM, HBM],
        out_specs=(VMEM, VMEM),
        scratch_shapes=[
            pltpu.SMEM((32,), jnp.int32),
            pltpu.VMEM((2, 48, 12, 2, 256), BF16),
            pltpu.VMEM((2, 2, 12, 32, 256), BF16),
            pltpu.VMEM((2, 64, 128), F32),
            pltpu.SemaphoreType.DMA,
            pltpu.SemaphoreType.DMA((2, 2)),
            pltpu.SemaphoreType.DMA((2, 2)),
        ],
        compiler_params=limit(6),
    )(hbm(vector_pick), hbm(jnp.swapaxes(candidates[0, 0, 0], 2, 3)), hbm(fine_residual[0, 0, 0]))

    exchanges = []
    for axis, direction in (("gz", 5), ("gy", 3), ("gx", 1)):
        pairs = matchings(axis)
        for order, pair in enumerate(pairs):
            exchanges.append((order, axis, direction, len(pairs) > 1, pair))
    exchanges.sort(key=lambda exchange: exchange[0])
    plan = [(axis, direction, order if both else None) for order, axis, direction, both, _ in exchanges]
    operator = pl.pallas_call(
        functools.partial(operator_kernel, plan=tuple(plan)),
        out_shape=jax.ShapeDtypeStruct((128, 128 * (2 + len(plan))), BF16),
        in_specs=[HBM],
        out_specs=VMEM,
        scratch_shapes=[pltpu.VMEM((2, 9, 64, 128), F32), pltpu.SemaphoreType.DMA((2,))],
        compiler_params=limit(3),
    )(hbm(coarse_links[:, 0, 0]))

    def neighbours(value):
        return [lax.ppermute(value, axis, pair) for _, axis, _, _, pair in exchanges]

    first = pl.pallas_call(
        first_kernel,
        out_shape=vector,
        in_specs=[VMEM] * (2 + len(plan)),
        out_specs=VMEM,
        compiler_params=limit(3),
    )(operator, restricted, *neighbours(restricted))
    error, correction = pl.pallas_call(
        second_kernel,
        out_shape=(
            jax.ShapeDtypeStruct((128, 64), F32),
            jax.ShapeDtypeStruct((2, 2, 12, 32, 256), BF16),
        ),
        in_specs=[VMEM] * (4 + len(plan)),
        out_specs=(HBM, HBM),
        scratch_shapes=[
            pltpu.VMEM((128, 64), F32),
            pltpu.VMEM((2, 2, 12, 32, 256), BF16),
            pltpu.VMEM((2, 64, 128), F32),
            pltpu.SemaphoreType.DMA,
            pltpu.SemaphoreType.DMA((2, 4)),
        ],
        compiler_params=limit(4),
    )(operator, matrix, restricted, first, *neighbours(first))
    error = jnp.swapaxes(error.reshape((2, 2, 32, 64)), 2, 3)
    return (correction[None, None, None], error[None, None, None])


def solution(mesh):
    blocks = P("gx", "gy", "gz", None, None, None, None, None)
    return jax.shard_map(
        on_device,
        mesh=mesh,
        in_specs=(blocks, blocks, P(), P(None, "gy", "gz", None, None, None, None)),
        out_specs=(blocks, P("gx", "gy", "gz", None, None, None, None)),
        check_vma=False,
    )
```

time: 55.2 us -> 23.1 us (0.42)
  blocking collectives: 19.8 us -> 0 us
  matrix products: 7.38 us -> 0 us
  starting transfers between devices: 6.45 us -> 12.2 us
  waiting for transfers between devices: 10.3 us -> 4.7 us
  local copies, waits for them, and re-layouts: 5.43 us -> 0 us
  Pallas kernels: 0 us -> 5.35 us
  other arithmetic: 4.6 us -> 0 us
    all_to_all x2 -> x0, blocking collectives: 19.8 us -> none  [the longest x1 11.8 us: on_device(): lax.all_to_all(restricted, 'gx', split_axis=6, concat_axis=0, tiled=True)]
    dot_general x4 -> x0, matrix products: 7.38 us -> none  [the longest x2 4.69 us: apply_operator(): jnp.einsum('abcdeij,abcdejr->abcdir', local_links, columns, precision=lax...]
    ppermute x8 -> x10, starting transfers between devices: 6.45 us -> 12.2 us  [neighbours(): lax.ppermute(value, axis, pair)]
    ppermute x8 -> x10, waiting for transfers between devices: 10.3 us -> 4.7 us  [neighbours(): lax.ppermute(value, axis, pair)]
    pallas_call x0 -> x4, Pallas kernels: none -> 5.35 us  [the longest x1 2.26 us: on_device(): pl.pallas_call(restrict_kernel, out_shape=(vector, jax.ShapeDtypeStruct((...]
    gather x1 -> x0, local copies, waits for them, and re-layouts: 3.4 us -> none  [on_device(): chosen = jnp.take(candidates[0, 0, 0], vector_pick, axis=1)]
    all_to_all x2 -> x0, other arithmetic: 1.46 us -> none  [the longest x1 0.73 us: on_device(): lax.all_to_all(iterate, 'gx', split_axis=0, concat_axis=6, tiled=True)]
    another operation x4 -> x0, other arithmetic: 1.24 us -> none  [the longest x1 0.95 us: prolong_local(): jnp.stack([real_part.reshape(merged_shape), imag_part.reshape(merged_shap...]
  transfers between devices with their start and end apart: 8 -> 10, of which waited for: 5 -> 5; matrix products, arithmetic and copies ran while one was open for 0% -> 0% of each run, Pallas kernels for 0% -> 5%
where the time goes in v1:
time: 23.1 us; the launch traced here: 23 us
  starting transfers between devices  12.2 us (53%)
  Pallas kernels  5.35 us (23%)
  waiting for transfers between devices  4.7 us (20%)
  between operations  0.67 us (3%)
    ppermute x10, starting transfers between devices, neighbours(): lax.ppermute(value, axis, pair)  12.2 us
    ppermute x10, waiting for transfers between devices, neighbours(): lax.ppermute(value, axis, pair)  4.7 us
    pallas_call x1, Pallas kernels, on_device(): pl.pallas_call(restrict_kernel, out_shape=(vector, jax.ShapeDtypeStruct((...  2.26 us
    pallas_call x1, Pallas kernels, on_device(): pl.pallas_call(second_kernel, out_shape=(jax.ShapeDtypeStruct((128, 64),...  1.65 us
    pallas_call x1, Pallas kernels, on_device(): pl.pallas_call(functools.partial(operator_kernel, plan=tuple(plan)), out_...  1.09 us
  transfers between devices with their start and end apart: 10, of which 5 were waited for; matrix products, arithmetic and copies ran while one was open for 0% of the time, Pallas kernels for 5%

profile of v1, /device:TPU:0, one launch (start us, length us, event | category | flops | bytes accessed | tf_op | source)
XLA Modules:
  0.0 23.0 jit_solution(14964023438558546573)
XLA Ops:
  0.6 2.3 %shard_map.60 = (f32[64,128]{1,0:T(8,128)S(1)}, bf16[2,12,64,256]{3,2,1,0:T(8,128)(2,1)S(1)}) custom-call(s32[32]{0:T(128)} %pick_ref.1, bf16[2,48,12,2,256]{4,3,2,1,0:T(2,128)(2,1)} %bitcast.12, bf16[2,2,12,32,256]{4,3,2,1,0:T(8,128)(2,1)} %bitcast.13), custom_call_target="tpu_custom_call" | custom-call | tf_op jit(solution)/shard_map/pallas_call | solution.py:142
  2.9 5.1 %collective-permute-start.4 = (f32[64,128]{1,0:T(8,128)S(1)}, f32[64,128]{1,0:T(8,128)S(1)}, u32[]{:S(2)}, u32[]{:S(2)}) collective-permute-start(f32[64,128]{1,0:T(8,128)S(1)} %get-tuple-element.7.own_ref.source_ref), channel_id=1, source_target_pairs={{0,24},{8,16},{16,8},{24,0},{1,25},{9,17},{17,9},{25,1},{2,26},{10... | collective-permute-start | bytes 98312 | tf_op jit(solution)/shard_map/ppermute | solution.py:176
  8.0 2.4 %collective-permute-start.3 = (f32[64,128]{1,0:T(8,128)S(1)}, f32[64,128]{1,0:T(8,128)S(1)}, u32[]{:S(2)}, u32[]{:S(2)}) collective-permute-start(f32[64,128]{1,0:T(8,128)S(1)} %get-tuple-element.7.own_ref.source_ref), channel_id=1, source_target_pairs={{0,6},{2,4},{4,2},{6,0},{1,7},{3,5},{5,3},{7,1},{8,14},{10,12},{12... | collective-permute-start | bytes 98312 | tf_op jit(solution)/shard_map/ppermute | solution.py:176
  10.5 0.0 collective-permute-start.2
  10.5 0.5 %collective-permute-start.1 = (f32[64,128]{1,0:T(8,128)S(1)}, f32[64,128]{1,0:T(8,128)S(1)}, u32[]{:S(2)}, u32[]{:S(2)}) collective-permute-start(f32[64,128]{1,0:T(8,128)S(1)} %get-tuple-element.7.own_ref.source_ref), channel_id=1, source_target_pairs={{0,2},{2,0},{4,6},{6,4},{1,3},{3,1},{5,7},{7,5},{8,10},{10,8},{12,... | collective-permute-start | bytes 98312 | tf_op jit(solution)/shard_map/ppermute | solution.py:176
  11.0 0.0 collective-permute-start
  11.0 1.1 %shard_map.59.operator_ref = bf16[128,896]{1,0:T(8,128)(2,1)S(1)} custom-call(f32[4,2,9,64,128]{4,3,2,1,0:T(8,128)} %bitcast.11), custom_call_target="tpu_custom_call" | custom-call | tf_op jit(solution)/shard_map/pallas_call | solution.py:166
  12.1 0.0 collective-permute-done.4.refs_4_
  12.1 0.9 %collective-permute-done.3.refs_3_ = f32[64,128]{1,0:T(8,128)S(1)} collective-permute-done((f32[64,128]{1,0:T(8,128)S(1)}, f32[64,128]{1,0:T(8,128)S(1)}, u32[]{:S(2)}, u32[]{:S(2)}) %collective-permute-start.3) | collective-permute-done | bytes 32800 | tf_op jit(solution)/shard_map/ppermute | solution.py:176
  13.0 1.4 %collective-permute-done.2.refs_2_ = f32[64,128]{1,0:T(8,128)S(1)} collective-permute-done((f32[64,128]{1,0:T(8,128)S(1)}, f32[64,128]{1,0:T(8,128)S(1)}, u32[]{:S(2)}, u32[]{:S(2)}) %collective-permute-start.2) | collective-permute-done | bytes 32800 | tf_op jit(solution)/shard_map/ppermute | solution.py:176
  14.4 0.0 collective-permute-done.1.refs_1_
  14.4 0.0 collective-permute-done.refs_0_
  14.4 0.4 %shard_map.61.own_ref = f32[64,128]{1,0:T(8,128)S(1)} custom-call(bf16[128,896]{1,0:T(8,128)(2,1)S(1)} %shard_map.59.operator_ref, f32[64,128]{1,0:T(8,128)S(1)} %get-tuple-element.7.own_ref.source_ref, f32[64,128]{1,0:T(8,128)S(1)} %collective-permute-done.refs_0_, f32[64,128]{1,0:T(8,128)S(1)} %collective-permute-done.1.refs_1_, ...), custom_call_target="tpu_custom_call" | custom-call | tf_op jit(solution)/shard_map/pallas_call | solution.py:178
  14.7 1.0 %collective-permute-start.9 = (f32[64,128]{1,0:T(8,128)S(1)}, f32[64,128]{1,0:T(8,128)S(1)}, u32[]{:S(2)}, u32[]{:S(2)}) collective-permute-start(f32[64,128]{1,0:T(8,128)S(1)} %shard_map.61.own_ref), channel_id=1, source_target_pairs={{0,24},{8,16},{16,8},{24,0},{1,25},{9,17},{17,9},{25,1},{2,26},{10... | collective-permute-start | bytes 98312 | tf_op jit(solution)/shard_map/ppermute | solution.py:176
  15.7 0.9 %collective-permute-start.8 = (f32[64,128]{1,0:T(8,128)S(1)}, f32[64,128]{1,0:T(8,128)S(1)}, u32[]{:S(2)}, u32[]{:S(2)}) collective-permute-start(f32[64,128]{1,0:T(8,128)S(1)} %shard_map.61.own_ref), channel_id=1, source_target_pairs={{0,6},{2,4},{4,2},{6,0},{1,7},{3,5},{5,3},{7,1},{8,14},{10,12},{12... | collective-permute-start | bytes 98312 | tf_op jit(solution)/shard_map/ppermute | solution.py:176
  16.6 0.8 %collective-permute-start.7 = (f32[64,128]{1,0:T(8,128)S(1)}, f32[64,128]{1,0:T(8,128)S(1)}, u32[]{:S(2)}, u32[]{:S(2)}) collective-permute-start(f32[64,128]{1,0:T(8,128)S(1)} %shard_map.61.own_ref), channel_id=1, source_target_pairs={{0,8},{8,0},{16,24},{24,16},{1,9},{9,1},{17,25},{25,17},{2,10},{10... | collective-permute-start | bytes 98312 | tf_op jit(solution)/shard_map/ppermute | solution.py:176
  17.4 1.5 %collective-permute-start.6 = (f32[64,128]{1,0:T(8,128)S(1)}, f32[64,128]{1,0:T(8,128)S(1)}, u32[]{:S(2)}, u32[]{:S(2)}) collective-permute-start(f32[64,128]{1,0:T(8,128)S(1)} %shard_map.61.own_ref), channel_id=1, source_target_pairs={{0,2},{2,0},{4,6},{6,4},{1,3},{3,1},{5,7},{7,5},{8,10},{10,8},{12,... | collective-permute-start | bytes 98312 | tf_op jit(solution)/shard_map/ppermute | solution.py:176
  18.9 0.0 collective-permute-start.5
  18.9 1.8 %collective-permute-done.9.refs_4_ = f32[64,128]{1,0:T(8,128)S(1)} collective-permute-done((f32[64,128]{1,0:T(8,128)S(1)}, f32[64,128]{1,0:T(8,128)S(1)}, u32[]{:S(2)}, u32[]{:S(2)}) %collective-permute-start.9) | collective-permute-done | bytes 32800 | tf_op jit(solution)/shard_map/ppermute | solution.py:176
  20.6 0.0 collective-permute-done.8.refs_3_
  20.7 0.2 %collective-permute-done.7.refs_2_ = f32[64,128]{1,0:T(8,128)S(1)} collective-permute-done((f32[64,128]{1,0:T(8,128)S(1)}, f32[64,128]{1,0:T(8,128)S(1)}, u32[]{:S(2)}, u32[]{:S(2)}) %collective-permute-start.7) | collective-permute-done | bytes 32800 | tf_op jit(solution)/shard_map/ppermute | solution.py:176
  20.9 0.4 %collective-permute-done.6.refs_1_ = f32[64,128]{1,0:T(8,128)S(1)} collective-permute-done((f32[64,128]{1,0:T(8,128)S(1)}, f32[64,128]{1,0:T(8,128)S(1)}, u32[]{:S(2)}, u32[]{:S(2)}) %collective-permute-start.6) | collective-permute-done | bytes 32800 | tf_op jit(solution)/shard_map/ppermute | solution.py:176
  21.3 0.0 collective-permute-done.5.refs_0_
  21.3 1.6 %shard_map.62 = (f32[128,64]{1,0:T(8,128)}, bf16[2,2,12,32,256]{4,3,2,1,0:T(8,128)(2,1)}) custom-call(bf16[128,896]{1,0:T(8,128)(2,1)S(1)} %shard_map.59.operator_ref, bf16[2,12,64,256]{3,2,1,0:T(8,128)(2,1)S(1)} %get-tuple-element.6.matrix_ref, f32[64,128]{1,0:T(8,128)S(1)} %get-tuple-element.7.own_ref.source_ref, f32[64,128]{1,0:T(8,128)S(1)} %shard_map.61.own_ref, ...), custom_call_target="tpu_custom_call" | custom-call | tf_op jit(solution)/shard_map/pallas_call | solution.py:185
Async XLA Ops:
  2.9 9.2 %collective-permute-start.4 = (f32[64,128]{1,0:T(8,128)S(1)}, f32[64,128]{1,0:T(8,128)S(1)}, u32[]{:S(2)}, u32[]{:S(2)}) collective-permute-start(f32[64,128]{1,0:T(8,128)S(1)} %get-tuple-element.7.own_ref.source_ref), channel_id=1, source_target_pairs={{0,24},{8,16},{16,8},{24,0},{1,25},{9,17},{17,9},{25,1},{2,26},{10... | collective-permute-start | bytes 98312 | tf_op jit(solution)/shard_map/ppermute | solution.py:176
  8.0 5.0 %collective-permute-start.3 = (f32[64,128]{1,0:T(8,128)S(1)}, f32[64,128]{1,0:T(8,128)S(1)}, u32[]{:S(2)}, u32[]{:S(2)}) collective-permute-start(f32[64,128]{1,0:T(8,128)S(1)} %get-tuple-element.7.own_ref.source_ref), channel_id=1, source_target_pairs={{0,6},{2,4},{4,2},{6,0},{1,7},{3,5},{5,3},{7,1},{8,14},{10,12},{12... | collective-permute-start | bytes 98312 | tf_op jit(solution)/shard_map/ppermute | solution.py:176
  10.5 3.9 %collective-permute-start.2 = (f32[64,128]{1,0:T(8,128)S(1)}, f32[64,128]{1,0:T(8,128)S(1)}, u32[]{:S(2)}, u32[]{:S(2)}) collective-permute-start(f32[64,128]{1,0:T(8,128)S(1)} %get-tuple-element.7.own_ref.source_ref), channel_id=1, source_target_pairs={{0,8},{8,0},{16,24},{24,16},{1,9},{9,1},{17,25},{25,17},{2,10},{10... | collective-permute-start | bytes 98312 | tf_op jit(solution)/shard_map/ppermute | solution.py:176
  10.5 3.9 %collective-permute-start.1 = (f32[64,128]{1,0:T(8,128)S(1)}, f32[64,128]{1,0:T(8,128)S(1)}, u32[]{:S(2)}, u32[]{:S(2)}) collective-permute-start(f32[64,128]{1,0:T(8,128)S(1)} %get-tuple-element.7.own_ref.source_ref), channel_id=1, source_target_pairs={{0,2},{2,0},{4,6},{6,4},{1,3},{3,1},{5,7},{7,5},{8,10},{10,8},{12,... | collective-permute-start | bytes 98312 | tf_op jit(solution)/shard_map/ppermute | solution.py:176
  11.0 3.4 %collective-permute-start = (f32[64,128]{1,0:T(8,128)S(1)}, f32[64,128]{1,0:T(8,128)S(1)}, u32[]{:S(2)}, u32[]{:S(2)}) collective-permute-start(f32[64,128]{1,0:T(8,128)S(1)} %get-tuple-element.7.own_ref.source_ref), channel_id=1, source_target_pairs={{0,1},{1,0},{2,3},{3,2},{4,5},{5,4},{6,7},{7,6},{8,9},{9,8},{10,11... | collective-permute-start | bytes 98312 | tf_op jit(solution)/shard_map/ppermute | solution.py:176
  14.7 5.9 %collective-permute-start.9 = (f32[64,128]{1,0:T(8,128)S(1)}, f32[64,128]{1,0:T(8,128)S(1)}, u32[]{:S(2)}, u32[]{:S(2)}) collective-permute-start(f32[64,128]{1,0:T(8,128)S(1)} %shard_map.61.own_ref), channel_id=1, source_target_pairs={{0,24},{8,16},{16,8},{24,0},{1,25},{9,17},{17,9},{25,1},{2,26},{10... | collective-permute-start | bytes 98312 | tf_op jit(solution)/shard_map/ppermute | solution.py:176
  15.7 4.9 %collective-permute-start.8 = (f32[64,128]{1,0:T(8,128)S(1)}, f32[64,128]{1,0:T(8,128)S(1)}, u32[]{:S(2)}, u32[]{:S(2)}) collective-permute-start(f32[64,128]{1,0:T(8,128)S(1)} %shard_map.61.own_ref), channel_id=1, source_target_pairs={{0,6},{2,4},{4,2},{6,0},{1,7},{3,5},{5,3},{7,1},{8,14},{10,12},{12... | collective-permute-start | bytes 98312 | tf_op jit(solution)/shard_map/ppermute | solution.py:176
  16.6 4.3 %collective-permute-start.7 = (f32[64,128]{1,0:T(8,128)S(1)}, f32[64,128]{1,0:T(8,128)S(1)}, u32[]{:S(2)}, u32[]{:S(2)}) collective-permute-start(f32[64,128]{1,0:T(8,128)S(1)} %shard_map.61.own_ref), channel_id=1, source_target_pairs={{0,8},{8,0},{16,24},{24,16},{1,9},{9,1},{17,25},{25,17},{2,10},{10... | collective-permute-start | bytes 98312 | tf_op jit(solution)/shard_map/ppermute | solution.py:176
  17.4 3.9 %collective-permute-start.6 = (f32[64,128]{1,0:T(8,128)S(1)}, f32[64,128]{1,0:T(8,128)S(1)}, u32[]{:S(2)}, u32[]{:S(2)}) collective-permute-start(f32[64,128]{1,0:T(8,128)S(1)} %shard_map.61.own_ref), channel_id=1, source_target_pairs={{0,2},{2,0},{4,6},{6,4},{1,3},{3,1},{5,7},{7,5},{8,10},{10,8},{12,... | collective-permute-start | bytes 98312 | tf_op jit(solution)/shard_map/ppermute | solution.py:176
  18.9 2.4 %collective-permute-start.5 = (f32[64,128]{1,0:T(8,128)S(1)}, f32[64,128]{1,0:T(8,128)S(1)}, u32[]{:S(2)}, u32[]{:S(2)}) collective-permute-start(f32[64,128]{1,0:T(8,128)S(1)} %shard_map.61.own_ref), channel_id=1, source_target_pairs={{0,1},{1,0},{2,3},{3,2},{4,5},{5,4},{6,7},{7,6},{8,9},{9,8},{10,11... | collective-permute-start | bytes 98312 | tf_op jit(solution)/shard_map/ppermute | solution.py:176

commit v2 on v1

--- a/solution.py
+++ b/solution.py
@@ -15,13 +15,15 @@
 MIB = 1 << 20
 
 
-def matchings(axis):
-    size = lax.axis_size(axis)
-    first = [(i, i ^ 1) for i in range(size)]
-    if size == 2:
-        return [first]
-    second = [(i, (i + 1) % size if i % 2 else (i - 1) % size) for i in range(size)]
-    return [first, second]
+EXCHANGES = (("gz", 5, 0), ("gz", 5, 1), ("gx", 1, 0), ("gy", 3, 0), ("gy", 3, 1), ("gx", 1, 1))
+
+
+def needed(order, size):
+    return order == 0 or size > 2
+
+
+def partners(order, size):
+    return [(i, (i + (1 if i % 2 == order else -1)) % size) for i in range(size)]
 
 
 def turned(value):
@@ -68,47 +70,52 @@
         out_ref[pl.ds(32 * h, 32), :] = plain - turned(crossed)
 
 
-def operator_kernel(links_ref, out_ref, held, sems, *, plan):
+def operator_kernel(links_ref, high_ref, low_ref, held, sems, *, plan):
     line = lax.axis_index("gx")
     copies = [pltpu.make_async_copy(links_ref.at[line, t], held.at[t], sems.at[t]) for t in range(2)]
     for copy in copies:
         copy.start()
     for t in range(2):
         copies[t].wait()
-        rows = pl.ds(64 * t, 64)
-        out_ref[rows, 0:128] = (-held[t, 0]).astype(BF16)
-        out_ref[rows, 128:256] = (held[t, 7] + held[t, 8]).astype(BF16)
-        column = 256
+        blocks = [-held[t, 0], held[t, 7] + held[t, 8]]
         for axis, direction, order in plan:
-            if order is None:
-                block = held[t, direction] + held[t, direction + 1]
+            if lax.axis_size(axis) == 2:
+                blocks.append(held[t, direction] + held[t, direction + 1])
             else:
                 odd = lax.rem(lax.axis_index(axis), 2)
-                block = held[t, direction + (odd if order == 0 else 1 - odd)]
-            out_ref[rows, column : column + 128] = block.astype(BF16)
-            column += 128
-
-
-def summed(operator_ref, own, others):
-    pieces = []
-    for value in [own, pltpu.roll(own, 64, 1)] + others:
-        pieces += [value, turned(value)]
-    columns = jnp.concatenate(pieces, axis=0).astype(BF16)
-    product = jnp.dot(operator_ref[...], columns, preferred_element_type=F32)
-    lane = lax.broadcasted_iota(jnp.int32, own.shape, 1)
-    return jnp.where(lane < 64, product[:64], product[64:])
-
-
-def first_kernel(operator_ref, own_ref, *refs):
+                blocks.append(held[t, direction + (odd if order == 0 else 1 - odd)])
+        for part in range(2):
+            rows = pl.ds(128 * part + 64 * t, 64)
+            wide = jnp.concatenate([block[:, 64 * part : 64 * part + 64] for block in blocks], axis=1)
+            high = wide.astype(BF16)
+            high_ref[rows, :] = high
+            low_ref[rows, :] = (wide - high.astype(F32)).astype(BF16)
+
+
+def summed(high_ref, low_ref, own, others):
+    stacked = jnp.concatenate([own, pltpu.roll(own, 64, 1)] + others, axis=0)
+    high = stacked.astype(BF16)
+    low = (stacked - high.astype(F32)).astype(BF16)
+    product = jnp.dot(high_ref[...], jnp.concatenate([high, low], axis=1), preferred_element_type=F32)
+    product = product[:, :128] + product[:, 128:]
+    product = product + jnp.dot(low_ref[...], high, preferred_element_type=F32)
+    early = lax.broadcasted_iota(jnp.int32, own.shape, 1) < 64
+    by_real = jnp.where(early, product[:64], product[64:128])
+    by_imag = jnp.where(early, product[128:192], product[192:])
+    return by_real + turned(by_imag)
+
+
+def first_kernel(high_ref, low_ref, own_ref, *refs):
     others, out_ref = refs[:-1], refs[-1]
     own = own_ref[...]
-    out_ref[...] = 0.75 * own + 0.25 * summed(operator_ref, own, [ref[...] for ref in others])
-
-
-def second_kernel(operator_ref, matrix_ref, source_ref, own_ref, *refs):
+    image = summed(high_ref, low_ref, own, [ref[...] for ref in others])
+    out_ref[...] = 0.75 * own + 0.25 * image
+
+
+def second_kernel(high_ref, low_ref, matrix_ref, source_ref, own_ref, *refs):
     others, (error_ref, out_ref, error, result, rows, error_sem, sems) = refs[:-7], refs[-7:]
     own = own_ref[...]
-    image = summed(operator_ref, own, [ref[...] for ref in others])
+    image = summed(high_ref, low_ref, own, [ref[...] for ref in others])
     final = 0.5 * (own + source_ref[...] + image)
     error[...] = final.T
     copies = [pltpu.make_async_copy(error, error_ref, error_sem)]
@@ -156,39 +163,34 @@
         compiler_params=limit(6),
     )(hbm(vector_pick), hbm(jnp.swapaxes(candidates[0, 0, 0], 2, 3)), hbm(fine_residual[0, 0, 0]))
 
-    exchanges = []
-    for axis, direction in (("gz", 5), ("gy", 3), ("gx", 1)):
-        pairs = matchings(axis)
-        for order, pair in enumerate(pairs):
-            exchanges.append((order, axis, direction, len(pairs) > 1, pair))
-    exchanges.sort(key=lambda exchange: exchange[0])
-    plan = [(axis, direction, order if both else None) for order, axis, direction, both, _ in exchanges]
-    operator = pl.pallas_call(
-        functools.partial(operator_kernel, plan=tuple(plan)),
-        out_shape=jax.ShapeDtypeStruct((128, 128 * (2 + len(plan))), BF16),
+    plan = tuple(move for move in EXCHANGES if needed(move[2], lax.axis_size(move[0])))
+    half_operator = jax.ShapeDtypeStruct((256, 64 * (2 + len(plan))), BF16)
+    high, low = pl.pallas_call(
+        functools.partial(operator_kernel, plan=plan),
+        out_shape=(half_operator, half_operator),
         in_specs=[HBM],
-        out_specs=VMEM,
+        out_specs=(VMEM, VMEM),
         scratch_shapes=[pltpu.VMEM((2, 9, 64, 128), F32), pltpu.SemaphoreType.DMA((2,))],
         compiler_params=limit(3),
     )(hbm(coarse_links[:, 0, 0]))
 
     def neighbours(value):
-        return [lax.ppermute(value, axis, pair) for _, axis, _, _, pair in exchanges]
+        return [lax.ppermute(value, axis, partners(order, lax.axis_size(axis))) for axis, _, order in plan]
 
     first = pl.pallas_call(
         first_kernel,
         out_shape=vector,
-        in_specs=[VMEM] * (2 + len(plan)),
+        in_specs=[VMEM] * (3 + len(plan)),
         out_specs=VMEM,
         compiler_params=limit(3),
-    )(operator, restricted, *neighbours(restricted))
+    )(high, low, restricted, *neighbours(restricted))
     error, correction = pl.pallas_call(
         second_kernel,
         out_shape=(
             jax.ShapeDtypeStruct((128, 64), F32),
             jax.ShapeDtypeStruct((2, 2, 12, 32, 256), BF16),
         ),
-        in_specs=[VMEM] * (4 + len(plan)),
+        in_specs=[VMEM] * (5 + len(plan)),
         out_specs=(HBM, HBM),
         scratch_shapes=[
             pltpu.VMEM((128, 64), F32),
@@ -198,7 +200,7 @@
             pltpu.SemaphoreType.DMA((2, 4)),
         ],
         compiler_params=limit(4),
-    )(operator, matrix, restricted, first, *neighbours(first))
+    )(high, low, matrix, restricted, first, *neighbours(first))
     error = jnp.swapaxes(error.reshape((2, 2, 32, 64)), 2, 3)
     return (correction[None, None, None], error[None, None, None])
 

time: 23.1 us -> 23.4 us (1.013)
  starting transfers between devices: 12.2 us -> 10.3 us
  waiting for transfers between devices: 4.7 us -> 6.56 us
  Pallas kernels: 5.35 us -> 5.67 us
    ppermute x10, starting transfers between devices: 12.2 us -> 10.3 us  [neighbours(): lax.ppermute(value, axis, partners(order, lax.axis_size(axis)))]
    ppermute x10, waiting for transfers between devices: 4.7 us -> 6.56 us  [neighbours(): lax.ppermute(value, axis, partners(order, lax.axis_size(axis)))]
where the time goes in v2:
time: 23.4 us; the launch traced here: 23.2 us
  starting transfers between devices  10.3 us (44%)
  waiting for transfers between devices  6.56 us (28%)
  Pallas kernels  5.67 us (24%)
  between operations  0.67 us (3%)
    ppermute x10, starting transfers between devices, neighbours(): lax.ppermute(value, axis, partners(order, lax.axis_size(axis)))  10.3 us
    ppermute x10, waiting for transfers between devices, neighbours(): lax.ppermute(value, axis, partners(order, lax.axis_size(axis)))  6.56 us
    pallas_call x1, Pallas kernels, on_device(): pl.pallas_call(restrict_kernel, out_shape=(vector, jax.ShapeDtypeStruct((...  2.26 us
    pallas_call x1, Pallas kernels, on_device(): pl.pallas_call(second_kernel, out_shape=(jax.ShapeDtypeStruct((128, 64),...  1.73 us
    pallas_call x1, Pallas kernels, on_device(): pl.pallas_call(functools.partial(operator_kernel, plan=plan), out_shape=(...  1.24 us
  transfers between devices with their start and end apart: 10, of which 5 were waited for; matrix products, arithmetic and copies ran while one was open for 0% of the time, Pallas kernels for 5%

profile of v2, /device:TPU:0, one launch (start us, length us, event | category | flops | bytes accessed | tf_op | source)
XLA Modules:
  0.0 23.2 jit_solution(16271422899280733419)
XLA Ops:
  0.6 2.3 %shard_map.60 = (f32[64,128]{1,0:T(8,128)S(1)}, bf16[2,12,64,256]{3,2,1,0:T(8,128)(2,1)S(1)}) custom-call(s32[32]{0:T(128)} %pick_ref.1, bf16[2,48,12,2,256]{4,3,2,1,0:T(2,128)(2,1)} %bitcast.12, bf16[2,2,12,32,256]{4,3,2,1,0:T(8,128)(2,1)} %bitcast.13), custom_call_target="tpu_custom_call" | custom-call | tf_op jit(solution)/shard_map/pallas_call | solution.py:149
  2.9 5.1 %collective-permute-start.4 = (f32[64,128]{1,0:T(8,128)S(1)}, f32[64,128]{1,0:T(8,128)S(1)}, u32[]{:S(2)}, u32[]{:S(2)}) collective-permute-start(f32[64,128]{1,0:T(8,128)S(1)} %get-tuple-element.11.own_ref.source_ref), channel_id=1, source_target_pairs={{0,24},{8,16},{16,8},{24,0},{1,25},{9,17},{17,9},{25,1},{2,26},{10... | collective-permute-start | bytes 98312 | tf_op jit(solution)/shard_map/ppermute | solution.py:178
  8.0 2.4 %collective-permute-start.3 = (f32[64,128]{1,0:T(8,128)S(1)}, f32[64,128]{1,0:T(8,128)S(1)}, u32[]{:S(2)}, u32[]{:S(2)}) collective-permute-start(f32[64,128]{1,0:T(8,128)S(1)} %get-tuple-element.11.own_ref.source_ref), channel_id=1, source_target_pairs={{0,6},{2,4},{4,2},{6,0},{1,7},{3,5},{5,3},{7,1},{8,14},{10,12},{12... | collective-permute-start | bytes 98312 | tf_op jit(solution)/shard_map/ppermute | solution.py:178
  10.5 0.5 %collective-permute-start.2 = (f32[64,128]{1,0:T(8,128)S(1)}, f32[64,128]{1,0:T(8,128)S(1)}, u32[]{:S(2)}, u32[]{:S(2)}) collective-permute-start(f32[64,128]{1,0:T(8,128)S(1)} %get-tuple-element.11.own_ref.source_ref), channel_id=1, source_target_pairs={{0,2},{2,0},{4,6},{6,4},{1,3},{3,1},{5,7},{7,5},{8,10},{10,8},{12,... | collective-permute-start | bytes 98312 | tf_op jit(solution)/shard_map/ppermute | solution.py:178
  11.0 0.0 collective-permute-start.1
  11.0 0.0 collective-permute-start
  11.0 1.2 %shard_map.59 = (bf16[256,448]{1,0:T(8,128)(2,1)S(1)}, bf16[256,448]{1,0:T(8,128)(2,1)S(1)}) custom-call(f32[4,2,9,64,128]{4,3,2,1,0:T(8,128)} %bitcast.11), custom_call_target="tpu_custom_call" | custom-call | tf_op jit(solution)/shard_map/pallas_call | solution.py:168
  12.3 0.0 collective-permute-done.4.refs_4_
  12.3 0.7 %collective-permute-done.3.refs_3_ = f32[64,128]{1,0:T(8,128)S(1)} collective-permute-done((f32[64,128]{1,0:T(8,128)S(1)}, f32[64,128]{1,0:T(8,128)S(1)}, u32[]{:S(2)}, u32[]{:S(2)}) %collective-permute-start.3) | collective-permute-done | bytes 32800 | tf_op jit(solution)/shard_map/ppermute | solution.py:178
  13.0 1.4 %collective-permute-done.2.refs_2_ = f32[64,128]{1,0:T(8,128)S(1)} collective-permute-done((f32[64,128]{1,0:T(8,128)S(1)}, f32[64,128]{1,0:T(8,128)S(1)}, u32[]{:S(2)}, u32[]{:S(2)}) %collective-permute-start.2) | collective-permute-done | bytes 32800 | tf_op jit(solution)/shard_map/ppermute | solution.py:178
  14.4 0.5 %collective-permute-done.1.refs_1_ = f32[64,128]{1,0:T(8,128)S(1)} collective-permute-done((f32[64,128]{1,0:T(8,128)S(1)}, f32[64,128]{1,0:T(8,128)S(1)}, u32[]{:S(2)}, u32[]{:S(2)}) %collective-permute-start.1) | collective-permute-done | bytes 32800 | tf_op jit(solution)/shard_map/ppermute | solution.py:178
  14.9 0.0 collective-permute-done.refs_0_
  14.9 0.4 %shard_map.61.own_ref = f32[64,128]{1,0:T(8,128)S(1)} custom-call(bf16[256,448]{1,0:T(8,128)(2,1)S(1)} %get-tuple-element.8.high_ref, bf16[256,448]{1,0:T(8,128)(2,1)S(1)} %get-tuple-element.9.low_ref, f32[64,128]{1,0:T(8,128)S(1)} %get-tuple-element.11.own_ref.source_ref, f32[64,128]{1,0:T(8,128)S(1)} %collective-permute-done.refs_0_, ...), custom_call_target="tpu_custom_call" | custom-call | tf_op jit(solution)/shard_map/pallas_call | solution.py:180
  15.4 0.3 %collective-permute-start.9 = (f32[64,128]{1,0:T(8,128)S(1)}, f32[64,128]{1,0:T(8,128)S(1)}, u32[]{:S(2)}, u32[]{:S(2)}) collective-permute-start(f32[64,128]{1,0:T(8,128)S(1)} %shard_map.61.own_ref), channel_id=1, source_target_pairs={{0,24},{8,16},{16,8},{24,0},{1,25},{9,17},{17,9},{25,1},{2,26},{10... | collective-permute-start | bytes 98312 | tf_op jit(solution)/shard_map/ppermute | solution.py:178
  15.6 1.4 %collective-permute-start.8 = (f32[64,128]{1,0:T(8,128)S(1)}, f32[64,128]{1,0:T(8,128)S(1)}, u32[]{:S(2)}, u32[]{:S(2)}) collective-permute-start(f32[64,128]{1,0:T(8,128)S(1)} %shard_map.61.own_ref), channel_id=1, source_target_pairs={{0,6},{2,4},{4,2},{6,0},{1,7},{3,5},{5,3},{7,1},{8,14},{10,12},{12... | collective-permute-start | bytes 98312 | tf_op jit(solution)/shard_map/ppermute | solution.py:178
  17.1 0.5 %collective-permute-start.7 = (f32[64,128]{1,0:T(8,128)S(1)}, f32[64,128]{1,0:T(8,128)S(1)}, u32[]{:S(2)}, u32[]{:S(2)}) collective-permute-start(f32[64,128]{1,0:T(8,128)S(1)} %shard_map.61.own_ref), channel_id=1, source_target_pairs={{0,2},{2,0},{4,6},{6,4},{1,3},{3,1},{5,7},{7,5},{8,10},{10,8},{12,... | collective-permute-start | bytes 98312 | tf_op jit(solution)/shard_map/ppermute | solution.py:178
  17.6 0.0 collective-permute-start.6
  17.6 0.0 collective-permute-start.5
  17.6 3.6 %collective-permute-done.9.refs_4_ = f32[64,128]{1,0:T(8,128)S(1)} collective-permute-done((f32[64,128]{1,0:T(8,128)S(1)}, f32[64,128]{1,0:T(8,128)S(1)}, u32[]{:S(2)}, u32[]{:S(2)}) %collective-permute-start.9) | collective-permute-done | bytes 32800 | tf_op jit(solution)/shard_map/ppermute | solution.py:178
  21.1 0.0 collective-permute-done.8.refs_3_
  21.1 0.0 collective-permute-done.7.refs_2_
  21.1 0.3 %collective-permute-done.6.refs_1_ = f32[64,128]{1,0:T(8,128)S(1)} collective-permute-done((f32[64,128]{1,0:T(8,128)S(1)}, f32[64,128]{1,0:T(8,128)S(1)}, u32[]{:S(2)}, u32[]{:S(2)}) %collective-permute-start.6) | collective-permute-done | bytes 32800 | tf_op jit(solution)/shard_map/ppermute | solution.py:178
  21.5 0.0 collective-permute-done.5.refs_0_
  21.5 1.7 %shard_map.62 = (f32[128,64]{1,0:T(8,128)}, bf16[2,2,12,32,256]{4,3,2,1,0:T(8,128)(2,1)}) custom-call(bf16[256,448]{1,0:T(8,128)(2,1)S(1)} %get-tuple-element.8.high_ref, bf16[256,448]{1,0:T(8,128)(2,1)S(1)} %get-tuple-element.9.low_ref, bf16[2,12,64,256]{3,2,1,0:T(8,128)(2,1)S(1)} %get-tuple-element.10.matrix_ref, ...), custom_call_target="tpu_custom_call" | custom-call | tf_op jit(solution)/shard_map/pallas_call | solution.py:187
Async XLA Ops:
  2.9 9.4 %collective-permute-start.4 = (f32[64,128]{1,0:T(8,128)S(1)}, f32[64,128]{1,0:T(8,128)S(1)}, u32[]{:S(2)}, u32[]{:S(2)}) collective-permute-start(f32[64,128]{1,0:T(8,128)S(1)} %get-tuple-element.11.own_ref.source_ref), channel_id=1, source_target_pairs={{0,24},{8,16},{16,8},{24,0},{1,25},{9,17},{17,9},{25,1},{2,26},{10... | collective-permute-start | bytes 98312 | tf_op jit(solution)/shard_map/ppermute | solution.py:178
  8.0 5.0 %collective-permute-start.3 = (f32[64,128]{1,0:T(8,128)S(1)}, f32[64,128]{1,0:T(8,128)S(1)}, u32[]{:S(2)}, u32[]{:S(2)}) collective-permute-start(f32[64,128]{1,0:T(8,128)S(1)} %get-tuple-element.11.own_ref.source_ref), channel_id=1, source_target_pairs={{0,6},{2,4},{4,2},{6,0},{1,7},{3,5},{5,3},{7,1},{8,14},{10,12},{12... | collective-permute-start | bytes 98312 | tf_op jit(solution)/shard_map/ppermute | solution.py:178
  10.5 3.9 %collective-permute-start.2 = (f32[64,128]{1,0:T(8,128)S(1)}, f32[64,128]{1,0:T(8,128)S(1)}, u32[]{:S(2)}, u32[]{:S(2)}) collective-permute-start(f32[64,128]{1,0:T(8,128)S(1)} %get-tuple-element.11.own_ref.source_ref), channel_id=1, source_target_pairs={{0,2},{2,0},{4,6},{6,4},{1,3},{3,1},{5,7},{7,5},{8,10},{10,8},{12,... | collective-permute-start | bytes 98312 | tf_op jit(solution)/shard_map/ppermute | solution.py:178
  11.0 3.9 %collective-permute-start.1 = (f32[64,128]{1,0:T(8,128)S(1)}, f32[64,128]{1,0:T(8,128)S(1)}, u32[]{:S(2)}, u32[]{:S(2)}) collective-permute-start(f32[64,128]{1,0:T(8,128)S(1)} %get-tuple-element.11.own_ref.source_ref), channel_id=1, source_target_pairs={{0,8},{8,0},{16,24},{24,16},{1,9},{9,1},{17,25},{25,17},{2,10},{10... | collective-permute-start | bytes 98312 | tf_op jit(solution)/shard_map/ppermute | solution.py:178
  11.0 3.9 %collective-permute-start = (f32[64,128]{1,0:T(8,128)S(1)}, f32[64,128]{1,0:T(8,128)S(1)}, u32[]{:S(2)}, u32[]{:S(2)}) collective-permute-start(f32[64,128]{1,0:T(8,128)S(1)} %get-tuple-element.11.own_ref.source_ref), channel_id=1, source_target_pairs={{0,1},{1,0},{2,3},{3,2},{4,5},{5,4},{6,7},{7,6},{8,9},{9,8},{10,11... | collective-permute-start | bytes 98312 | tf_op jit(solution)/shard_map/ppermute | solution.py:178
  15.4 5.8 %collective-permute-start.9 = (f32[64,128]{1,0:T(8,128)S(1)}, f32[64,128]{1,0:T(8,128)S(1)}, u32[]{:S(2)}, u32[]{:S(2)}) collective-permute-start(f32[64,128]{1,0:T(8,128)S(1)} %shard_map.61.own_ref), channel_id=1, source_target_pairs={{0,24},{8,16},{16,8},{24,0},{1,25},{9,17},{17,9},{25,1},{2,26},{10... | collective-permute-start | bytes 98312 | tf_op jit(solution)/shard_map/ppermute | solution.py:178
  15.6 5.5 %collective-permute-start.8 = (f32[64,128]{1,0:T(8,128)S(1)}, f32[64,128]{1,0:T(8,128)S(1)}, u32[]{:S(2)}, u32[]{:S(2)}) collective-permute-start(f32[64,128]{1,0:T(8,128)S(1)} %shard_map.61.own_ref), channel_id=1, source_target_pairs={{0,6},{2,4},{4,2},{6,0},{1,7},{3,5},{5,3},{7,1},{8,14},{10,12},{12... | collective-permute-start | bytes 98312 | tf_op jit(solution)/shard_map/ppermute | solution.py:178
  17.1 4.0 %collective-permute-start.7 = (f32[64,128]{1,0:T(8,128)S(1)}, f32[64,128]{1,0:T(8,128)S(1)}, u32[]{:S(2)}, u32[]{:S(2)}) collective-permute-start(f32[64,128]{1,0:T(8,128)S(1)} %shard_map.61.own_ref), channel_id=1, source_target_pairs={{0,2},{2,0},{4,6},{6,4},{1,3},{3,1},{5,7},{7,5},{8,10},{10,8},{12,... | collective-permute-start | bytes 98312 | tf_op jit(solution)/shard_map/ppermute | solution.py:178
  17.6 3.9 %collective-permute-start.6 = (f32[64,128]{1,0:T(8,128)S(1)}, f32[64,128]{1,0:T(8,128)S(1)}, u32[]{:S(2)}, u32[]{:S(2)}) collective-permute-start(f32[64,128]{1,0:T(8,128)S(1)} %shard_map.61.own_ref), channel_id=1, source_target_pairs={{0,8},{8,0},{16,24},{24,16},{1,9},{9,1},{17,25},{25,17},{2,10},{10... | collective-permute-start | bytes 98312 | tf_op jit(solution)/shard_map/ppermute | solution.py:178
  17.6 3.9 %collective-permute-start.5 = (f32[64,128]{1,0:T(8,128)S(1)}, f32[64,128]{1,0:T(8,128)S(1)}, u32[]{:S(2)}, u32[]{:S(2)}) collective-permute-start(f32[64,128]{1,0:T(8,128)S(1)} %shard_map.61.own_ref), channel_id=1, source_target_pairs={{0,1},{1,0},{2,3},{3,2},{4,5},{5,4},{6,7},{7,6},{8,9},{9,8},{10,11... | collective-permute-start | bytes 98312 | tf_op jit(solution)/shard_map/ppermute | solution.py:178

commit v3 on v2

--- a/solution.py
+++ b/solution.py
@@ -15,15 +15,19 @@
 MIB = 1 << 20
 
 
-EXCHANGES = (("gz", 5, 0), ("gz", 5, 1), ("gx", 1, 0), ("gy", 3, 0), ("gy", 3, 1), ("gx", 1, 1))
-
-
-def needed(order, size):
-    return order == 0 or size > 2
-
-
-def partners(order, size):
-    return [(i, (i + (1 if i % 2 == order else -1)) % size) for i in range(size)]
+MOVES = (("gz", 5, 0), ("gz", 5, 1), ("gy", 3, 0), ("gx", 1, 0), ("gy", 3, 1), ("gx", 1, 1))
+
+
+def present(moves):
+    return tuple(move for move in moves if move[2] == 0 or lax.axis_size(move[0]) > 2)
+
+
+def received(value, moves):
+    found = []
+    for axis, _, order in moves:
+        size = lax.axis_size(axis)
+        found.append(lax.ppermute(value, axis, [(i, (i + (1 if i % 2 == order else -1)) % size) for i in range(size)]))
+    return found
 
 
 def turned(value):
@@ -70,53 +74,59 @@
         out_ref[pl.ds(32 * h, 32), :] = plain - turned(crossed)
 
 
-def operator_kernel(links_ref, high_ref, low_ref, held, sems, *, plan):
+def operator_kernel(links_ref, own_high_ref, own_low_ref, far_high_ref, far_low_ref, held, sems, *, moves):
     line = lax.axis_index("gx")
     copies = [pltpu.make_async_copy(links_ref.at[line, t], held.at[t], sems.at[t]) for t in range(2)]
     for copy in copies:
         copy.start()
+
+    def block(t, move):
+        axis, direction, order = move
+        if lax.axis_size(axis) == 2:
+            return held[t, direction] + held[t, direction + 1]
+        odd = lax.rem(lax.axis_index(axis), 2)
+        return held[t, direction + (odd if order == 0 else 1 - odd)]
+
     for t in range(2):
         copies[t].wait()
-        blocks = [-held[t, 0], held[t, 7] + held[t, 8]]
-        for axis, direction, order in plan:
-            if lax.axis_size(axis) == 2:
-                blocks.append(held[t, direction] + held[t, direction + 1])
-            else:
-                odd = lax.rem(lax.axis_index(axis), 2)
-                blocks.append(held[t, direction + (odd if order == 0 else 1 - odd)])
-        for part in range(2):
-            rows = pl.ds(128 * part + 64 * t, 64)
-            wide = jnp.concatenate([block[:, 64 * part : 64 * part + 64] for block in blocks], axis=1)
-            high = wide.astype(BF16)
-            high_ref[rows, :] = high
-            low_ref[rows, :] = (wide - high.astype(F32)).astype(BF16)
-
-
-def summed(high_ref, low_ref, own, others):
-    stacked = jnp.concatenate([own, pltpu.roll(own, 64, 1)] + others, axis=0)
+        own = [-held[t, 0], held[t, 7] + held[t, 8]]
+        far = [block(t, move) for move in moves]
+        for blocks, high_ref, low_ref in ((own, own_high_ref, own_low_ref), (far, far_high_ref, far_low_ref)):
+            for part in range(2):
+                rows = pl.ds(128 * part + 64 * t, 64)
+                wide = jnp.concatenate([links[:, 64 * part : 64 * part + 64] for links in blocks], axis=1)
+                high = wide.astype(BF16)
+                high_ref[rows, :] = high
+                low_ref[rows, :] = (wide - high.astype(F32)).astype(BF16)
+
+
+def summed(high_ref, low_ref, values):
+    stacked = jnp.concatenate(values, axis=0)
     high = stacked.astype(BF16)
     low = (stacked - high.astype(F32)).astype(BF16)
     product = jnp.dot(high_ref[...], jnp.concatenate([high, low], axis=1), preferred_element_type=F32)
     product = product[:, :128] + product[:, 128:]
     product = product + jnp.dot(low_ref[...], high, preferred_element_type=F32)
-    early = lax.broadcasted_iota(jnp.int32, own.shape, 1) < 64
+    early = lax.broadcasted_iota(jnp.int32, (64, 128), 1) < 64
     by_real = jnp.where(early, product[:64], product[64:128])
     by_imag = jnp.where(early, product[128:192], product[192:])
     return by_real + turned(by_imag)
 
 
-def first_kernel(high_ref, low_ref, own_ref, *refs):
+def own_kernel(high_ref, low_ref, source_ref, own_ref, out_ref, *, weight):
+    own = own_ref[...]
+    base = 0.75 * own if weight == 0.25 else 0.5 * (own + source_ref[...])
+    out_ref[...] = base + weight * summed(high_ref, low_ref, [own, pltpu.roll(own, 64, 1)])
+
+
+def first_kernel(high_ref, low_ref, base_ref, *refs):
     others, out_ref = refs[:-1], refs[-1]
-    own = own_ref[...]
-    image = summed(high_ref, low_ref, own, [ref[...] for ref in others])
-    out_ref[...] = 0.75 * own + 0.25 * image
-
-
-def second_kernel(high_ref, low_ref, matrix_ref, source_ref, own_ref, *refs):
+    out_ref[...] = base_ref[...] + 0.25 * summed(high_ref, low_ref, [ref[...] for ref in others])
+
+
+def second_kernel(high_ref, low_ref, matrix_ref, base_ref, *refs):
     others, (error_ref, out_ref, error, result, rows, error_sem, sems) = refs[:-7], refs[-7:]
-    own = own_ref[...]
-    image = summed(high_ref, low_ref, own, [ref[...] for ref in others])
-    final = 0.5 * (own + source_ref[...] + image)
+    final = base_ref[...] + 0.5 * summed(high_ref, low_ref, [ref[...] for ref in others])
     error[...] = final.T
     copies = [pltpu.make_async_copy(error, error_ref, error_sem)]
     copies[0].start()
@@ -163,34 +173,42 @@
         compiler_params=limit(6),
     )(hbm(vector_pick), hbm(jnp.swapaxes(candidates[0, 0, 0], 2, 3)), hbm(fine_residual[0, 0, 0]))
 
-    plan = tuple(move for move in EXCHANGES if needed(move[2], lax.axis_size(move[0])))
-    half_operator = jax.ShapeDtypeStruct((256, 64 * (2 + len(plan))), BF16)
-    high, low = pl.pallas_call(
-        functools.partial(operator_kernel, plan=plan),
-        out_shape=(half_operator, half_operator),
+    moves = present(MOVES)
+    own_half = jax.ShapeDtypeStruct((256, 128), BF16)
+    far_half = jax.ShapeDtypeStruct((256, 64 * len(moves)), BF16)
+    operators = pl.pallas_call(
+        functools.partial(operator_kernel, moves=moves),
+        out_shape=(own_half, own_half, far_half, far_half),
         in_specs=[HBM],
-        out_specs=(VMEM, VMEM),
+        out_specs=(VMEM,) * 4,
         scratch_shapes=[pltpu.VMEM((2, 9, 64, 128), F32), pltpu.SemaphoreType.DMA((2,))],
         compiler_params=limit(3),
     )(hbm(coarse_links[:, 0, 0]))
-
-    def neighbours(value):
-        return [lax.ppermute(value, axis, partners(order, lax.axis_size(axis))) for axis, _, order in plan]
+    own_operator, far_operator = operators[:2], operators[2:]
+
+    def partly(value, weight):
+        return pl.pallas_call(
+            functools.partial(own_kernel, weight=weight),
+            out_shape=vector,
+            in_specs=[VMEM] * 4,
+            out_specs=VMEM,
+            compiler_params=limit(3),
+        )(*own_operator, restricted, value)
 
     first = pl.pallas_call(
         first_kernel,
         out_shape=vector,
-        in_specs=[VMEM] * (3 + len(plan)),
+        in_specs=[VMEM] * (3 + len(moves)),
         out_specs=VMEM,
         compiler_params=limit(3),
-    )(high, low, restricted, *neighbours(restricted))
+    )(*far_operator, partly(restricted, 0.25), *received(restricted, moves))
     error, correction = pl.pallas_call(
         second_kernel,
         out_shape=(
             jax.ShapeDtypeStruct((128, 64), F32),
             jax.ShapeDtypeStruct((2, 2, 12, 32, 256), BF16),
         ),
-        in_specs=[VMEM] * (5 + len(plan)),
+        in_specs=[VMEM] * (4 + len(moves)),
         out_specs=(HBM, HBM),
         scratch_shapes=[
             pltpu.VMEM((128, 64), F32),
@@ -200,7 +218,7 @@
             pltpu.SemaphoreType.DMA((2, 4)),
         ],
         compiler_params=limit(4),
-    )(high, low, matrix, restricted, first, *neighbours(first))
+    )(*far_operator, matrix, partly(first, 0.5), *received(first, moves))
     error = jnp.swapaxes(error.reshape((2, 2, 32, 64)), 2, 3)
     return (correction[None, None, None], error[None, None, None])
 

time: 23.4 us -> 23.1 us (0.987)
  waiting for transfers between devices: 6.56 us -> 3.85 us
  starting transfers between devices: 10.3 us -> 12.2 us
  Pallas kernels: 5.67 us -> 6.21 us
    ppermute x10, waiting for transfers between devices: 6.56 us -> 3.85 us  [received(): lax.ppermute(value, axis, [(i, (i + (1 if i % 2 == order else -1)) % size...]
    ppermute x10, starting transfers between devices: 10.3 us -> 12.2 us  [received(): lax.ppermute(value, axis, [(i, (i + (1 if i % 2 == order else -1)) % size...]
    pallas_call x1 -> x3, Pallas kernels: 1.24 us -> 1.92 us  [the longest x1 1.24 us: on_device(): pl.pallas_call(functools.partial(operator_kernel, moves=moves), out_shape...]
  transfers between devices with their start and end apart: 10 -> 10, of which waited for: 5 -> 5; matrix products, arithmetic and copies ran while one was open for 0% -> 0% of each run, Pallas kernels for 5% -> 8%
where the time goes in v3:
time: 23.1 us; the launch traced here: 23 us
  starting transfers between devices  12.2 us (53%)
  Pallas kernels  6.21 us (27%)
  waiting for transfers between devices  3.85 us (17%)
  between operations  0.68 us (3%)
    ppermute x10, starting transfers between devices, received(): lax.ppermute(value, axis, [(i, (i + (1 if i % 2 == order else -1)) % size...  12.2 us
    ppermute x10, waiting for transfers between devices, received(): lax.ppermute(value, axis, [(i, (i + (1 if i % 2 == order else -1)) % size...  3.85 us
    pallas_call x1, Pallas kernels, on_device(): pl.pallas_call(restrict_kernel, out_shape=(vector, jax.ShapeDtypeStruct((...  2.26 us
    pallas_call x1, Pallas kernels, on_device(): pl.pallas_call(second_kernel, out_shape=(jax.ShapeDtypeStruct((128, 64),...  1.68 us
    pallas_call x1, Pallas kernels, on_device(): pl.pallas_call(functools.partial(operator_kernel, moves=moves), out_shape...  1.24 us
    pallas_call x2, Pallas kernels, partly(): pl.pallas_call(functools.partial(own_kernel, weight=weight), out_shape=ve...  0.68 us
  transfers between devices with their start and end apart: 10, of which 5 were waited for; matrix products, arithmetic and copies ran while one was open for 0% of the time, Pallas kernels for 8%

profile of v3, /device:TPU:0, one launch (start us, length us, event | category | flops | bytes accessed | tf_op | source)
XLA Modules:
  0.0 23.0 jit_solution(9089787312267516211)
XLA Ops:
  0.6 2.3 %shard_map.60 = (f32[64,128]{1,0:T(8,128)S(1)}, bf16[2,12,64,256]{3,2,1,0:T(8,128)(2,1)S(1)}) custom-call(s32[32]{0:T(128)} %pick_ref.1, bf16[2,48,12,2,256]{4,3,2,1,0:T(2,128)(2,1)} %bitcast.12, bf16[2,2,12,32,256]{4,3,2,1,0:T(8,128)(2,1)} %bitcast.13), custom_call_target="tpu_custom_call" | custom-call | tf_op jit(solution)/shard_map/pallas_call | solution.py:159
  2.9 5.1 %collective-permute-start.4 = (f32[64,128]{1,0:T(8,128)S(1)}, f32[64,128]{1,0:T(8,128)S(1)}, u32[]{:S(2)}, u32[]{:S(2)}) collective-permute-start(f32[64,128]{1,0:T(8,128)S(1)} %get-tuple-element.15.source_ref.own_ref), channel_id=1, source_target_pairs={{0,24},{8,16},{16,8},{24,0},{1,25},{9,17},{17,9},{25,1},{2,26},{10... | collective-permute-start | bytes 98312 | tf_op jit(solution)/shard_map/ppermute | solution.py:29
  8.0 2.4 %collective-permute-start.3 = (f32[64,128]{1,0:T(8,128)S(1)}, f32[64,128]{1,0:T(8,128)S(1)}, u32[]{:S(2)}, u32[]{:S(2)}) collective-permute-start(f32[64,128]{1,0:T(8,128)S(1)} %get-tuple-element.15.source_ref.own_ref), channel_id=1, source_target_pairs={{0,6},{2,4},{4,2},{6,0},{1,7},{3,5},{5,3},{7,1},{8,14},{10,12},{12... | collective-permute-start | bytes 98312 | tf_op jit(solution)/shard_map/ppermute | solution.py:29
  10.5 0.0 collective-permute-start.2
  10.5 0.5 %collective-permute-start.1 = (f32[64,128]{1,0:T(8,128)S(1)}, f32[64,128]{1,0:T(8,128)S(1)}, u32[]{:S(2)}, u32[]{:S(2)}) collective-permute-start(f32[64,128]{1,0:T(8,128)S(1)} %get-tuple-element.15.source_ref.own_ref), channel_id=1, source_target_pairs={{0,2},{2,0},{4,6},{6,4},{1,3},{3,1},{5,7},{7,5},{8,10},{10,8},{12,... | collective-permute-start | bytes 98312 | tf_op jit(solution)/shard_map/ppermute | solution.py:29
  11.0 0.0 collective-permute-start
  11.0 1.2 %shard_map.59 = (bf16[256,128]{1,0:T(8,128)(2,1)S(1)}, bf16[256,128]{1,0:T(8,128)(2,1)S(1)}, bf16[256,320]{1,0:T(8,128)(2,1)S(1)}, bf16[256,320]{1,0:T(8,128)(2,1)S(1)}) custom-call(f32[4,2,9,64,128]{4,3,2,1,0:T(8,128)} %bitcast.11), custom_call_target="tpu_custom_call" | custom-call | tf_op jit(solution)/shard_map/pallas_call | solution.py:179
  12.3 0.3 %shard_map.61.base_ref = f32[64,128]{1,0:T(8,128)S(1)} custom-call(bf16[256,128]{1,0:T(8,128)(2,1)S(1)} %get-tuple-element.13.high_ref, bf16[256,128]{1,0:T(8,128)(2,1)S(1)} %get-tuple-element.14.low_ref, f32[64,128]{1,0:T(8,128)S(1)} %get-tuple-element.15.source_ref.own_ref, f32[64,128]{1,0:T(8,128)S(1)} %get-tuple-element.15.source_ref.own_ref), custom_call_target="tpu_custom_call" | custom-call | tf_op jit(solution)/shard_map/pallas_call | solution.py:190
  12.6 0.0 collective-permute-done.4.refs_4_
  12.6 0.4 %collective-permute-done.3.refs_3_ = f32[64,128]{1,0:T(8,128)S(1)} collective-permute-done((f32[64,128]{1,0:T(8,128)S(1)}, f32[64,128]{1,0:T(8,128)S(1)}, u32[]{:S(2)}, u32[]{:S(2)}) %collective-permute-start.3) | collective-permute-done | bytes 32800 | tf_op jit(solution)/shard_map/ppermute | solution.py:29
  13.0 1.4 %collective-permute-done.2.refs_2_ = f32[64,128]{1,0:T(8,128)S(1)} collective-permute-done((f32[64,128]{1,0:T(8,128)S(1)}, f32[64,128]{1,0:T(8,128)S(1)}, u32[]{:S(2)}, u32[]{:S(2)}) %collective-permute-start.2) | collective-permute-done | bytes 32800 | tf_op jit(solution)/shard_map/ppermute | solution.py:29
  14.4 0.3 %shard_map.62.own_ref = f32[64,128]{1,0:T(8,128)S(1)} custom-call(bf16[256,320]{1,0:T(8,128)(2,1)S(1)} %get-tuple-element.10.high_ref, bf16[256,320]{1,0:T(8,128)(2,1)S(1)} %get-tuple-element.11.low_ref, f32[64,128]{1,0:T(8,128)S(1)} %shard_map.61.base_ref, f32[64,128]{1,0:T(8,128)S(1)} %collective-permute-done.refs_0_, ...), custom_call_target="tpu_custom_call" | custom-call | tf_op jit(solution)/shard_map/pallas_call | solution.py:198
  14.7 1.0 %collective-permute-start.9 = (f32[64,128]{1,0:T(8,128)S(1)}, f32[64,128]{1,0:T(8,128)S(1)}, u32[]{:S(2)}, u32[]{:S(2)}) collective-permute-start(f32[64,128]{1,0:T(8,128)S(1)} %shard_map.62.own_ref), channel_id=1, source_target_pairs={{0,24},{8,16},{16,8},{24,0},{1,25},{9,17},{17,9},{25,1},{2,26},{10... | collective-permute-start | bytes 98312 | tf_op jit(solution)/shard_map/ppermute | solution.py:29
  15.7 0.9 %collective-permute-start.8 = (f32[64,128]{1,0:T(8,128)S(1)}, f32[64,128]{1,0:T(8,128)S(1)}, u32[]{:S(2)}, u32[]{:S(2)}) collective-permute-start(f32[64,128]{1,0:T(8,128)S(1)} %shard_map.62.own_ref), channel_id=1, source_target_pairs={{0,6},{2,4},{4,2},{6,0},{1,7},{3,5},{5,3},{7,1},{8,14},{10,12},{12... | collective-permute-start | bytes 98312 | tf_op jit(solution)/shard_map/ppermute | solution.py:29
  16.6 0.8 %collective-permute-start.7 = (f32[64,128]{1,0:T(8,128)S(1)}, f32[64,128]{1,0:T(8,128)S(1)}, u32[]{:S(2)}, u32[]{:S(2)}) collective-permute-start(f32[64,128]{1,0:T(8,128)S(1)} %shard_map.62.own_ref), channel_id=1, source_target_pairs={{0,8},{8,0},{16,24},{24,16},{1,9},{9,1},{17,25},{25,17},{2,10},{10... | collective-permute-start | bytes 98312 | tf_op jit(solution)/shard_map/ppermute | solution.py:29
  17.4 1.5 %collective-permute-start.6 = (f32[64,128]{1,0:T(8,128)S(1)}, f32[64,128]{1,0:T(8,128)S(1)}, u32[]{:S(2)}, u32[]{:S(2)}) collective-permute-start(f32[64,128]{1,0:T(8,128)S(1)} %shard_map.62.own_ref), channel_id=1, source_target_pairs={{0,2},{2,0},{4,6},{6,4},{1,3},{3,1},{5,7},{7,5},{8,10},{10,8},{12,... | collective-permute-start | bytes 98312 | tf_op jit(solution)/shard_map/ppermute | solution.py:29
  18.9 0.0 collective-permute-start.5
  18.9 0.3 %shard_map.63.base_ref = f32[64,128]{1,0:T(8,128)S(1)} custom-call(bf16[256,128]{1,0:T(8,128)(2,1)S(1)} %get-tuple-element.13.high_ref, bf16[256,128]{1,0:T(8,128)(2,1)S(1)} %get-tuple-element.14.low_ref, f32[64,128]{1,0:T(8,128)S(1)} %get-tuple-element.15.source_ref.own_ref, f32[64,128]{1,0:T(8,128)S(1)} %shard_map.62.own_ref), custom_call_target="tpu_custom_call" | custom-call | tf_op jit(solution)/shard_map/pallas_call | solution.py:190
  19.2 1.6 %collective-permute-done.9.refs_4_ = f32[64,128]{1,0:T(8,128)S(1)} collective-permute-done((f32[64,128]{1,0:T(8,128)S(1)}, f32[64,128]{1,0:T(8,128)S(1)}, u32[]{:S(2)}, u32[]{:S(2)}) %collective-permute-start.9) | collective-permute-done | bytes 32800 | tf_op jit(solution)/shard_map/ppermute | solution.py:29
  20.8 0.0 collective-permute-done.8.refs_3_
  20.8 0.1 collective-permute-done.7.refs_2_
  20.9 0.4 %collective-permute-done.6.refs_1_ = f32[64,128]{1,0:T(8,128)S(1)} collective-permute-done((f32[64,128]{1,0:T(8,128)S(1)}, f32[64,128]{1,0:T(8,128)S(1)}, u32[]{:S(2)}, u32[]{:S(2)}) %collective-permute-start.6) | collective-permute-done | bytes 32800 | tf_op jit(solution)/shard_map/ppermute | solution.py:29
  21.3 0.0 collective-permute-done.5.refs_0_
  21.3 1.7 %shard_map.64 = (f32[128,64]{1,0:T(8,128)}, bf16[2,2,12,32,256]{4,3,2,1,0:T(8,128)(2,1)}) custom-call(bf16[256,320]{1,0:T(8,128)(2,1)S(1)} %get-tuple-element.10.high_ref, bf16[256,320]{1,0:T(8,128)(2,1)S(1)} %get-tuple-element.11.low_ref, bf16[2,12,64,256]{3,2,1,0:T(8,128)(2,1)S(1)} %get-tuple-element.12.matrix_ref, f32[64,128]{1,0:T(8,128)S(1)} %shard_map.63.base_ref, ...), custom_call_target="tpu_custom_call" | custom-call | tf_op jit(solution)/shard_map/pallas_call | solution.py:205
  (2 shorter events, 0.0 us)
Async XLA Ops:
  2.9 9.7 %collective-permute-start.4 = (f32[64,128]{1,0:T(8,128)S(1)}, f32[64,128]{1,0:T(8,128)S(1)}, u32[]{:S(2)}, u32[]{:S(2)}) collective-permute-start(f32[64,128]{1,0:T(8,128)S(1)} %get-tuple-element.15.source_ref.own_ref), channel_id=1, source_target_pairs={{0,24},{8,16},{16,8},{24,0},{1,25},{9,17},{17,9},{25,1},{2,26},{10... | collective-permute-start | bytes 98312 | tf_op jit(solution)/shard_map/ppermute | solution.py:29
  8.0 5.0 %collective-permute-start.3 = (f32[64,128]{1,0:T(8,128)S(1)}, f32[64,128]{1,0:T(8,128)S(1)}, u32[]{:S(2)}, u32[]{:S(2)}) collective-permute-start(f32[64,128]{1,0:T(8,128)S(1)} %get-tuple-element.15.source_ref.own_ref), channel_id=1, source_target_pairs={{0,6},{2,4},{4,2},{6,0},{1,7},{3,5},{5,3},{7,1},{8,14},{10,12},{12... | collective-permute-start | bytes 98312 | tf_op jit(solution)/shard_map/ppermute | solution.py:29
  10.5 3.9 %collective-permute-start.2 = (f32[64,128]{1,0:T(8,128)S(1)}, f32[64,128]{1,0:T(8,128)S(1)}, u32[]{:S(2)}, u32[]{:S(2)}) collective-permute-start(f32[64,128]{1,0:T(8,128)S(1)} %get-tuple-element.15.source_ref.own_ref), channel_id=1, source_target_pairs={{0,8},{8,0},{16,24},{24,16},{1,9},{9,1},{17,25},{25,17},{2,10},{10... | collective-permute-start | bytes 98312 | tf_op jit(solution)/shard_map/ppermute | solution.py:29
  10.5 3.9 %collective-permute-start.1 = (f32[64,128]{1,0:T(8,128)S(1)}, f32[64,128]{1,0:T(8,128)S(1)}, u32[]{:S(2)}, u32[]{:S(2)}) collective-permute-start(f32[64,128]{1,0:T(8,128)S(1)} %get-tuple-element.15.source_ref.own_ref), channel_id=1, source_target_pairs={{0,2},{2,0},{4,6},{6,4},{1,3},{3,1},{5,7},{7,5},{8,10},{10,8},{12,... | collective-permute-start | bytes 98312 | tf_op jit(solution)/shard_map/ppermute | solution.py:29
  11.0 3.4 %collective-permute-start = (f32[64,128]{1,0:T(8,128)S(1)}, f32[64,128]{1,0:T(8,128)S(1)}, u32[]{:S(2)}, u32[]{:S(2)}) collective-permute-start(f32[64,128]{1,0:T(8,128)S(1)} %get-tuple-element.15.source_ref.own_ref), channel_id=1, source_target_pairs={{0,1},{1,0},{2,3},{3,2},{4,5},{5,4},{6,7},{7,6},{8,9},{9,8},{10,11... | collective-permute-start | bytes 98312 | tf_op jit(solution)/shard_map/ppermute | solution.py:29
  14.7 6.0 %collective-permute-start.9 = (f32[64,128]{1,0:T(8,128)S(1)}, f32[64,128]{1,0:T(8,128)S(1)}, u32[]{:S(2)}, u32[]{:S(2)}) collective-permute-start(f32[64,128]{1,0:T(8,128)S(1)} %shard_map.62.own_ref), channel_id=1, source_target_pairs={{0,24},{8,16},{16,8},{24,0},{1,25},{9,17},{17,9},{25,1},{2,26},{10... | collective-permute-start | bytes 98312 | tf_op jit(solution)/shard_map/ppermute | solution.py:29
  15.7 5.1 %collective-permute-start.8 = (f32[64,128]{1,0:T(8,128)S(1)}, f32[64,128]{1,0:T(8,128)S(1)}, u32[]{:S(2)}, u32[]{:S(2)}) collective-permute-start(f32[64,128]{1,0:T(8,128)S(1)} %shard_map.62.own_ref), channel_id=1, source_target_pairs={{0,6},{2,4},{4,2},{6,0},{1,7},{3,5},{5,3},{7,1},{8,14},{10,12},{12... | collective-permute-start | bytes 98312 | tf_op jit(solution)/shard_map/ppermute | solution.py:29
  16.6 4.3 %collective-permute-start.7 = (f32[64,128]{1,0:T(8,128)S(1)}, f32[64,128]{1,0:T(8,128)S(1)}, u32[]{:S(2)}, u32[]{:S(2)}) collective-permute-start(f32[64,128]{1,0:T(8,128)S(1)} %shard_map.62.own_ref), channel_id=1, source_target_pairs={{0,8},{8,0},{16,24},{24,16},{1,9},{9,1},{17,25},{25,17},{2,10},{10... | collective-permute-start | bytes 98312 | tf_op jit(solution)/shard_map/ppermute | solution.py:29
  17.4 3.9 %collective-permute-start.6 = (f32[64,128]{1,0:T(8,128)S(1)}, f32[64,128]{1,0:T(8,128)S(1)}, u32[]{:S(2)}, u32[]{:S(2)}) collective-permute-start(f32[64,128]{1,0:T(8,128)S(1)} %shard_map.62.own_ref), channel_id=1, source_target_pairs={{0,2},{2,0},{4,6},{6,4},{1,3},{3,1},{5,7},{7,5},{8,10},{10,8},{12,... | collective-permute-start | bytes 98312 | tf_op jit(solution)/shard_map/ppermute | solution.py:29
  18.9 2.4 %collective-permute-start.5 = (f32[64,128]{1,0:T(8,128)S(1)}, f32[64,128]{1,0:T(8,128)S(1)}, u32[]{:S(2)}, u32[]{:S(2)}) collective-permute-start(f32[64,128]{1,0:T(8,128)S(1)} %shard_map.62.own_ref), channel_id=1, source_target_pairs={{0,1},{1,0},{2,3},{3,2},{4,5},{5,4},{6,7},{7,6},{8,9},{9,8},{10,11... | collective-permute-start | bytes 98312 | tf_op jit(solution)/shard_map/ppermute | solution.py:29

commit v4 on v3

--- a/solution.py
+++ b/solution.py
@@ -38,40 +38,48 @@
     return jnp.where((lane // 32) % 2 == 0, -from_imag, from_real)
 
 
+PIECES = ((0, 0, 6), (0, 6, 12), (1, 0, 6), (1, 6, 9), (1, 9, 12))
+
+
 def restrict_kernel(
     pick_ref, pool_ref, source_ref, out_ref, matrix_ref, pick, pool, source, rows, pick_sem, pool_sems, source_sems
 ):
-    def copies(t, h):
-        part = pl.ds(6 * h, 6)
+    def copies(i):
+        t, start, stop = PIECES[i]
+        part = (t, slice(None), pl.ds(start, stop - start))
         return (
-            pltpu.make_async_copy(pool_ref.at[t, :, part], pool.at[t, :, part], pool_sems.at[t, h]),
-            pltpu.make_async_copy(source_ref.at[t, :, part], source.at[t, :, part], source_sems.at[t, h]),
+            pltpu.make_async_copy(pool_ref.at[part], pool.at[part], pool_sems.at[i]),
+            pltpu.make_async_copy(source_ref.at[part], source.at[part], source_sems.at[i]),
         )
 
-    chunks = [(t, h) for t in range(2) for h in range(2)]
+    def finish(h):
+        plain = rows[h, pl.ds(0, 32, stride=2), :]
+        crossed = rows[h, pl.ds(1, 32, stride=2), :]
+        out_ref[pl.ds(32 * h, 32), :] = plain - turned(crossed)
+
     picked = pltpu.make_async_copy(pick_ref, pick, pick_sem)
     picked.start()
-    for chunk in chunks:
-        for copy in copies(*chunk):
+    for i in range(len(PIECES)):
+        for copy in copies(i):
             copy.start()
     picked.wait()
     index = [pick[k] for k in range(32)]
-    for t, h in chunks:
-        for copy in copies(t, h):
+    total = None
+    for i, (t, start, stop) in enumerate(PIECES):
+        for copy in copies(i):
             copy.wait()
-        total = None
-        for a in range(6 * h, 6 * h + 6):
+        for a in range(start, stop):
             matrix = jnp.stack([pool[t, index[k], a] for k in range(32)], axis=0).reshape(64, 256)
             matrix_ref[t, a] = matrix
             term = lax.dot_general(
                 matrix, source[t, :, a].reshape(64, 256), (((1,), (1,)), ((), ())), preferred_element_type=F32
             )
-            total = term if total is None else total + term
-        rows[h, :, 64 * t : 64 * t + 64] = total
-    for h in range(2):
-        plain = rows[h, pl.ds(0, 32, stride=2), :]
-        crossed = rows[h, pl.ds(1, 32, stride=2), :]
-        out_ref[pl.ds(32 * h, 32), :] = plain - turned(crossed)
+            total = term if a % 6 == 0 else total + term
+        if stop % 6 == 0:
+            h = stop // 6 - 1
+            rows[h, :, 64 * t : 64 * t + 64] = total
+            if t == 1:
+                finish(h)
 
 
 def operator_kernel(links_ref, own_high_ref, own_low_ref, far_high_ref, far_low_ref, held, sems, *, moves):
@@ -167,8 +175,8 @@
             pltpu.VMEM((2, 2, 12, 32, 256), BF16),
             pltpu.VMEM((2, 64, 128), F32),
             pltpu.SemaphoreType.DMA,
-            pltpu.SemaphoreType.DMA((2, 2)),
-            pltpu.SemaphoreType.DMA((2, 2)),
+            pltpu.SemaphoreType.DMA((len(PIECES),)),
+            pltpu.SemaphoreType.DMA((len(PIECES),)),
         ],
         compiler_params=limit(6),
     )(hbm(vector_pick), hbm(jnp.swapaxes(candidates[0, 0, 0], 2, 3)), hbm(fine_residual[0, 0, 0]))

time: 23.1 us -> 23.2 us (level)
  no operation moved by 1% of the time
where the time goes in v4:
time: 23.2 us; the launch traced here: 23.1 us
  starting transfers between devices  12.2 us (53%)
  Pallas kernels  6.33 us (27%)
  waiting for transfers between devices  3.85 us (17%)
  between operations  0.68 us (3%)
    ppermute x10, starting transfers between devices, received(): lax.ppermute(value, axis, [(i, (i + (1 if i % 2 == order else -1)) % size...  12.2 us
    ppermute x10, waiting for transfers between devices, received(): lax.ppermute(value, axis, [(i, (i + (1 if i % 2 == order else -1)) % size...  3.85 us
    pallas_call x1, Pallas kernels, on_device(): pl.pallas_call(restrict_kernel, out_shape=(vector, jax.ShapeDtypeStruct((...  2.38 us
    pallas_call x1, Pallas kernels, on_device(): pl.pallas_call(second_kernel, out_shape=(jax.ShapeDtypeStruct((128, 64),...  1.67 us
    pallas_call x1, Pallas kernels, on_device(): pl.pallas_call(functools.partial(operator_kernel, moves=moves), out_shape...  1.24 us
    pallas_call x2, Pallas kernels, partly(): pl.pallas_call(functools.partial(own_kernel, weight=weight), out_shape=ve...  0.68 us
  transfers between devices with their start and end apart: 10, of which 5 were waited for; matrix products, arithmetic and copies ran while one was open for 0% of the time, Pallas kernels for 8%

profile of v4, /device:TPU:0, one launch (start us, length us, event | category | flops | bytes accessed | tf_op | source)
XLA Modules:
  0.0 23.1 jit_solution(6495716802804141447)
XLA Ops:
  0.6 2.4 %shard_map.60 = (f32[64,128]{1,0:T(8,128)S(1)}, bf16[2,12,64,256]{3,2,1,0:T(8,128)(2,1)S(1)}) custom-call(s32[32]{0:T(128)} %pick_ref.1, bf16[2,48,12,2,256]{4,3,2,1,0:T(2,128)(2,1)} %bitcast.12, bf16[2,2,12,32,256]{4,3,2,1,0:T(8,128)(2,1)} %bitcast.13), custom_call_target="tpu_custom_call" | custom-call | tf_op jit(solution)/shard_map/pallas_call | solution.py:167
  3.0 5.1 %collective-permute-start.4 = (f32[64,128]{1,0:T(8,128)S(1)}, f32[64,128]{1,0:T(8,128)S(1)}, u32[]{:S(2)}, u32[]{:S(2)}) collective-permute-start(f32[64,128]{1,0:T(8,128)S(1)} %get-tuple-element.15.source_ref.own_ref), channel_id=1, source_target_pairs={{0,24},{8,16},{16,8},{24,0},{1,25},{9,17},{17,9},{25,1},{2,26},{10... | collective-permute-start | bytes 98312 | tf_op jit(solution)/shard_map/ppermute | solution.py:29
  8.1 2.4 %collective-permute-start.3 = (f32[64,128]{1,0:T(8,128)S(1)}, f32[64,128]{1,0:T(8,128)S(1)}, u32[]{:S(2)}, u32[]{:S(2)}) collective-permute-start(f32[64,128]{1,0:T(8,128)S(1)} %get-tuple-element.15.source_ref.own_ref), channel_id=1, source_target_pairs={{0,6},{2,4},{4,2},{6,0},{1,7},{3,5},{5,3},{7,1},{8,14},{10,12},{12... | collective-permute-start | bytes 98312 | tf_op jit(solution)/shard_map/ppermute | solution.py:29
  10.6 0.0 collective-permute-start.2
  10.6 0.5 %collective-permute-start.1 = (f32[64,128]{1,0:T(8,128)S(1)}, f32[64,128]{1,0:T(8,128)S(1)}, u32[]{:S(2)}, u32[]{:S(2)}) collective-permute-start(f32[64,128]{1,0:T(8,128)S(1)} %get-tuple-element.15.source_ref.own_ref), channel_id=1, source_target_pairs={{0,2},{2,0},{4,6},{6,4},{1,3},{3,1},{5,7},{7,5},{8,10},{10,8},{12,... | collective-permute-start | bytes 98312 | tf_op jit(solution)/shard_map/ppermute | solution.py:29
  11.1 0.0 collective-permute-start
  11.1 1.2 %shard_map.59 = (bf16[256,128]{1,0:T(8,128)(2,1)S(1)}, bf16[256,128]{1,0:T(8,128)(2,1)S(1)}, bf16[256,320]{1,0:T(8,128)(2,1)S(1)}, bf16[256,320]{1,0:T(8,128)(2,1)S(1)}) custom-call(f32[4,2,9,64,128]{4,3,2,1,0:T(8,128)} %bitcast.11), custom_call_target="tpu_custom_call" | custom-call | tf_op jit(solution)/shard_map/pallas_call | solution.py:187
  12.4 0.3 %shard_map.61.base_ref = f32[64,128]{1,0:T(8,128)S(1)} custom-call(bf16[256,128]{1,0:T(8,128)(2,1)S(1)} %get-tuple-element.13.high_ref, bf16[256,128]{1,0:T(8,128)(2,1)S(1)} %get-tuple-element.14.low_ref, f32[64,128]{1,0:T(8,128)S(1)} %get-tuple-element.15.source_ref.own_ref, f32[64,128]{1,0:T(8,128)S(1)} %get-tuple-element.15.source_ref.own_ref), custom_call_target="tpu_custom_call" | custom-call | tf_op jit(solution)/shard_map/pallas_call | solution.py:198
  12.7 0.0 collective-permute-done.4.refs_4_
  12.7 0.4 %collective-permute-done.3.refs_3_ = f32[64,128]{1,0:T(8,128)S(1)} collective-permute-done((f32[64,128]{1,0:T(8,128)S(1)}, f32[64,128]{1,0:T(8,128)S(1)}, u32[]{:S(2)}, u32[]{:S(2)}) %collective-permute-start.3) | collective-permute-done | bytes 32800 | tf_op jit(solution)/shard_map/ppermute | solution.py:29
  13.1 1.4 %collective-permute-done.2.refs_2_ = f32[64,128]{1,0:T(8,128)S(1)} collective-permute-done((f32[64,128]{1,0:T(8,128)S(1)}, f32[64,128]{1,0:T(8,128)S(1)}, u32[]{:S(2)}, u32[]{:S(2)}) %collective-permute-start.2) | collective-permute-done | bytes 32800 | tf_op jit(solution)/shard_map/ppermute | solution.py:29
  14.5 0.0 collective-permute-done.1.refs_1_
  14.5 0.0 collective-permute-done.refs_0_
  14.5 0.3 %shard_map.62.own_ref = f32[64,128]{1,0:T(8,128)S(1)} custom-call(bf16[256,320]{1,0:T(8,128)(2,1)S(1)} %get-tuple-element.10.high_ref, bf16[256,320]{1,0:T(8,128)(2,1)S(1)} %get-tuple-element.11.low_ref, f32[64,128]{1,0:T(8,128)S(1)} %shard_map.61.base_ref, f32[64,128]{1,0:T(8,128)S(1)} %collective-permute-done.refs_0_, ...), custom_call_target="tpu_custom_call" | custom-call | tf_op jit(solution)/shard_map/pallas_call | solution.py:206
  14.9 1.0 %collective-permute-start.9 = (f32[64,128]{1,0:T(8,128)S(1)}, f32[64,128]{1,0:T(8,128)S(1)}, u32[]{:S(2)}, u32[]{:S(2)}) collective-permute-start(f32[64,128]{1,0:T(8,128)S(1)} %shard_map.62.own_ref), channel_id=1, source_target_pairs={{0,24},{8,16},{16,8},{24,0},{1,25},{9,17},{17,9},{25,1},{2,26},{10... | collective-permute-start | bytes 98312 | tf_op jit(solution)/shard_map/ppermute | solution.py:29
  15.8 0.9 %collective-permute-start.8 = (f32[64,128]{1,0:T(8,128)S(1)}, f32[64,128]{1,0:T(8,128)S(1)}, u32[]{:S(2)}, u32[]{:S(2)}) collective-permute-start(f32[64,128]{1,0:T(8,128)S(1)} %shard_map.62.own_ref), channel_id=1, source_target_pairs={{0,6},{2,4},{4,2},{6,0},{1,7},{3,5},{5,3},{7,1},{8,14},{10,12},{12... | collective-permute-start | bytes 98312 | tf_op jit(solution)/shard_map/ppermute | solution.py:29
  16.7 0.8 %collective-permute-start.7 = (f32[64,128]{1,0:T(8,128)S(1)}, f32[64,128]{1,0:T(8,128)S(1)}, u32[]{:S(2)}, u32[]{:S(2)}) collective-permute-start(f32[64,128]{1,0:T(8,128)S(1)} %shard_map.62.own_ref), channel_id=1, source_target_pairs={{0,8},{8,0},{16,24},{24,16},{1,9},{9,1},{17,25},{25,17},{2,10},{10... | collective-permute-start | bytes 98312 | tf_op jit(solution)/shard_map/ppermute | solution.py:29
  17.5 1.5 %collective-permute-start.6 = (f32[64,128]{1,0:T(8,128)S(1)}, f32[64,128]{1,0:T(8,128)S(1)}, u32[]{:S(2)}, u32[]{:S(2)}) collective-permute-start(f32[64,128]{1,0:T(8,128)S(1)} %shard_map.62.own_ref), channel_id=1, source_target_pairs={{0,2},{2,0},{4,6},{6,4},{1,3},{3,1},{5,7},{7,5},{8,10},{10,8},{12,... | collective-permute-start | bytes 98312 | tf_op jit(solution)/shard_map/ppermute | solution.py:29
  19.0 0.3 %shard_map.63.base_ref = f32[64,128]{1,0:T(8,128)S(1)} custom-call(bf16[256,128]{1,0:T(8,128)(2,1)S(1)} %get-tuple-element.13.high_ref, bf16[256,128]{1,0:T(8,128)(2,1)S(1)} %get-tuple-element.14.low_ref, f32[64,128]{1,0:T(8,128)S(1)} %get-tuple-element.15.source_ref.own_ref, f32[64,128]{1,0:T(8,128)S(1)} %shard_map.62.own_ref), custom_call_target="tpu_custom_call" | custom-call | tf_op jit(solution)/shard_map/pallas_call | solution.py:198
  19.3 1.6 %collective-permute-done.9.refs_4_ = f32[64,128]{1,0:T(8,128)S(1)} collective-permute-done((f32[64,128]{1,0:T(8,128)S(1)}, f32[64,128]{1,0:T(8,128)S(1)}, u32[]{:S(2)}, u32[]{:S(2)}) %collective-permute-start.9) | collective-permute-done | bytes 32800 | tf_op jit(solution)/shard_map/ppermute | solution.py:29
  20.9 0.0 collective-permute-done.8.refs_3_
  20.9 0.1 collective-permute-done.7.refs_2_
  21.0 0.4 %collective-permute-done.6.refs_1_ = f32[64,128]{1,0:T(8,128)S(1)} collective-permute-done((f32[64,128]{1,0:T(8,128)S(1)}, f32[64,128]{1,0:T(8,128)S(1)}, u32[]{:S(2)}, u32[]{:S(2)}) %collective-permute-start.6) | collective-permute-done | bytes 32800 | tf_op jit(solution)/shard_map/ppermute | solution.py:29
  21.4 1.7 %shard_map.64 = (f32[128,64]{1,0:T(8,128)}, bf16[2,2,12,32,256]{4,3,2,1,0:T(8,128)(2,1)}) custom-call(bf16[256,320]{1,0:T(8,128)(2,1)S(1)} %get-tuple-element.10.high_ref, bf16[256,320]{1,0:T(8,128)(2,1)S(1)} %get-tuple-element.11.low_ref, bf16[2,12,64,256]{3,2,1,0:T(8,128)(2,1)S(1)} %get-tuple-element.12.matrix_ref, f32[64,128]{1,0:T(8,128)S(1)} %shard_map.63.base_ref, ...), custom_call_target="tpu_custom_call" | custom-call | tf_op jit(solution)/shard_map/pallas_call | solution.py:213
  (2 shorter events, 0.0 us)
Async XLA Ops:
  3.0 9.7 %collective-permute-start.4 = (f32[64,128]{1,0:T(8,128)S(1)}, f32[64,128]{1,0:T(8,128)S(1)}, u32[]{:S(2)}, u32[]{:S(2)}) collective-permute-start(f32[64,128]{1,0:T(8,128)S(1)} %get-tuple-element.15.source_ref.own_ref), channel_id=1, source_target_pairs={{0,24},{8,16},{16,8},{24,0},{1,25},{9,17},{17,9},{25,1},{2,26},{10... | collective-permute-start | bytes 98312 | tf_op jit(solution)/shard_map/ppermute | solution.py:29
  8.1 5.0 %collective-permute-start.3 = (f32[64,128]{1,0:T(8,128)S(1)}, f32[64,128]{1,0:T(8,128)S(1)}, u32[]{:S(2)}, u32[]{:S(2)}) collective-permute-start(f32[64,128]{1,0:T(8,128)S(1)} %get-tuple-element.15.source_ref.own_ref), channel_id=1, source_target_pairs={{0,6},{2,4},{4,2},{6,0},{1,7},{3,5},{5,3},{7,1},{8,14},{10,12},{12... | collective-permute-start | bytes 98312 | tf_op jit(solution)/shard_map/ppermute | solution.py:29
  10.6 3.9 %collective-permute-start.2 = (f32[64,128]{1,0:T(8,128)S(1)}, f32[64,128]{1,0:T(8,128)S(1)}, u32[]{:S(2)}, u32[]{:S(2)}) collective-permute-start(f32[64,128]{1,0:T(8,128)S(1)} %get-tuple-element.15.source_ref.own_ref), channel_id=1, source_target_pairs={{0,8},{8,0},{16,24},{24,16},{1,9},{9,1},{17,25},{25,17},{2,10},{10... | collective-permute-start | bytes 98312 | tf_op jit(solution)/shard_map/ppermute | solution.py:29
  10.6 3.9 %collective-permute-start.1 = (f32[64,128]{1,0:T(8,128)S(1)}, f32[64,128]{1,0:T(8,128)S(1)}, u32[]{:S(2)}, u32[]{:S(2)}) collective-permute-start(f32[64,128]{1,0:T(8,128)S(1)} %get-tuple-element.15.source_ref.own_ref), channel_id=1, source_target_pairs={{0,2},{2,0},{4,6},{6,4},{1,3},{3,1},{5,7},{7,5},{8,10},{10,8},{12,... | collective-permute-start | bytes 98312 | tf_op jit(solution)/shard_map/ppermute | solution.py:29
  11.1 3.4 %collective-permute-start = (f32[64,128]{1,0:T(8,128)S(1)}, f32[64,128]{1,0:T(8,128)S(1)}, u32[]{:S(2)}, u32[]{:S(2)}) collective-permute-start(f32[64,128]{1,0:T(8,128)S(1)} %get-tuple-element.15.source_ref.own_ref), channel_id=1, source_target_pairs={{0,1},{1,0},{2,3},{3,2},{4,5},{5,4},{6,7},{7,6},{8,9},{9,8},{10,11... | collective-permute-start | bytes 98312 | tf_op jit(solution)/shard_map/ppermute | solution.py:29
  14.9 6.0 %collective-permute-start.9 = (f32[64,128]{1,0:T(8,128)S(1)}, f32[64,128]{1,0:T(8,128)S(1)}, u32[]{:S(2)}, u32[]{:S(2)}) collective-permute-start(f32[64,128]{1,0:T(8,128)S(1)} %shard_map.62.own_ref), channel_id=1, source_target_pairs={{0,24},{8,16},{16,8},{24,0},{1,25},{9,17},{17,9},{25,1},{2,26},{10... | collective-permute-start | bytes 98312 | tf_op jit(solution)/shard_map/ppermute | solution.py:29
  15.8 5.1 %collective-permute-start.8 = (f32[64,128]{1,0:T(8,128)S(1)}, f32[64,128]{1,0:T(8,128)S(1)}, u32[]{:S(2)}, u32[]{:S(2)}) collective-permute-start(f32[64,128]{1,0:T(8,128)S(1)} %shard_map.62.own_ref), channel_id=1, source_target_pairs={{0,6},{2,4},{4,2},{6,0},{1,7},{3,5},{5,3},{7,1},{8,14},{10,12},{12... | collective-permute-start | bytes 98312 | tf_op jit(solution)/shard_map/ppermute | solution.py:29
  16.7 4.3 %collective-permute-start.7 = (f32[64,128]{1,0:T(8,128)S(1)}, f32[64,128]{1,0:T(8,128)S(1)}, u32[]{:S(2)}, u32[]{:S(2)}) collective-permute-start(f32[64,128]{1,0:T(8,128)S(1)} %shard_map.62.own_ref), channel_id=1, source_target_pairs={{0,8},{8,0},{16,24},{24,16},{1,9},{9,1},{17,25},{25,17},{2,10},{10... | collective-permute-start | bytes 98312 | tf_op jit(solution)/shard_map/ppermute | solution.py:29
  17.5 3.9 %collective-permute-start.6 = (f32[64,128]{1,0:T(8,128)S(1)}, f32[64,128]{1,0:T(8,128)S(1)}, u32[]{:S(2)}, u32[]{:S(2)}) collective-permute-start(f32[64,128]{1,0:T(8,128)S(1)} %shard_map.62.own_ref), channel_id=1, source_target_pairs={{0,2},{2,0},{4,6},{6,4},{1,3},{3,1},{5,7},{7,5},{8,10},{10,8},{12,... | collective-permute-start | bytes 98312 | tf_op jit(solution)/shard_map/ppermute | solution.py:29
  19.0 2.4 %collective-permute-start.5 = (f32[64,128]{1,0:T(8,128)S(1)}, f32[64,128]{1,0:T(8,128)S(1)}, u32[]{:S(2)}, u32[]{:S(2)}) collective-permute-start(f32[64,128]{1,0:T(8,128)S(1)} %shard_map.62.own_ref), channel_id=1, source_target_pairs={{0,1},{1,0},{2,3},{3,2},{4,5},{5,4},{6,7},{7,6},{8,9},{9,8},{10,11... | collective-permute-start | bytes 98312 | tf_op jit(solution)/shard_map/ppermute | solution.py:29

commit v5 on v3

--- a/solution.py
+++ b/solution.py
@@ -41,33 +41,32 @@
 def restrict_kernel(
     pick_ref, pool_ref, source_ref, out_ref, matrix_ref, pick, pool, source, rows, pick_sem, pool_sems, source_sems
 ):
-    def copies(t, h):
-        part = pl.ds(6 * h, 6)
+    def copies(t):
         return (
-            pltpu.make_async_copy(pool_ref.at[t, :, part], pool.at[t, :, part], pool_sems.at[t, h]),
-            pltpu.make_async_copy(source_ref.at[t, :, part], source.at[t, :, part], source_sems.at[t, h]),
+            pltpu.make_async_copy(pool_ref.at[t], pool.at[t], pool_sems.at[t]),
+            pltpu.make_async_copy(source_ref.at[t], source.at[t], source_sems.at[t]),
         )
 
-    chunks = [(t, h) for t in range(2) for h in range(2)]
     picked = pltpu.make_async_copy(pick_ref, pick, pick_sem)
     picked.start()
-    for chunk in chunks:
-        for copy in copies(*chunk):
+    for t in range(2):
+        for copy in copies(t):
             copy.start()
     picked.wait()
     index = [pick[k] for k in range(32)]
-    for t, h in chunks:
-        for copy in copies(t, h):
+    for t in range(2):
+        for copy in copies(t):
             copy.wait()
-        total = None
-        for a in range(6 * h, 6 * h + 6):
-            matrix = jnp.stack([pool[t, index[k], a] for k in range(32)], axis=0).reshape(64, 256)
-            matrix_ref[t, a] = matrix
-            term = lax.dot_general(
-                matrix, source[t, :, a].reshape(64, 256), (((1,), (1,)), ((), ())), preferred_element_type=F32
-            )
-            total = term if total is None else total + term
-        rows[h, :, 64 * t : 64 * t + 64] = total
+        for h in range(2):
+            total = None
+            for a in range(6 * h, 6 * h + 6):
+                matrix = jnp.stack([pool[t, index[k], a] for k in range(32)], axis=0).reshape(64, 256)
+                matrix_ref[t, a] = matrix
+                term = lax.dot_general(
+                    matrix, source[t, :, a].reshape(64, 256), (((1,), (1,)), ((), ())), preferred_element_type=F32
+                )
+                total = term if total is None else total + term
+            rows[h, :, 64 * t : 64 * t + 64] = total
     for h in range(2):
         plain = rows[h, pl.ds(0, 32, stride=2), :]
         crossed = rows[h, pl.ds(1, 32, stride=2), :]
@@ -167,8 +166,8 @@
             pltpu.VMEM((2, 2, 12, 32, 256), BF16),
             pltpu.VMEM((2, 64, 128), F32),
             pltpu.SemaphoreType.DMA,
-            pltpu.SemaphoreType.DMA((2, 2)),
-            pltpu.SemaphoreType.DMA((2, 2)),
+            pltpu.SemaphoreType.DMA((2,)),
+            pltpu.SemaphoreType.DMA((2,)),
         ],
         compiler_params=limit(6),
     )(hbm(vector_pick), hbm(jnp.swapaxes(candidates[0, 0, 0], 2, 3)), hbm(fine_residual[0, 0, 0]))

time: 23.1 us -> 22.9 us (level)
  Pallas kernels: 6.21 us -> 5.96 us
    pallas_call x1, Pallas kernels: 2.26 us -> 2.01 us  [on_device(): pl.pallas_call(restrict_kernel, out_shape=(vector, jax.ShapeDtypeStruct((...]
where the time goes in v5:
time: 22.9 us; the launch traced here: 22.7 us
  starting transfers between devices  12.2 us (53%)
  Pallas kernels  5.96 us (26%)
  waiting for transfers between devices  3.85 us (17%)
  between operations  0.68 us (3%)
    ppermute x10, starting transfers between devices, received(): lax.ppermute(value, axis, [(i, (i + (1 if i % 2 == order else -1)) % size...  12.2 us
    ppermute x10, waiting for transfers between devices, received(): lax.ppermute(value, axis, [(i, (i + (1 if i % 2 == order else -1)) % size...  3.85 us
    pallas_call x1, Pallas kernels, on_device(): pl.pallas_call(restrict_kernel, out_shape=(vector, jax.ShapeDtypeStruct((...  2.01 us
    pallas_call x1, Pallas kernels, on_device(): pl.pallas_call(second_kernel, out_shape=(jax.ShapeDtypeStruct((128, 64),...  1.67 us
    pallas_call x1, Pallas kernels, on_device(): pl.pallas_call(functools.partial(operator_kernel, moves=moves), out_shape...  1.24 us
    pallas_call x2, Pallas kernels, partly(): pl.pallas_call(functools.partial(own_kernel, weight=weight), out_shape=ve...  0.68 us
  transfers between devices with their start and end apart: 10, of which 5 were waited for; matrix products, arithmetic and copies ran while one was open for 0% of the time, Pallas kernels for 8%

profile of v5, /device:TPU:0, one launch (start us, length us, event | category | flops | bytes accessed | tf_op | source)
XLA Modules:
  0.0 22.7 jit_solution(6340962020398288986)
XLA Ops:
  0.6 2.0 %shard_map.60 = (f32[64,128]{1,0:T(8,128)S(1)}, bf16[2,12,64,256]{3,2,1,0:T(8,128)(2,1)S(1)}) custom-call(s32[32]{0:T(128)} %pick_ref.1, bf16[2,48,12,2,256]{4,3,2,1,0:T(2,128)(2,1)} %bitcast.12, bf16[2,2,12,32,256]{4,3,2,1,0:T(8,128)(2,1)} %bitcast.13), custom_call_target="tpu_custom_call" | custom-call | tf_op jit(solution)/shard_map/pallas_call | solution.py:158
  2.7 5.1 %collective-permute-start.4 = (f32[64,128]{1,0:T(8,128)S(1)}, f32[64,128]{1,0:T(8,128)S(1)}, u32[]{:S(2)}, u32[]{:S(2)}) collective-permute-start(f32[64,128]{1,0:T(8,128)S(1)} %get-tuple-element.15.source_ref.own_ref), channel_id=1, source_target_pairs={{0,24},{8,16},{16,8},{24,0},{1,25},{9,17},{17,9},{25,1},{2,26},{10... | collective-permute-start | bytes 98312 | tf_op jit(solution)/shard_map/ppermute | solution.py:29
  7.8 2.4 %collective-permute-start.3 = (f32[64,128]{1,0:T(8,128)S(1)}, f32[64,128]{1,0:T(8,128)S(1)}, u32[]{:S(2)}, u32[]{:S(2)}) collective-permute-start(f32[64,128]{1,0:T(8,128)S(1)} %get-tuple-element.15.source_ref.own_ref), channel_id=1, source_target_pairs={{0,6},{2,4},{4,2},{6,0},{1,7},{3,5},{5,3},{7,1},{8,14},{10,12},{12... | collective-permute-start | bytes 98312 | tf_op jit(solution)/shard_map/ppermute | solution.py:29
  10.2 0.0 collective-permute-start.2
  10.2 0.5 %collective-permute-start.1 = (f32[64,128]{1,0:T(8,128)S(1)}, f32[64,128]{1,0:T(8,128)S(1)}, u32[]{:S(2)}, u32[]{:S(2)}) collective-permute-start(f32[64,128]{1,0:T(8,128)S(1)} %get-tuple-element.15.source_ref.own_ref), channel_id=1, source_target_pairs={{0,2},{2,0},{4,6},{6,4},{1,3},{3,1},{5,7},{7,5},{8,10},{10,8},{12,... | collective-permute-start | bytes 98312 | tf_op jit(solution)/shard_map/ppermute | solution.py:29
  10.8 0.0 collective-permute-start
  10.8 1.2 %shard_map.59 = (bf16[256,128]{1,0:T(8,128)(2,1)S(1)}, bf16[256,128]{1,0:T(8,128)(2,1)S(1)}, bf16[256,320]{1,0:T(8,128)(2,1)S(1)}, bf16[256,320]{1,0:T(8,128)(2,1)S(1)}) custom-call(f32[4,2,9,64,128]{4,3,2,1,0:T(8,128)} %bitcast.11), custom_call_target="tpu_custom_call" | custom-call | tf_op jit(solution)/shard_map/pallas_call | solution.py:178
  12.0 0.3 %shard_map.61.base_ref = f32[64,128]{1,0:T(8,128)S(1)} custom-call(bf16[256,128]{1,0:T(8,128)(2,1)S(1)} %get-tuple-element.13.high_ref, bf16[256,128]{1,0:T(8,128)(2,1)S(1)} %get-tuple-element.14.low_ref, f32[64,128]{1,0:T(8,128)S(1)} %get-tuple-element.15.source_ref.own_ref, f32[64,128]{1,0:T(8,128)S(1)} %get-tuple-element.15.source_ref.own_ref), custom_call_target="tpu_custom_call" | custom-call | tf_op jit(solution)/shard_map/pallas_call | solution.py:189
  12.4 0.0 collective-permute-done.4.refs_4_
  12.4 0.4 %collective-permute-done.3.refs_3_ = f32[64,128]{1,0:T(8,128)S(1)} collective-permute-done((f32[64,128]{1,0:T(8,128)S(1)}, f32[64,128]{1,0:T(8,128)S(1)}, u32[]{:S(2)}, u32[]{:S(2)}) %collective-permute-start.3) | collective-permute-done | bytes 32800 | tf_op jit(solution)/shard_map/ppermute | solution.py:29
  12.7 1.4 %collective-permute-done.2.refs_2_ = f32[64,128]{1,0:T(8,128)S(1)} collective-permute-done((f32[64,128]{1,0:T(8,128)S(1)}, f32[64,128]{1,0:T(8,128)S(1)}, u32[]{:S(2)}, u32[]{:S(2)}) %collective-permute-start.2) | collective-permute-done | bytes 32800 | tf_op jit(solution)/shard_map/ppermute | solution.py:29
  14.1 0.3 %shard_map.62.own_ref = f32[64,128]{1,0:T(8,128)S(1)} custom-call(bf16[256,320]{1,0:T(8,128)(2,1)S(1)} %get-tuple-element.10.high_ref, bf16[256,320]{1,0:T(8,128)(2,1)S(1)} %get-tuple-element.11.low_ref, f32[64,128]{1,0:T(8,128)S(1)} %shard_map.61.base_ref, f32[64,128]{1,0:T(8,128)S(1)} %collective-permute-done.refs_0_, ...), custom_call_target="tpu_custom_call" | custom-call | tf_op jit(solution)/shard_map/pallas_call | solution.py:197
  14.5 1.0 %collective-permute-start.9 = (f32[64,128]{1,0:T(8,128)S(1)}, f32[64,128]{1,0:T(8,128)S(1)}, u32[]{:S(2)}, u32[]{:S(2)}) collective-permute-start(f32[64,128]{1,0:T(8,128)S(1)} %shard_map.62.own_ref), channel_id=1, source_target_pairs={{0,24},{8,16},{16,8},{24,0},{1,25},{9,17},{17,9},{25,1},{2,26},{10... | collective-permute-start | bytes 98312 | tf_op jit(solution)/shard_map/ppermute | solution.py:29
  15.4 0.9 %collective-permute-start.8 = (f32[64,128]{1,0:T(8,128)S(1)}, f32[64,128]{1,0:T(8,128)S(1)}, u32[]{:S(2)}, u32[]{:S(2)}) collective-permute-start(f32[64,128]{1,0:T(8,128)S(1)} %shard_map.62.own_ref), channel_id=1, source_target_pairs={{0,6},{2,4},{4,2},{6,0},{1,7},{3,5},{5,3},{7,1},{8,14},{10,12},{12... | collective-permute-start | bytes 98312 | tf_op jit(solution)/shard_map/ppermute | solution.py:29
  16.4 0.8 %collective-permute-start.7 = (f32[64,128]{1,0:T(8,128)S(1)}, f32[64,128]{1,0:T(8,128)S(1)}, u32[]{:S(2)}, u32[]{:S(2)}) collective-permute-start(f32[64,128]{1,0:T(8,128)S(1)} %shard_map.62.own_ref), channel_id=1, source_target_pairs={{0,8},{8,0},{16,24},{24,16},{1,9},{9,1},{17,25},{25,17},{2,10},{10... | collective-permute-start | bytes 98312 | tf_op jit(solution)/shard_map/ppermute | solution.py:29
  17.1 1.5 %collective-permute-start.6 = (f32[64,128]{1,0:T(8,128)S(1)}, f32[64,128]{1,0:T(8,128)S(1)}, u32[]{:S(2)}, u32[]{:S(2)}) collective-permute-start(f32[64,128]{1,0:T(8,128)S(1)} %shard_map.62.own_ref), channel_id=1, source_target_pairs={{0,2},{2,0},{4,6},{6,4},{1,3},{3,1},{5,7},{7,5},{8,10},{10,8},{12,... | collective-permute-start | bytes 98312 | tf_op jit(solution)/shard_map/ppermute | solution.py:29
  18.6 0.0 collective-permute-start.5
  18.6 0.3 %shard_map.63.base_ref = f32[64,128]{1,0:T(8,128)S(1)} custom-call(bf16[256,128]{1,0:T(8,128)(2,1)S(1)} %get-tuple-element.13.high_ref, bf16[256,128]{1,0:T(8,128)(2,1)S(1)} %get-tuple-element.14.low_ref, f32[64,128]{1,0:T(8,128)S(1)} %get-tuple-element.15.source_ref.own_ref, f32[64,128]{1,0:T(8,128)S(1)} %shard_map.62.own_ref), custom_call_target="tpu_custom_call" | custom-call | tf_op jit(solution)/shard_map/pallas_call | solution.py:189
  19.0 1.5 %collective-permute-done.9.refs_4_ = f32[64,128]{1,0:T(8,128)S(1)} collective-permute-done((f32[64,128]{1,0:T(8,128)S(1)}, f32[64,128]{1,0:T(8,128)S(1)}, u32[]{:S(2)}, u32[]{:S(2)}) %collective-permute-start.9) | collective-permute-done | bytes 32800 | tf_op jit(solution)/shard_map/ppermute | solution.py:29
  20.5 0.0 collective-permute-done.8.refs_3_
  20.6 0.1 collective-permute-done.7.refs_2_
  20.6 0.4 %collective-permute-done.6.refs_1_ = f32[64,128]{1,0:T(8,128)S(1)} collective-permute-done((f32[64,128]{1,0:T(8,128)S(1)}, f32[64,128]{1,0:T(8,128)S(1)}, u32[]{:S(2)}, u32[]{:S(2)}) %collective-permute-start.6) | collective-permute-done | bytes 32800 | tf_op jit(solution)/shard_map/ppermute | solution.py:29
  21.1 0.0 collective-permute-done.5.refs_0_
  21.1 1.7 %shard_map.64 = (f32[128,64]{1,0:T(8,128)}, bf16[2,2,12,32,256]{4,3,2,1,0:T(8,128)(2,1)}) custom-call(bf16[256,320]{1,0:T(8,128)(2,1)S(1)} %get-tuple-element.10.high_ref, bf16[256,320]{1,0:T(8,128)(2,1)S(1)} %get-tuple-element.11.low_ref, bf16[2,12,64,256]{3,2,1,0:T(8,128)(2,1)S(1)} %get-tuple-element.12.matrix_ref, f32[64,128]{1,0:T(8,128)S(1)} %shard_map.63.base_ref, ...), custom_call_target="tpu_custom_call" | custom-call | tf_op jit(solution)/shard_map/pallas_call | solution.py:204
  (2 shorter events, 0.0 us)
Async XLA Ops:
  2.7 9.7 %collective-permute-start.4 = (f32[64,128]{1,0:T(8,128)S(1)}, f32[64,128]{1,0:T(8,128)S(1)}, u32[]{:S(2)}, u32[]{:S(2)}) collective-permute-start(f32[64,128]{1,0:T(8,128)S(1)} %get-tuple-element.15.source_ref.own_ref), channel_id=1, source_target_pairs={{0,24},{8,16},{16,8},{24,0},{1,25},{9,17},{17,9},{25,1},{2,26},{10... | collective-permute-start | bytes 98312 | tf_op jit(solution)/shard_map/ppermute | solution.py:29
  7.8 5.0 %collective-permute-start.3 = (f32[64,128]{1,0:T(8,128)S(1)}, f32[64,128]{1,0:T(8,128)S(1)}, u32[]{:S(2)}, u32[]{:S(2)}) collective-permute-start(f32[64,128]{1,0:T(8,128)S(1)} %get-tuple-element.15.source_ref.own_ref), channel_id=1, source_target_pairs={{0,6},{2,4},{4,2},{6,0},{1,7},{3,5},{5,3},{7,1},{8,14},{10,12},{12... | collective-permute-start | bytes 98312 | tf_op jit(solution)/shard_map/ppermute | solution.py:29
  10.2 3.9 %collective-permute-start.2 = (f32[64,128]{1,0:T(8,128)S(1)}, f32[64,128]{1,0:T(8,128)S(1)}, u32[]{:S(2)}, u32[]{:S(2)}) collective-permute-start(f32[64,128]{1,0:T(8,128)S(1)} %get-tuple-element.15.source_ref.own_ref), channel_id=1, source_target_pairs={{0,8},{8,0},{16,24},{24,16},{1,9},{9,1},{17,25},{25,17},{2,10},{10... | collective-permute-start | bytes 98312 | tf_op jit(solution)/shard_map/ppermute | solution.py:29
  10.2 3.9 %collective-permute-start.1 = (f32[64,128]{1,0:T(8,128)S(1)}, f32[64,128]{1,0:T(8,128)S(1)}, u32[]{:S(2)}, u32[]{:S(2)}) collective-permute-start(f32[64,128]{1,0:T(8,128)S(1)} %get-tuple-element.15.source_ref.own_ref), channel_id=1, source_target_pairs={{0,2},{2,0},{4,6},{6,4},{1,3},{3,1},{5,7},{7,5},{8,10},{10,8},{12,... | collective-permute-start | bytes 98312 | tf_op jit(solution)/shard_map/ppermute | solution.py:29
  10.8 3.4 %collective-permute-start = (f32[64,128]{1,0:T(8,128)S(1)}, f32[64,128]{1,0:T(8,128)S(1)}, u32[]{:S(2)}, u32[]{:S(2)}) collective-permute-start(f32[64,128]{1,0:T(8,128)S(1)} %get-tuple-element.15.source_ref.own_ref), channel_id=1, source_target_pairs={{0,1},{1,0},{2,3},{3,2},{4,5},{5,4},{6,7},{7,6},{8,9},{9,8},{10,11... | collective-permute-start | bytes 98312 | tf_op jit(solution)/shard_map/ppermute | solution.py:29
  14.5 6.0 %collective-permute-start.9 = (f32[64,128]{1,0:T(8,128)S(1)}, f32[64,128]{1,0:T(8,128)S(1)}, u32[]{:S(2)}, u32[]{:S(2)}) collective-permute-start(f32[64,128]{1,0:T(8,128)S(1)} %shard_map.62.own_ref), channel_id=1, source_target_pairs={{0,24},{8,16},{16,8},{24,0},{1,25},{9,17},{17,9},{25,1},{2,26},{10... | collective-permute-start | bytes 98312 | tf_op jit(solution)/shard_map/ppermute | solution.py:29
  15.4 5.1 %collective-permute-start.8 = (f32[64,128]{1,0:T(8,128)S(1)}, f32[64,128]{1,0:T(8,128)S(1)}, u32[]{:S(2)}, u32[]{:S(2)}) collective-permute-start(f32[64,128]{1,0:T(8,128)S(1)} %shard_map.62.own_ref), channel_id=1, source_target_pairs={{0,6},{2,4},{4,2},{6,0},{1,7},{3,5},{5,3},{7,1},{8,14},{10,12},{12... | collective-permute-start | bytes 98312 | tf_op jit(solution)/shard_map/ppermute | solution.py:29
  16.4 4.3 %collective-permute-start.7 = (f32[64,128]{1,0:T(8,128)S(1)}, f32[64,128]{1,0:T(8,128)S(1)}, u32[]{:S(2)}, u32[]{:S(2)}) collective-permute-start(f32[64,128]{1,0:T(8,128)S(1)} %shard_map.62.own_ref), channel_id=1, source_target_pairs={{0,8},{8,0},{16,24},{24,16},{1,9},{9,1},{17,25},{25,17},{2,10},{10... | collective-permute-start | bytes 98312 | tf_op jit(solution)/shard_map/ppermute | solution.py:29
  17.1 3.9 %collective-permute-start.6 = (f32[64,128]{1,0:T(8,128)S(1)}, f32[64,128]{1,0:T(8,128)S(1)}, u32[]{:S(2)}, u32[]{:S(2)}) collective-permute-start(f32[64,128]{1,0:T(8,128)S(1)} %shard_map.62.own_ref), channel_id=1, source_target_pairs={{0,2},{2,0},{4,6},{6,4},{1,3},{3,1},{5,7},{7,5},{8,10},{10,8},{12,... | collective-permute-start | bytes 98312 | tf_op jit(solution)/shard_map/ppermute | solution.py:29
  18.6 2.4 %collective-permute-start.5 = (f32[64,128]{1,0:T(8,128)S(1)}, f32[64,128]{1,0:T(8,128)S(1)}, u32[]{:S(2)}, u32[]{:S(2)}) collective-permute-start(f32[64,128]{1,0:T(8,128)S(1)} %shard_map.62.own_ref), channel_id=1, source_target_pairs={{0,1},{1,0},{2,3},{3,2},{4,5},{5,4},{6,7},{7,6},{8,9},{9,8},{10,11... | collective-permute-start | bytes 98312 | tf_op jit(solution)/shard_map/ppermute | solution.py:29

commit v6 on v5

--- a/solution.py
+++ b/solution.py
@@ -136,14 +136,13 @@
         rows[h, pl.ds(1, 32, stride=2), :] = crossed[32 * h : 32 * h + 32]
         spread = rows[h].T.astype(BF16)
         for t in range(2):
-            for start in (6 * h, 6 * h + 3):
-                for a in range(start, start + 3):
-                    product = jnp.dot(spread[64 * t : 64 * t + 64], matrix_ref[t, a], preferred_element_type=F32)
-                    result[t, :, a] = product.astype(BF16).reshape(2, 32, 256)
-                part = (t, slice(None), pl.ds(start, 3))
-                copy = pltpu.make_async_copy(result.at[part], out_ref.at[part], sems.at[t, start // 3])
-                copy.start()
-                copies.append(copy)
+            for a in range(6 * h, 6 * h + 6):
+                product = jnp.dot(spread[64 * t : 64 * t + 64], matrix_ref[t, a], preferred_element_type=F32)
+                result[t, :, a] = product.astype(BF16).reshape(2, 32, 256)
+            part = (t, slice(None), pl.ds(6 * h, 6))
+            copy = pltpu.make_async_copy(result.at[part], out_ref.at[part], sems.at[t, h])
+            copy.start()
+            copies.append(copy)
     for copy in copies:
         copy.wait()
 
@@ -214,7 +213,7 @@
             pltpu.VMEM((2, 2, 12, 32, 256), BF16),
             pltpu.VMEM((2, 64, 128), F32),
             pltpu.SemaphoreType.DMA,
-            pltpu.SemaphoreType.DMA((2, 4)),
+            pltpu.SemaphoreType.DMA((2, 2)),
         ],
         compiler_params=limit(4),
     )(*far_operator, matrix, partly(first, 0.5), *received(first, moves))

time: 22.9 us -> 22.9 us (level)
  no operation moved by 1% of the time
where the time goes in v6:
time: 22.9 us; the launch traced here: 22.7 us
  starting transfers between devices  12.2 us (53%)
  Pallas kernels  5.95 us (26%)
  waiting for transfers between devices  3.85 us (17%)
  between operations  0.68 us (3%)
    ppermute x10, starting transfers between devices, received(): lax.ppermute(value, axis, [(i, (i + (1 if i % 2 == order else -1)) % size...  12.2 us
    ppermute x10, waiting for transfers between devices, received(): lax.ppermute(value, axis, [(i, (i + (1 if i % 2 == order else -1)) % size...  3.85 us
    pallas_call x1, Pallas kernels, on_device(): pl.pallas_call(restrict_kernel, out_shape=(vector, jax.ShapeDtypeStruct((...  2.01 us
    pallas_call x1, Pallas kernels, on_device(): pl.pallas_call(second_kernel, out_shape=(jax.ShapeDtypeStruct((128, 64),...  1.67 us
    pallas_call x1, Pallas kernels, on_device(): pl.pallas_call(functools.partial(operator_kernel, moves=moves), out_shape...  1.24 us
    pallas_call x2, Pallas kernels, partly(): pl.pallas_call(functools.partial(own_kernel, weight=weight), out_shape=ve...  0.68 us
  transfers between devices with their start and end apart: 10, of which 5 were waited for; matrix products, arithmetic and copies ran while one was open for 0% of the time, Pallas kernels for 8%

profile of v6, /device:TPU:0, one launch (start us, length us, event | category | flops | bytes accessed | tf_op | source)
XLA Modules:
  0.0 22.7 jit_solution(8359946006717369933)
XLA Ops:
  0.6 2.0 %shard_map.60 = (f32[64,128]{1,0:T(8,128)S(1)}, bf16[2,12,64,256]{3,2,1,0:T(8,128)(2,1)S(1)}) custom-call(s32[32]{0:T(128)} %pick_ref.1, bf16[2,48,12,2,256]{4,3,2,1,0:T(2,128)(2,1)} %bitcast.12, bf16[2,2,12,32,256]{4,3,2,1,0:T(8,128)(2,1)} %bitcast.13), custom_call_target="tpu_custom_call" | custom-call | tf_op jit(solution)/shard_map/pallas_call | solution.py:157
  2.7 5.1 %collective-permute-start.4 = (f32[64,128]{1,0:T(8,128)S(1)}, f32[64,128]{1,0:T(8,128)S(1)}, u32[]{:S(2)}, u32[]{:S(2)}) collective-permute-start(f32[64,128]{1,0:T(8,128)S(1)} %get-tuple-element.15.source_ref.own_ref), channel_id=1, source_target_pairs={{0,24},{8,16},{16,8},{24,0},{1,25},{9,17},{17,9},{25,1},{2,26},{10... | collective-permute-start | bytes 98312 | tf_op jit(solution)/shard_map/ppermute | solution.py:29
  7.8 2.4 %collective-permute-start.3 = (f32[64,128]{1,0:T(8,128)S(1)}, f32[64,128]{1,0:T(8,128)S(1)}, u32[]{:S(2)}, u32[]{:S(2)}) collective-permute-start(f32[64,128]{1,0:T(8,128)S(1)} %get-tuple-element.15.source_ref.own_ref), channel_id=1, source_target_pairs={{0,6},{2,4},{4,2},{6,0},{1,7},{3,5},{5,3},{7,1},{8,14},{10,12},{12... | collective-permute-start | bytes 98312 | tf_op jit(solution)/shard_map/ppermute | solution.py:29
  10.2 0.0 collective-permute-start.2
  10.2 0.5 %collective-permute-start.1 = (f32[64,128]{1,0:T(8,128)S(1)}, f32[64,128]{1,0:T(8,128)S(1)}, u32[]{:S(2)}, u32[]{:S(2)}) collective-permute-start(f32[64,128]{1,0:T(8,128)S(1)} %get-tuple-element.15.source_ref.own_ref), channel_id=1, source_target_pairs={{0,2},{2,0},{4,6},{6,4},{1,3},{3,1},{5,7},{7,5},{8,10},{10,8},{12,... | collective-permute-start | bytes 98312 | tf_op jit(solution)/shard_map/ppermute | solution.py:29
  10.8 0.0 collective-permute-start
  10.8 1.2 %shard_map.59 = (bf16[256,128]{1,0:T(8,128)(2,1)S(1)}, bf16[256,128]{1,0:T(8,128)(2,1)S(1)}, bf16[256,320]{1,0:T(8,128)(2,1)S(1)}, bf16[256,320]{1,0:T(8,128)(2,1)S(1)}) custom-call(f32[4,2,9,64,128]{4,3,2,1,0:T(8,128)} %bitcast.11), custom_call_target="tpu_custom_call" | custom-call | tf_op jit(solution)/shard_map/pallas_call | solution.py:177
  12.0 0.3 %shard_map.61.base_ref = f32[64,128]{1,0:T(8,128)S(1)} custom-call(bf16[256,128]{1,0:T(8,128)(2,1)S(1)} %get-tuple-element.13.high_ref, bf16[256,128]{1,0:T(8,128)(2,1)S(1)} %get-tuple-element.14.low_ref, f32[64,128]{1,0:T(8,128)S(1)} %get-tuple-element.15.source_ref.own_ref, f32[64,128]{1,0:T(8,128)S(1)} %get-tuple-element.15.source_ref.own_ref), custom_call_target="tpu_custom_call" | custom-call | tf_op jit(solution)/shard_map/pallas_call | solution.py:188
  12.4 0.0 collective-permute-done.4.refs_4_
  12.4 0.4 %collective-permute-done.3.refs_3_ = f32[64,128]{1,0:T(8,128)S(1)} collective-permute-done((f32[64,128]{1,0:T(8,128)S(1)}, f32[64,128]{1,0:T(8,128)S(1)}, u32[]{:S(2)}, u32[]{:S(2)}) %collective-permute-start.3) | collective-permute-done | bytes 32800 | tf_op jit(solution)/shard_map/ppermute | solution.py:29
  12.7 1.4 %collective-permute-done.2.refs_2_ = f32[64,128]{1,0:T(8,128)S(1)} collective-permute-done((f32[64,128]{1,0:T(8,128)S(1)}, f32[64,128]{1,0:T(8,128)S(1)}, u32[]{:S(2)}, u32[]{:S(2)}) %collective-permute-start.2) | collective-permute-done | bytes 32800 | tf_op jit(solution)/shard_map/ppermute | solution.py:29
  14.1 0.0 collective-permute-done.1.refs_1_
  14.1 0.0 collective-permute-done.refs_0_
  14.1 0.3 %shard_map.62.own_ref = f32[64,128]{1,0:T(8,128)S(1)} custom-call(bf16[256,320]{1,0:T(8,128)(2,1)S(1)} %get-tuple-element.10.high_ref, bf16[256,320]{1,0:T(8,128)(2,1)S(1)} %get-tuple-element.11.low_ref, f32[64,128]{1,0:T(8,128)S(1)} %shard_map.61.base_ref, f32[64,128]{1,0:T(8,128)S(1)} %collective-permute-done.refs_0_, ...), custom_call_target="tpu_custom_call" | custom-call | tf_op jit(solution)/shard_map/pallas_call | solution.py:196
  14.5 1.0 %collective-permute-start.9 = (f32[64,128]{1,0:T(8,128)S(1)}, f32[64,128]{1,0:T(8,128)S(1)}, u32[]{:S(2)}, u32[]{:S(2)}) collective-permute-start(f32[64,128]{1,0:T(8,128)S(1)} %shard_map.62.own_ref), channel_id=1, source_target_pairs={{0,24},{8,16},{16,8},{24,0},{1,25},{9,17},{17,9},{25,1},{2,26},{10... | collective-permute-start | bytes 98312 | tf_op jit(solution)/shard_map/ppermute | solution.py:29
  15.4 0.9 %collective-permute-start.8 = (f32[64,128]{1,0:T(8,128)S(1)}, f32[64,128]{1,0:T(8,128)S(1)}, u32[]{:S(2)}, u32[]{:S(2)}) collective-permute-start(f32[64,128]{1,0:T(8,128)S(1)} %shard_map.62.own_ref), channel_id=1, source_target_pairs={{0,6},{2,4},{4,2},{6,0},{1,7},{3,5},{5,3},{7,1},{8,14},{10,12},{12... | collective-permute-start | bytes 98312 | tf_op jit(solution)/shard_map/ppermute | solution.py:29
  16.4 0.8 %collective-permute-start.7 = (f32[64,128]{1,0:T(8,128)S(1)}, f32[64,128]{1,0:T(8,128)S(1)}, u32[]{:S(2)}, u32[]{:S(2)}) collective-permute-start(f32[64,128]{1,0:T(8,128)S(1)} %shard_map.62.own_ref), channel_id=1, source_target_pairs={{0,8},{8,0},{16,24},{24,16},{1,9},{9,1},{17,25},{25,17},{2,10},{10... | collective-permute-start | bytes 98312 | tf_op jit(solution)/shard_map/ppermute | solution.py:29
  17.1 1.5 %collective-permute-start.6 = (f32[64,128]{1,0:T(8,128)S(1)}, f32[64,128]{1,0:T(8,128)S(1)}, u32[]{:S(2)}, u32[]{:S(2)}) collective-permute-start(f32[64,128]{1,0:T(8,128)S(1)} %shard_map.62.own_ref), channel_id=1, source_target_pairs={{0,2},{2,0},{4,6},{6,4},{1,3},{3,1},{5,7},{7,5},{8,10},{10,8},{12,... | collective-permute-start | bytes 98312 | tf_op jit(solution)/shard_map/ppermute | solution.py:29
  18.6 0.3 %shard_map.63.base_ref = f32[64,128]{1,0:T(8,128)S(1)} custom-call(bf16[256,128]{1,0:T(8,128)(2,1)S(1)} %get-tuple-element.13.high_ref, bf16[256,128]{1,0:T(8,128)(2,1)S(1)} %get-tuple-element.14.low_ref, f32[64,128]{1,0:T(8,128)S(1)} %get-tuple-element.15.source_ref.own_ref, f32[64,128]{1,0:T(8,128)S(1)} %shard_map.62.own_ref), custom_call_target="tpu_custom_call" | custom-call | tf_op jit(solution)/shard_map/pallas_call | solution.py:188
  19.0 1.5 %collective-permute-done.9.refs_4_ = f32[64,128]{1,0:T(8,128)S(1)} collective-permute-done((f32[64,128]{1,0:T(8,128)S(1)}, f32[64,128]{1,0:T(8,128)S(1)}, u32[]{:S(2)}, u32[]{:S(2)}) %collective-permute-start.9) | collective-permute-done | bytes 32800 | tf_op jit(solution)/shard_map/ppermute | solution.py:29
  20.5 0.0 collective-permute-done.8.refs_3_
  20.6 0.1 collective-permute-done.7.refs_2_
  20.6 0.4 %collective-permute-done.6.refs_1_ = f32[64,128]{1,0:T(8,128)S(1)} collective-permute-done((f32[64,128]{1,0:T(8,128)S(1)}, f32[64,128]{1,0:T(8,128)S(1)}, u32[]{:S(2)}, u32[]{:S(2)}) %collective-permute-start.6) | collective-permute-done | bytes 32800 | tf_op jit(solution)/shard_map/ppermute | solution.py:29
  21.1 1.7 %shard_map.64 = (f32[128,64]{1,0:T(8,128)}, bf16[2,2,12,32,256]{4,3,2,1,0:T(8,128)(2,1)}) custom-call(bf16[256,320]{1,0:T(8,128)(2,1)S(1)} %get-tuple-element.10.high_ref, bf16[256,320]{1,0:T(8,128)(2,1)S(1)} %get-tuple-element.11.low_ref, bf16[2,12,64,256]{3,2,1,0:T(8,128)(2,1)S(1)} %get-tuple-element.12.matrix_ref, f32[64,128]{1,0:T(8,128)S(1)} %shard_map.63.base_ref, ...), custom_call_target="tpu_custom_call" | custom-call | tf_op jit(solution)/shard_map/pallas_call | solution.py:203
  (2 shorter events, 0.0 us)
Async XLA Ops:
  2.7 9.7 %collective-permute-start.4 = (f32[64,128]{1,0:T(8,128)S(1)}, f32[64,128]{1,0:T(8,128)S(1)}, u32[]{:S(2)}, u32[]{:S(2)}) collective-permute-start(f32[64,128]{1,0:T(8,128)S(1)} %get-tuple-element.15.source_ref.own_ref), channel_id=1, source_target_pairs={{0,24},{8,16},{16,8},{24,0},{1,25},{9,17},{17,9},{25,1},{2,26},{10... | collective-permute-start | bytes 98312 | tf_op jit(solution)/shard_map/ppermute | solution.py:29
  7.8 5.0 %collective-permute-start.3 = (f32[64,128]{1,0:T(8,128)S(1)}, f32[64,128]{1,0:T(8,128)S(1)}, u32[]{:S(2)}, u32[]{:S(2)}) collective-permute-start(f32[64,128]{1,0:T(8,128)S(1)} %get-tuple-element.15.source_ref.own_ref), channel_id=1, source_target_pairs={{0,6},{2,4},{4,2},{6,0},{1,7},{3,5},{5,3},{7,1},{8,14},{10,12},{12... | collective-permute-start | bytes 98312 | tf_op jit(solution)/shard_map/ppermute | solution.py:29
  10.2 3.9 %collective-permute-start.2 = (f32[64,128]{1,0:T(8,128)S(1)}, f32[64,128]{1,0:T(8,128)S(1)}, u32[]{:S(2)}, u32[]{:S(2)}) collective-permute-start(f32[64,128]{1,0:T(8,128)S(1)} %get-tuple-element.15.source_ref.own_ref), channel_id=1, source_target_pairs={{0,8},{8,0},{16,24},{24,16},{1,9},{9,1},{17,25},{25,17},{2,10},{10... | collective-permute-start | bytes 98312 | tf_op jit(solution)/shard_map/ppermute | solution.py:29
  10.2 3.9 %collective-permute-start.1 = (f32[64,128]{1,0:T(8,128)S(1)}, f32[64,128]{1,0:T(8,128)S(1)}, u32[]{:S(2)}, u32[]{:S(2)}) collective-permute-start(f32[64,128]{1,0:T(8,128)S(1)} %get-tuple-element.15.source_ref.own_ref), channel_id=1, source_target_pairs={{0,2},{2,0},{4,6},{6,4},{1,3},{3,1},{5,7},{7,5},{8,10},{10,8},{12,... | collective-permute-start | bytes 98312 | tf_op jit(solution)/shard_map/ppermute | solution.py:29
  10.8 3.4 %collective-permute-start = (f32[64,128]{1,0:T(8,128)S(1)}, f32[64,128]{1,0:T(8,128)S(1)}, u32[]{:S(2)}, u32[]{:S(2)}) collective-permute-start(f32[64,128]{1,0:T(8,128)S(1)} %get-tuple-element.15.source_ref.own_ref), channel_id=1, source_target_pairs={{0,1},{1,0},{2,3},{3,2},{4,5},{5,4},{6,7},{7,6},{8,9},{9,8},{10,11... | collective-permute-start | bytes 98312 | tf_op jit(solution)/shard_map/ppermute | solution.py:29
  14.5 6.0 %collective-permute-start.9 = (f32[64,128]{1,0:T(8,128)S(1)}, f32[64,128]{1,0:T(8,128)S(1)}, u32[]{:S(2)}, u32[]{:S(2)}) collective-permute-start(f32[64,128]{1,0:T(8,128)S(1)} %shard_map.62.own_ref), channel_id=1, source_target_pairs={{0,24},{8,16},{16,8},{24,0},{1,25},{9,17},{17,9},{25,1},{2,26},{10... | collective-permute-start | bytes 98312 | tf_op jit(solution)/shard_map/ppermute | solution.py:29
  15.4 5.1 %collective-permute-start.8 = (f32[64,128]{1,0:T(8,128)S(1)}, f32[64,128]{1,0:T(8,128)S(1)}, u32[]{:S(2)}, u32[]{:S(2)}) collective-permute-start(f32[64,128]{1,0:T(8,128)S(1)} %shard_map.62.own_ref), channel_id=1, source_target_pairs={{0,6},{2,4},{4,2},{6,0},{1,7},{3,5},{5,3},{7,1},{8,14},{10,12},{12... | collective-permute-start | bytes 98312 | tf_op jit(solution)/shard_map/ppermute | solution.py:29
  16.4 4.3 %collective-permute-start.7 = (f32[64,128]{1,0:T(8,128)S(1)}, f32[64,128]{1,0:T(8,128)S(1)}, u32[]{:S(2)}, u32[]{:S(2)}) collective-permute-start(f32[64,128]{1,0:T(8,128)S(1)} %shard_map.62.own_ref), channel_id=1, source_target_pairs={{0,8},{8,0},{16,24},{24,16},{1,9},{9,1},{17,25},{25,17},{2,10},{10... | collective-permute-start | bytes 98312 | tf_op jit(solution)/shard_map/ppermute | solution.py:29
  17.1 3.9 %collective-permute-start.6 = (f32[64,128]{1,0:T(8,128)S(1)}, f32[64,128]{1,0:T(8,128)S(1)}, u32[]{:S(2)}, u32[]{:S(2)}) collective-permute-start(f32[64,128]{1,0:T(8,128)S(1)} %shard_map.62.own_ref), channel_id=1, source_target_pairs={{0,2},{2,0},{4,6},{6,4},{1,3},{3,1},{5,7},{7,5},{8,10},{10,8},{12,... | collective-permute-start | bytes 98312 | tf_op jit(solution)/shard_map/ppermute | solution.py:29
  18.6 2.4 %collective-permute-start.5 = (f32[64,128]{1,0:T(8,128)S(1)}, f32[64,128]{1,0:T(8,128)S(1)}, u32[]{:S(2)}, u32[]{:S(2)}) collective-permute-start(f32[64,128]{1,0:T(8,128)S(1)} %shard_map.62.own_ref), channel_id=1, source_target_pairs={{0,1},{1,0},{2,3},{3,2},{4,5},{5,4},{6,7},{7,6},{8,9},{9,8},{10,11... | collective-permute-start | bytes 98312 | tf_op jit(solution)/shard_map/ppermute | solution.py:29

commit v7 on v6

--- a/solution.py
+++ b/solution.py
@@ -39,24 +39,21 @@
 
 
 def restrict_kernel(
-    pick_ref, pool_ref, source_ref, out_ref, matrix_ref, pick, pool, source, rows, pick_sem, pool_sems, source_sems
+    pick_ref, pool_ref, source_ref, out_ref, matrix_ref, pick, pool, source, rows, pick_sem, pool_sems, source_sem
 ):
-    def copies(t):
-        return (
-            pltpu.make_async_copy(pool_ref.at[t], pool.at[t], pool_sems.at[t]),
-            pltpu.make_async_copy(source_ref.at[t], source.at[t], source_sems.at[t]),
-        )
-
+    pools = [pltpu.make_async_copy(pool_ref.at[t], pool.at[t], pool_sems.at[t]) for t in range(2)]
+    fine = pltpu.make_async_copy(source_ref, source, source_sem)
     picked = pltpu.make_async_copy(pick_ref, pick, pick_sem)
     picked.start()
-    for t in range(2):
-        for copy in copies(t):
-            copy.start()
+    pools[0].start()
+    fine.start()
+    pools[1].start()
     picked.wait()
     index = [pick[k] for k in range(32)]
     for t in range(2):
-        for copy in copies(t):
-            copy.wait()
+        pools[t].wait()
+        if t == 0:
+            fine.wait()
         for h in range(2):
             total = None
             for a in range(6 * h, 6 * h + 6):
@@ -166,7 +163,7 @@
             pltpu.VMEM((2, 64, 128), F32),
             pltpu.SemaphoreType.DMA,
             pltpu.SemaphoreType.DMA((2,)),
-            pltpu.SemaphoreType.DMA((2,)),
+            pltpu.SemaphoreType.DMA,
         ],
         compiler_params=limit(6),
     )(hbm(vector_pick), hbm(jnp.swapaxes(candidates[0, 0, 0], 2, 3)), hbm(fine_residual[0, 0, 0]))

time: 22.9 us -> 23 us (level)
  no operation moved by 1% of the time
where the time goes in v7:
time: 23 us; the launch traced here: 22.8 us
  starting transfers between devices  12.2 us (53%)
  Pallas kernels  6.08 us (26%)
  waiting for transfers between devices  3.85 us (17%)
  between operations  0.68 us (3%)
    ppermute x10, starting transfers between devices, received(): lax.ppermute(value, axis, [(i, (i + (1 if i % 2 == order else -1)) % size...  12.2 us
    ppermute x10, waiting for transfers between devices, received(): lax.ppermute(value, axis, [(i, (i + (1 if i % 2 == order else -1)) % size...  3.85 us
    pallas_call x1, Pallas kernels, on_device(): pl.pallas_call(restrict_kernel, out_shape=(vector, jax.ShapeDtypeStruct((...  2.14 us
    pallas_call x1, Pallas kernels, on_device(): pl.pallas_call(second_kernel, out_shape=(jax.ShapeDtypeStruct((128, 64),...  1.67 us
    pallas_call x1, Pallas kernels, on_device(): pl.pallas_call(functools.partial(operator_kernel, moves=moves), out_shape...  1.24 us
    pallas_call x2, Pallas kernels, partly(): pl.pallas_call(functools.partial(own_kernel, weight=weight), out_shape=ve...  0.68 us
  transfers between devices with their start and end apart: 10, of which 5 were waited for; matrix products, arithmetic and copies ran while one was open for 0% of the time, Pallas kernels for 8%

profile of v7, /device:TPU:0, one launch (start us, length us, event | category | flops | bytes accessed | tf_op | source)
XLA Modules:
  0.0 22.8 jit_solution(13244426766603998325)
XLA Ops:
  0.6 2.1 %shard_map.60 = (f32[64,128]{1,0:T(8,128)S(1)}, bf16[2,12,64,256]{3,2,1,0:T(8,128)(2,1)S(1)}) custom-call(s32[32]{0:T(128)} %pick_ref.1, bf16[2,48,12,2,256]{4,3,2,1,0:T(2,128)(2,1)} %bitcast.12, bf16[2,2,12,32,256]{4,3,2,1,0:T(8,128)(2,1)} %bitcast.13), custom_call_target="tpu_custom_call" | custom-call | tf_op jit(solution)/shard_map/pallas_call | solution.py:154
  2.8 5.1 %collective-permute-start.4 = (f32[64,128]{1,0:T(8,128)S(1)}, f32[64,128]{1,0:T(8,128)S(1)}, u32[]{:S(2)}, u32[]{:S(2)}) collective-permute-start(f32[64,128]{1,0:T(8,128)S(1)} %get-tuple-element.15.source_ref.own_ref), channel_id=1, source_target_pairs={{0,24},{8,16},{16,8},{24,0},{1,25},{9,17},{17,9},{25,1},{2,26},{10... | collective-permute-start | bytes 98312 | tf_op jit(solution)/shard_map/ppermute | solution.py:29
  7.9 2.4 %collective-permute-start.3 = (f32[64,128]{1,0:T(8,128)S(1)}, f32[64,128]{1,0:T(8,128)S(1)}, u32[]{:S(2)}, u32[]{:S(2)}) collective-permute-start(f32[64,128]{1,0:T(8,128)S(1)} %get-tuple-element.15.source_ref.own_ref), channel_id=1, source_target_pairs={{0,6},{2,4},{4,2},{6,0},{1,7},{3,5},{5,3},{7,1},{8,14},{10,12},{12... | collective-permute-start | bytes 98312 | tf_op jit(solution)/shard_map/ppermute | solution.py:29
  10.3 0.0 collective-permute-start.2
  10.3 0.5 %collective-permute-start.1 = (f32[64,128]{1,0:T(8,128)S(1)}, f32[64,128]{1,0:T(8,128)S(1)}, u32[]{:S(2)}, u32[]{:S(2)}) collective-permute-start(f32[64,128]{1,0:T(8,128)S(1)} %get-tuple-element.15.source_ref.own_ref), channel_id=1, source_target_pairs={{0,2},{2,0},{4,6},{6,4},{1,3},{3,1},{5,7},{7,5},{8,10},{10,8},{12,... | collective-permute-start | bytes 98312 | tf_op jit(solution)/shard_map/ppermute | solution.py:29
  10.9 0.0 collective-permute-start
  10.9 1.2 %shard_map.59 = (bf16[256,128]{1,0:T(8,128)(2,1)S(1)}, bf16[256,128]{1,0:T(8,128)(2,1)S(1)}, bf16[256,320]{1,0:T(8,128)(2,1)S(1)}, bf16[256,320]{1,0:T(8,128)(2,1)S(1)}) custom-call(f32[4,2,9,64,128]{4,3,2,1,0:T(8,128)} %bitcast.11), custom_call_target="tpu_custom_call" | custom-call | tf_op jit(solution)/shard_map/pallas_call | solution.py:174
  12.1 0.3 %shard_map.61.base_ref = f32[64,128]{1,0:T(8,128)S(1)} custom-call(bf16[256,128]{1,0:T(8,128)(2,1)S(1)} %get-tuple-element.13.high_ref, bf16[256,128]{1,0:T(8,128)(2,1)S(1)} %get-tuple-element.14.low_ref, f32[64,128]{1,0:T(8,128)S(1)} %get-tuple-element.15.source_ref.own_ref, f32[64,128]{1,0:T(8,128)S(1)} %get-tuple-element.15.source_ref.own_ref), custom_call_target="tpu_custom_call" | custom-call | tf_op jit(solution)/shard_map/pallas_call | solution.py:185
  12.5 0.0 collective-permute-done.4.refs_4_
  12.5 0.4 %collective-permute-done.3.refs_3_ = f32[64,128]{1,0:T(8,128)S(1)} collective-permute-done((f32[64,128]{1,0:T(8,128)S(1)}, f32[64,128]{1,0:T(8,128)S(1)}, u32[]{:S(2)}, u32[]{:S(2)}) %collective-permute-start.3) | collective-permute-done | bytes 32800 | tf_op jit(solution)/shard_map/ppermute | solution.py:29
  12.9 1.4 %collective-permute-done.2.refs_2_ = f32[64,128]{1,0:T(8,128)S(1)} collective-permute-done((f32[64,128]{1,0:T(8,128)S(1)}, f32[64,128]{1,0:T(8,128)S(1)}, u32[]{:S(2)}, u32[]{:S(2)}) %collective-permute-start.2) | collective-permute-done | bytes 32800 | tf_op jit(solution)/shard_map/ppermute | solution.py:29
  14.3 0.3 %shard_map.62.own_ref = f32[64,128]{1,0:T(8,128)S(1)} custom-call(bf16[256,320]{1,0:T(8,128)(2,1)S(1)} %get-tuple-element.10.high_ref, bf16[256,320]{1,0:T(8,128)(2,1)S(1)} %get-tuple-element.11.low_ref, f32[64,128]{1,0:T(8,128)S(1)} %shard_map.61.base_ref, f32[64,128]{1,0:T(8,128)S(1)} %collective-permute-done.refs_0_, ...), custom_call_target="tpu_custom_call" | custom-call | tf_op jit(solution)/shard_map/pallas_call | solution.py:193
  14.6 1.0 %collective-permute-start.9 = (f32[64,128]{1,0:T(8,128)S(1)}, f32[64,128]{1,0:T(8,128)S(1)}, u32[]{:S(2)}, u32[]{:S(2)}) collective-permute-start(f32[64,128]{1,0:T(8,128)S(1)} %shard_map.62.own_ref), channel_id=1, source_target_pairs={{0,24},{8,16},{16,8},{24,0},{1,25},{9,17},{17,9},{25,1},{2,26},{10... | collective-permute-start | bytes 98312 | tf_op jit(solution)/shard_map/ppermute | solution.py:29
  15.6 0.9 %collective-permute-start.8 = (f32[64,128]{1,0:T(8,128)S(1)}, f32[64,128]{1,0:T(8,128)S(1)}, u32[]{:S(2)}, u32[]{:S(2)}) collective-permute-start(f32[64,128]{1,0:T(8,128)S(1)} %shard_map.62.own_ref), channel_id=1, source_target_pairs={{0,6},{2,4},{4,2},{6,0},{1,7},{3,5},{5,3},{7,1},{8,14},{10,12},{12... | collective-permute-start | bytes 98312 | tf_op jit(solution)/shard_map/ppermute | solution.py:29
  16.5 0.8 %collective-permute-start.7 = (f32[64,128]{1,0:T(8,128)S(1)}, f32[64,128]{1,0:T(8,128)S(1)}, u32[]{:S(2)}, u32[]{:S(2)}) collective-permute-start(f32[64,128]{1,0:T(8,128)S(1)} %shard_map.62.own_ref), channel_id=1, source_target_pairs={{0,8},{8,0},{16,24},{24,16},{1,9},{9,1},{17,25},{25,17},{2,10},{10... | collective-permute-start | bytes 98312 | tf_op jit(solution)/shard_map/ppermute | solution.py:29
  17.3 1.5 %collective-permute-start.6 = (f32[64,128]{1,0:T(8,128)S(1)}, f32[64,128]{1,0:T(8,128)S(1)}, u32[]{:S(2)}, u32[]{:S(2)}) collective-permute-start(f32[64,128]{1,0:T(8,128)S(1)} %shard_map.62.own_ref), channel_id=1, source_target_pairs={{0,2},{2,0},{4,6},{6,4},{1,3},{3,1},{5,7},{7,5},{8,10},{10,8},{12,... | collective-permute-start | bytes 98312 | tf_op jit(solution)/shard_map/ppermute | solution.py:29
  18.8 0.0 collective-permute-start.5
  18.8 0.3 %shard_map.63.base_ref = f32[64,128]{1,0:T(8,128)S(1)} custom-call(bf16[256,128]{1,0:T(8,128)(2,1)S(1)} %get-tuple-element.13.high_ref, bf16[256,128]{1,0:T(8,128)(2,1)S(1)} %get-tuple-element.14.low_ref, f32[64,128]{1,0:T(8,128)S(1)} %get-tuple-element.15.source_ref.own_ref, f32[64,128]{1,0:T(8,128)S(1)} %shard_map.62.own_ref), custom_call_target="tpu_custom_call" | custom-call | tf_op jit(solution)/shard_map/pallas_call | solution.py:185
  19.1 1.6 %collective-permute-done.9.refs_4_ = f32[64,128]{1,0:T(8,128)S(1)} collective-permute-done((f32[64,128]{1,0:T(8,128)S(1)}, f32[64,128]{1,0:T(8,128)S(1)}, u32[]{:S(2)}, u32[]{:S(2)}) %collective-permute-start.9) | collective-permute-done | bytes 32800 | tf_op jit(solution)/shard_map/ppermute | solution.py:29
  20.7 0.0 collective-permute-done.8.refs_3_
  20.7 0.1 collective-permute-done.7.refs_2_
  20.8 0.4 %collective-permute-done.6.refs_1_ = f32[64,128]{1,0:T(8,128)S(1)} collective-permute-done((f32[64,128]{1,0:T(8,128)S(1)}, f32[64,128]{1,0:T(8,128)S(1)}, u32[]{:S(2)}, u32[]{:S(2)}) %collective-permute-start.6) | collective-permute-done | bytes 32800 | tf_op jit(solution)/shard_map/ppermute | solution.py:29
  21.2 0.0 collective-permute-done.5.refs_0_
  21.2 1.7 %shard_map.64 = (f32[128,64]{1,0:T(8,128)}, bf16[2,2,12,32,256]{4,3,2,1,0:T(8,128)(2,1)}) custom-call(bf16[256,320]{1,0:T(8,128)(2,1)S(1)} %get-tuple-element.10.high_ref, bf16[256,320]{1,0:T(8,128)(2,1)S(1)} %get-tuple-element.11.low_ref, bf16[2,12,64,256]{3,2,1,0:T(8,128)(2,1)S(1)} %get-tuple-element.12.matrix_ref, f32[64,128]{1,0:T(8,128)S(1)} %shard_map.63.base_ref, ...), custom_call_target="tpu_custom_call" | custom-call | tf_op jit(solution)/shard_map/pallas_call | solution.py:200
  (2 shorter events, 0.0 us)
Async XLA Ops:
  2.8 9.7 %collective-permute-start.4 = (f32[64,128]{1,0:T(8,128)S(1)}, f32[64,128]{1,0:T(8,128)S(1)}, u32[]{:S(2)}, u32[]{:S(2)}) collective-permute-start(f32[64,128]{1,0:T(8,128)S(1)} %get-tuple-element.15.source_ref.own_ref), channel_id=1, source_target_pairs={{0,24},{8,16},{16,8},{24,0},{1,25},{9,17},{17,9},{25,1},{2,26},{10... | collective-permute-start | bytes 98312 | tf_op jit(solution)/shard_map/ppermute | solution.py:29
  7.9 5.0 %collective-permute-start.3 = (f32[64,128]{1,0:T(8,128)S(1)}, f32[64,128]{1,0:T(8,128)S(1)}, u32[]{:S(2)}, u32[]{:S(2)}) collective-permute-start(f32[64,128]{1,0:T(8,128)S(1)} %get-tuple-element.15.source_ref.own_ref), channel_id=1, source_target_pairs={{0,6},{2,4},{4,2},{6,0},{1,7},{3,5},{5,3},{7,1},{8,14},{10,12},{12... | collective-permute-start | bytes 98312 | tf_op jit(solution)/shard_map/ppermute | solution.py:29
  10.3 3.9 %collective-permute-start.2 = (f32[64,128]{1,0:T(8,128)S(1)}, f32[64,128]{1,0:T(8,128)S(1)}, u32[]{:S(2)}, u32[]{:S(2)}) collective-permute-start(f32[64,128]{1,0:T(8,128)S(1)} %get-tuple-element.15.source_ref.own_ref), channel_id=1, source_target_pairs={{0,8},{8,0},{16,24},{24,16},{1,9},{9,1},{17,25},{25,17},{2,10},{10... | collective-permute-start | bytes 98312 | tf_op jit(solution)/shard_map/ppermute | solution.py:29
  10.3 3.9 %collective-permute-start.1 = (f32[64,128]{1,0:T(8,128)S(1)}, f32[64,128]{1,0:T(8,128)S(1)}, u32[]{:S(2)}, u32[]{:S(2)}) collective-permute-start(f32[64,128]{1,0:T(8,128)S(1)} %get-tuple-element.15.source_ref.own_ref), channel_id=1, source_target_pairs={{0,2},{2,0},{4,6},{6,4},{1,3},{3,1},{5,7},{7,5},{8,10},{10,8},{12,... | collective-permute-start | bytes 98312 | tf_op jit(solution)/shard_map/ppermute | solution.py:29
  10.9 3.4 %collective-permute-start = (f32[64,128]{1,0:T(8,128)S(1)}, f32[64,128]{1,0:T(8,128)S(1)}, u32[]{:S(2)}, u32[]{:S(2)}) collective-permute-start(f32[64,128]{1,0:T(8,128)S(1)} %get-tuple-element.15.source_ref.own_ref), channel_id=1, source_target_pairs={{0,1},{1,0},{2,3},{3,2},{4,5},{5,4},{6,7},{7,6},{8,9},{9,8},{10,11... | collective-permute-start | bytes 98312 | tf_op jit(solution)/shard_map/ppermute | solution.py:29
  14.6 6.0 %collective-permute-start.9 = (f32[64,128]{1,0:T(8,128)S(1)}, f32[64,128]{1,0:T(8,128)S(1)}, u32[]{:S(2)}, u32[]{:S(2)}) collective-permute-start(f32[64,128]{1,0:T(8,128)S(1)} %shard_map.62.own_ref), channel_id=1, source_target_pairs={{0,24},{8,16},{16,8},{24,0},{1,25},{9,17},{17,9},{25,1},{2,26},{10... | collective-permute-start | bytes 98312 | tf_op jit(solution)/shard_map/ppermute | solution.py:29
  15.6 5.1 %collective-permute-start.8 = (f32[64,128]{1,0:T(8,128)S(1)}, f32[64,128]{1,0:T(8,128)S(1)}, u32[]{:S(2)}, u32[]{:S(2)}) collective-permute-start(f32[64,128]{1,0:T(8,128)S(1)} %shard_map.62.own_ref), channel_id=1, source_target_pairs={{0,6},{2,4},{4,2},{6,0},{1,7},{3,5},{5,3},{7,1},{8,14},{10,12},{12... | collective-permute-start | bytes 98312 | tf_op jit(solution)/shard_map/ppermute | solution.py:29
  16.5 4.3 %collective-permute-start.7 = (f32[64,128]{1,0:T(8,128)S(1)}, f32[64,128]{1,0:T(8,128)S(1)}, u32[]{:S(2)}, u32[]{:S(2)}) collective-permute-start(f32[64,128]{1,0:T(8,128)S(1)} %shard_map.62.own_ref), channel_id=1, source_target_pairs={{0,8},{8,0},{16,24},{24,16},{1,9},{9,1},{17,25},{25,17},{2,10},{10... | collective-permute-start | bytes 98312 | tf_op jit(solution)/shard_map/ppermute | solution.py:29
  17.3 3.9 %collective-permute-start.6 = (f32[64,128]{1,0:T(8,128)S(1)}, f32[64,128]{1,0:T(8,128)S(1)}, u32[]{:S(2)}, u32[]{:S(2)}) collective-permute-start(f32[64,128]{1,0:T(8,128)S(1)} %shard_map.62.own_ref), channel_id=1, source_target_pairs={{0,2},{2,0},{4,6},{6,4},{1,3},{3,1},{5,7},{7,5},{8,10},{10,8},{12,... | collective-permute-start | bytes 98312 | tf_op jit(solution)/shard_map/ppermute | solution.py:29
  18.8 2.4 %collective-permute-start.5 = (f32[64,128]{1,0:T(8,128)S(1)}, f32[64,128]{1,0:T(8,128)S(1)}, u32[]{:S(2)}, u32[]{:S(2)}) collective-permute-start(f32[64,128]{1,0:T(8,128)S(1)} %shard_map.62.own_ref), channel_id=1, source_target_pairs={{0,1},{1,0},{2,3},{3,2},{4,5},{5,4},{6,7},{7,6},{8,9},{9,8},{10,11... | collective-permute-start | bytes 98312 | tf_op jit(solution)/shard_map/ppermute | solution.py:29

commit v8 on v6

--- a/solution.py
+++ b/solution.py
@@ -58,15 +58,17 @@
         for copy in copies(t):
             copy.wait()
         for h in range(2):
-            total = None
-            for a in range(6 * h, 6 * h + 6):
-                matrix = jnp.stack([pool[t, index[k], a] for k in range(32)], axis=0).reshape(64, 256)
-                matrix_ref[t, a] = matrix
-                term = lax.dot_general(
-                    matrix, source[t, :, a].reshape(64, 256), (((1,), (1,)), ((), ())), preferred_element_type=F32
-                )
-                total = term if total is None else total + term
-            rows[h, :, 64 * t : 64 * t + 64] = total
+            span = slice(1536 * h, 1536 * h + 1536)
+            groups = [
+                jnp.stack([pool[t, index[k], :, span] for k in range(start, start + 8)], axis=0).reshape(16, 1536)
+                for start in range(0, 32, 8)
+            ]
+            matrix = jnp.concatenate(groups, axis=0)
+            matrix_ref[t, :, span] = matrix
+            fine = jnp.concatenate([source[t, :, a].reshape(64, 256) for a in range(6 * h, 6 * h + 6)], axis=1)
+            rows[h, :, 64 * t : 64 * t + 64] = lax.dot_general(
+                matrix, fine, (((1,), (1,)), ((), ())), preferred_element_type=F32
+            )
     for h in range(2):
         plain = rows[h, pl.ds(0, 32, stride=2), :]
         crossed = rows[h, pl.ds(1, 32, stride=2), :]
@@ -137,7 +139,7 @@
         spread = rows[h].T.astype(BF16)
         for t in range(2):
             for a in range(6 * h, 6 * h + 6):
-                product = jnp.dot(spread[64 * t : 64 * t + 64], matrix_ref[t, a], preferred_element_type=F32)
+                product = jnp.dot(spread[64 * t : 64 * t + 64], matrix_ref[t, :, 256 * a : 256 * a + 256], preferred_element_type=F32)
                 result[t, :, a] = product.astype(BF16).reshape(2, 32, 256)
             part = (t, slice(None), pl.ds(6 * h, 6))
             copy = pltpu.make_async_copy(result.at[part], out_ref.at[part], sems.at[t, h])
@@ -156,12 +158,12 @@
     hbm = functools.partial(pltpu.with_memory_space_constraint, memory_space=pltpu.HBM)
     restricted, matrix = pl.pallas_call(
         restrict_kernel,
-        out_shape=(vector, jax.ShapeDtypeStruct((2, 12, 64, 256), BF16)),
+        out_shape=(vector, jax.ShapeDtypeStruct((2, 64, 3072), BF16)),
         in_specs=[HBM, HBM, HBM],
         out_specs=(VMEM, VMEM),
         scratch_shapes=[
             pltpu.SMEM((32,), jnp.int32),
-            pltpu.VMEM((2, 48, 12, 2, 256), BF16),
+            pltpu.VMEM((2, 48, 2, 3072), BF16),
             pltpu.VMEM((2, 2, 12, 32, 256), BF16),
             pltpu.VMEM((2, 64, 128), F32),
             pltpu.SemaphoreType.DMA,
@@ -169,7 +171,7 @@
             pltpu.SemaphoreType.DMA((2,)),
         ],
         compiler_params=limit(6),
-    )(hbm(vector_pick), hbm(jnp.swapaxes(candidates[0, 0, 0], 2, 3)), hbm(fine_residual[0, 0, 0]))
+    )(hbm(vector_pick), hbm(candidates.reshape((2, 48, 2, 3072))), hbm(fine_residual[0, 0, 0]))
 
     moves = present(MOVES)
     own_half = jax.ShapeDtypeStruct((256, 128), BF16)

time: 22.9 us -> 22.8 us (level)
  transfers between devices with their start and end apart: 10 -> 10, of which waited for: 5 -> 5; matrix products, arithmetic and copies ran while one was open for 0% -> 0% of each run, Pallas kernels for 8% -> 9%
where the time goes in v8:
time: 22.8 us; the launch traced here: 22.6 us
  starting transfers between devices  12.2 us (54%)
  Pallas kernels  5.87 us (26%)
  waiting for transfers between devices  3.85 us (17%)
  between operations  0.68 us (3%)
    ppermute x10, starting transfers between devices, received(): lax.ppermute(value, axis, [(i, (i + (1 if i % 2 == order else -1)) % size...  12.2 us
    ppermute x10, waiting for transfers between devices, received(): lax.ppermute(value, axis, [(i, (i + (1 if i % 2 == order else -1)) % size...  3.85 us
    pallas_call x1, Pallas kernels, on_device(): pl.pallas_call(restrict_kernel, out_shape=(vector, jax.ShapeDtypeStruct((...  1.93 us
    pallas_call x1, Pallas kernels, on_device(): pl.pallas_call(second_kernel, out_shape=(jax.ShapeDtypeStruct((128, 64),...  1.67 us
    pallas_call x1, Pallas kernels, on_device(): pl.pallas_call(functools.partial(operator_kernel, moves=moves), out_shape...  1.24 us
    pallas_call x2, Pallas kernels, partly(): pl.pallas_call(functools.partial(own_kernel, weight=weight), out_shape=ve...  0.68 us
  transfers between devices with their start and end apart: 10, of which 5 were waited for; matrix products, arithmetic and copies ran while one was open for 0% of the time, Pallas kernels for 9%

profile of v8, /device:TPU:0, one launch (start us, length us, event | category | flops | bytes accessed | tf_op | source)
XLA Modules:
  0.0 22.6 jit_solution(10196881113022231263)
XLA Ops:
  0.6 1.9 %shard_map.60 = (f32[64,128]{1,0:T(8,128)S(1)}, bf16[2,64,3072]{2,1,0:T(8,128)(2,1)S(1)}) custom-call(s32[32]{0:T(128)} %pick_ref.1, bf16[2,48,2,3072]{3,2,1,0:T(2,128)(2,1)} %bitcast.10, bf16[2,2,12,32,256]{4,3,2,1,0:T(8,128)(2,1)} %bitcast.11), custom_call_target="tpu_custom_call" | custom-call | tf_op jit(solution)/shard_map/pallas_call | solution.py:159
  2.6 5.1 %collective-permute-start.4 = (f32[64,128]{1,0:T(8,128)S(1)}, f32[64,128]{1,0:T(8,128)S(1)}, u32[]{:S(2)}, u32[]{:S(2)}) collective-permute-start(f32[64,128]{1,0:T(8,128)S(1)} %get-tuple-element.15.source_ref.own_ref), channel_id=1, source_target_pairs={{0,24},{8,16},{16,8},{24,0},{1,25},{9,17},{17,9},{25,1},{2,26},{10... | collective-permute-start | bytes 98312 | tf_op jit(solution)/shard_map/ppermute | solution.py:29
  7.7 2.4 %collective-permute-start.3 = (f32[64,128]{1,0:T(8,128)S(1)}, f32[64,128]{1,0:T(8,128)S(1)}, u32[]{:S(2)}, u32[]{:S(2)}) collective-permute-start(f32[64,128]{1,0:T(8,128)S(1)} %get-tuple-element.15.source_ref.own_ref), channel_id=1, source_target_pairs={{0,6},{2,4},{4,2},{6,0},{1,7},{3,5},{5,3},{7,1},{8,14},{10,12},{12... | collective-permute-start | bytes 98312 | tf_op jit(solution)/shard_map/ppermute | solution.py:29
  10.1 0.0 collective-permute-start.2
  10.1 0.5 %collective-permute-start.1 = (f32[64,128]{1,0:T(8,128)S(1)}, f32[64,128]{1,0:T(8,128)S(1)}, u32[]{:S(2)}, u32[]{:S(2)}) collective-permute-start(f32[64,128]{1,0:T(8,128)S(1)} %get-tuple-element.15.source_ref.own_ref), channel_id=1, source_target_pairs={{0,2},{2,0},{4,6},{6,4},{1,3},{3,1},{5,7},{7,5},{8,10},{10,8},{12,... | collective-permute-start | bytes 98312 | tf_op jit(solution)/shard_map/ppermute | solution.py:29
  10.7 0.0 collective-permute-start
  10.7 1.2 %shard_map.59 = (bf16[256,128]{1,0:T(8,128)(2,1)S(1)}, bf16[256,128]{1,0:T(8,128)(2,1)S(1)}, bf16[256,320]{1,0:T(8,128)(2,1)S(1)}, bf16[256,320]{1,0:T(8,128)(2,1)S(1)}) custom-call(f32[4,2,9,64,128]{4,3,2,1,0:T(8,128)} %bitcast.9), custom_call_target="tpu_custom_call" | custom-call | tf_op jit(solution)/shard_map/pallas_call | solution.py:179
  11.9 0.3 %shard_map.61.base_ref = f32[64,128]{1,0:T(8,128)S(1)} custom-call(bf16[256,128]{1,0:T(8,128)(2,1)S(1)} %get-tuple-element.13.high_ref, bf16[256,128]{1,0:T(8,128)(2,1)S(1)} %get-tuple-element.14.low_ref, f32[64,128]{1,0:T(8,128)S(1)} %get-tuple-element.15.source_ref.own_ref, f32[64,128]{1,0:T(8,128)S(1)} %get-tuple-element.15.source_ref.own_ref), custom_call_target="tpu_custom_call" | custom-call | tf_op jit(solution)/shard_map/pallas_call | solution.py:190
  12.3 0.0 collective-permute-done.4.refs_4_
  12.3 0.4 %collective-permute-done.3.refs_3_ = f32[64,128]{1,0:T(8,128)S(1)} collective-permute-done((f32[64,128]{1,0:T(8,128)S(1)}, f32[64,128]{1,0:T(8,128)S(1)}, u32[]{:S(2)}, u32[]{:S(2)}) %collective-permute-start.3) | collective-permute-done | bytes 32800 | tf_op jit(solution)/shard_map/ppermute | solution.py:29
  12.7 1.4 %collective-permute-done.2.refs_2_ = f32[64,128]{1,0:T(8,128)S(1)} collective-permute-done((f32[64,128]{1,0:T(8,128)S(1)}, f32[64,128]{1,0:T(8,128)S(1)}, u32[]{:S(2)}, u32[]{:S(2)}) %collective-permute-start.2) | collective-permute-done | bytes 32800 | tf_op jit(solution)/shard_map/ppermute | solution.py:29
  14.1 0.0 collective-permute-done.1.refs_1_
  14.1 0.0 collective-permute-done.refs_0_
  14.1 0.3 %shard_map.62.own_ref = f32[64,128]{1,0:T(8,128)S(1)} custom-call(bf16[256,320]{1,0:T(8,128)(2,1)S(1)} %get-tuple-element.10.high_ref, bf16[256,320]{1,0:T(8,128)(2,1)S(1)} %get-tuple-element.11.low_ref, f32[64,128]{1,0:T(8,128)S(1)} %shard_map.61.base_ref, f32[64,128]{1,0:T(8,128)S(1)} %collective-permute-done.refs_0_, ...), custom_call_target="tpu_custom_call" | custom-call | tf_op jit(solution)/shard_map/pallas_call | solution.py:198
  14.4 1.0 %collective-permute-start.9 = (f32[64,128]{1,0:T(8,128)S(1)}, f32[64,128]{1,0:T(8,128)S(1)}, u32[]{:S(2)}, u32[]{:S(2)}) collective-permute-start(f32[64,128]{1,0:T(8,128)S(1)} %shard_map.62.own_ref), channel_id=1, source_target_pairs={{0,24},{8,16},{16,8},{24,0},{1,25},{9,17},{17,9},{25,1},{2,26},{10... | collective-permute-start | bytes 98312 | tf_op jit(solution)/shard_map/ppermute | solution.py:29
  15.4 0.9 %collective-permute-start.8 = (f32[64,128]{1,0:T(8,128)S(1)}, f32[64,128]{1,0:T(8,128)S(1)}, u32[]{:S(2)}, u32[]{:S(2)}) collective-permute-start(f32[64,128]{1,0:T(8,128)S(1)} %shard_map.62.own_ref), channel_id=1, source_target_pairs={{0,6},{2,4},{4,2},{6,0},{1,7},{3,5},{5,3},{7,1},{8,14},{10,12},{12... | collective-permute-start | bytes 98312 | tf_op jit(solution)/shard_map/ppermute | solution.py:29
  16.3 0.8 %collective-permute-start.7 = (f32[64,128]{1,0:T(8,128)S(1)}, f32[64,128]{1,0:T(8,128)S(1)}, u32[]{:S(2)}, u32[]{:S(2)}) collective-permute-start(f32[64,128]{1,0:T(8,128)S(1)} %shard_map.62.own_ref), channel_id=1, source_target_pairs={{0,8},{8,0},{16,24},{24,16},{1,9},{9,1},{17,25},{25,17},{2,10},{10... | collective-permute-start | bytes 98312 | tf_op jit(solution)/shard_map/ppermute | solution.py:29
  17.1 1.5 %collective-permute-start.6 = (f32[64,128]{1,0:T(8,128)S(1)}, f32[64,128]{1,0:T(8,128)S(1)}, u32[]{:S(2)}, u32[]{:S(2)}) collective-permute-start(f32[64,128]{1,0:T(8,128)S(1)} %shard_map.62.own_ref), channel_id=1, source_target_pairs={{0,2},{2,0},{4,6},{6,4},{1,3},{3,1},{5,7},{7,5},{8,10},{10,8},{12,... | collective-permute-start | bytes 98312 | tf_op jit(solution)/shard_map/ppermute | solution.py:29
  18.5 0.3 %shard_map.63.base_ref = f32[64,128]{1,0:T(8,128)S(1)} custom-call(bf16[256,128]{1,0:T(8,128)(2,1)S(1)} %get-tuple-element.13.high_ref, bf16[256,128]{1,0:T(8,128)(2,1)S(1)} %get-tuple-element.14.low_ref, f32[64,128]{1,0:T(8,128)S(1)} %get-tuple-element.15.source_ref.own_ref, f32[64,128]{1,0:T(8,128)S(1)} %shard_map.62.own_ref), custom_call_target="tpu_custom_call" | custom-call | tf_op jit(solution)/shard_map/pallas_call | solution.py:190
  18.9 1.6 %collective-permute-done.9.refs_4_ = f32[64,128]{1,0:T(8,128)S(1)} collective-permute-done((f32[64,128]{1,0:T(8,128)S(1)}, f32[64,128]{1,0:T(8,128)S(1)}, u32[]{:S(2)}, u32[]{:S(2)}) %collective-permute-start.9) | collective-permute-done | bytes 32800 | tf_op jit(solution)/shard_map/ppermute | solution.py:29
  20.4 0.0 collective-permute-done.8.refs_3_
  20.5 0.1 collective-permute-done.7.refs_2_
  20.5 0.4 %collective-permute-done.6.refs_1_ = f32[64,128]{1,0:T(8,128)S(1)} collective-permute-done((f32[64,128]{1,0:T(8,128)S(1)}, f32[64,128]{1,0:T(8,128)S(1)}, u32[]{:S(2)}, u32[]{:S(2)}) %collective-permute-start.6) | collective-permute-done | bytes 32800 | tf_op jit(solution)/shard_map/ppermute | solution.py:29
  21.0 1.7 %shard_map.64 = (f32[128,64]{1,0:T(8,128)}, bf16[2,2,12,32,256]{4,3,2,1,0:T(8,128)(2,1)}) custom-call(bf16[256,320]{1,0:T(8,128)(2,1)S(1)} %get-tuple-element.10.high_ref, bf16[256,320]{1,0:T(8,128)(2,1)S(1)} %get-tuple-element.11.low_ref, bf16[2,64,3072]{2,1,0:T(8,128)(2,1)S(1)} %get-tuple-element.12.matrix_ref, f32[64,128]{1,0:T(8,128)S(1)} %shard_map.63.base_ref, ...), custom_call_target="tpu_custom_call" | custom-call | tf_op jit(solution)/shard_map/pallas_call | solution.py:205
  (2 shorter events, 0.0 us)
Async XLA Ops:
  2.6 9.7 %collective-permute-start.4 = (f32[64,128]{1,0:T(8,128)S(1)}, f32[64,128]{1,0:T(8,128)S(1)}, u32[]{:S(2)}, u32[]{:S(2)}) collective-permute-start(f32[64,128]{1,0:T(8,128)S(1)} %get-tuple-element.15.source_ref.own_ref), channel_id=1, source_target_pairs={{0,24},{8,16},{16,8},{24,0},{1,25},{9,17},{17,9},{25,1},{2,26},{10... | collective-permute-start | bytes 98312 | tf_op jit(solution)/shard_map/ppermute | solution.py:29
  7.7 5.0 %collective-permute-start.3 = (f32[64,128]{1,0:T(8,128)S(1)}, f32[64,128]{1,0:T(8,128)S(1)}, u32[]{:S(2)}, u32[]{:S(2)}) collective-permute-start(f32[64,128]{1,0:T(8,128)S(1)} %get-tuple-element.15.source_ref.own_ref), channel_id=1, source_target_pairs={{0,6},{2,4},{4,2},{6,0},{1,7},{3,5},{5,3},{7,1},{8,14},{10,12},{12... | collective-permute-start | bytes 98312 | tf_op jit(solution)/shard_map/ppermute | solution.py:29
  10.1 3.9 %collective-permute-start.2 = (f32[64,128]{1,0:T(8,128)S(1)}, f32[64,128]{1,0:T(8,128)S(1)}, u32[]{:S(2)}, u32[]{:S(2)}) collective-permute-start(f32[64,128]{1,0:T(8,128)S(1)} %get-tuple-element.15.source_ref.own_ref), channel_id=1, source_target_pairs={{0,8},{8,0},{16,24},{24,16},{1,9},{9,1},{17,25},{25,17},{2,10},{10... | collective-permute-start | bytes 98312 | tf_op jit(solution)/shard_map/ppermute | solution.py:29
  10.1 3.9 %collective-permute-start.1 = (f32[64,128]{1,0:T(8,128)S(1)}, f32[64,128]{1,0:T(8,128)S(1)}, u32[]{:S(2)}, u32[]{:S(2)}) collective-permute-start(f32[64,128]{1,0:T(8,128)S(1)} %get-tuple-element.15.source_ref.own_ref), channel_id=1, source_target_pairs={{0,2},{2,0},{4,6},{6,4},{1,3},{3,1},{5,7},{7,5},{8,10},{10,8},{12,... | collective-permute-start | bytes 98312 | tf_op jit(solution)/shard_map/ppermute | solution.py:29
  10.7 3.4 %collective-permute-start = (f32[64,128]{1,0:T(8,128)S(1)}, f32[64,128]{1,0:T(8,128)S(1)}, u32[]{:S(2)}, u32[]{:S(2)}) collective-permute-start(f32[64,128]{1,0:T(8,128)S(1)} %get-tuple-element.15.source_ref.own_ref), channel_id=1, source_target_pairs={{0,1},{1,0},{2,3},{3,2},{4,5},{5,4},{6,7},{7,6},{8,9},{9,8},{10,11... | collective-permute-start | bytes 98312 | tf_op jit(solution)/shard_map/ppermute | solution.py:29
  14.4 6.0 %collective-permute-start.9 = (f32[64,128]{1,0:T(8,128)S(1)}, f32[64,128]{1,0:T(8,128)S(1)}, u32[]{:S(2)}, u32[]{:S(2)}) collective-permute-start(f32[64,128]{1,0:T(8,128)S(1)} %shard_map.62.own_ref), channel_id=1, source_target_pairs={{0,24},{8,16},{16,8},{24,0},{1,25},{9,17},{17,9},{25,1},{2,26},{10... | collective-permute-start | bytes 98312 | tf_op jit(solution)/shard_map/ppermute | solution.py:29
  15.4 5.1 %collective-permute-start.8 = (f32[64,128]{1,0:T(8,128)S(1)}, f32[64,128]{1,0:T(8,128)S(1)}, u32[]{:S(2)}, u32[]{:S(2)}) collective-permute-start(f32[64,128]{1,0:T(8,128)S(1)} %shard_map.62.own_ref), channel_id=1, source_target_pairs={{0,6},{2,4},{4,2},{6,0},{1,7},{3,5},{5,3},{7,1},{8,14},{10,12},{12... | collective-permute-start | bytes 98312 | tf_op jit(solution)/shard_map/ppermute | solution.py:29
  16.3 4.3 %collective-permute-start.7 = (f32[64,128]{1,0:T(8,128)S(1)}, f32[64,128]{1,0:T(8,128)S(1)}, u32[]{:S(2)}, u32[]{:S(2)}) collective-permute-start(f32[64,128]{1,0:T(8,128)S(1)} %shard_map.62.own_ref), channel_id=1, source_target_pairs={{0,8},{8,0},{16,24},{24,16},{1,9},{9,1},{17,25},{25,17},{2,10},{10... | collective-permute-start | bytes 98312 | tf_op jit(solution)/shard_map/ppermute | solution.py:29
  17.1 3.9 %collective-permute-start.6 = (f32[64,128]{1,0:T(8,128)S(1)}, f32[64,128]{1,0:T(8,128)S(1)}, u32[]{:S(2)}, u32[]{:S(2)}) collective-permute-start(f32[64,128]{1,0:T(8,128)S(1)} %shard_map.62.own_ref), channel_id=1, source_target_pairs={{0,2},{2,0},{4,6},{6,4},{1,3},{3,1},{5,7},{7,5},{8,10},{10,8},{12,... | collective-permute-start | bytes 98312 | tf_op jit(solution)/shard_map/ppermute | solution.py:29
  18.5 2.4 %collective-permute-start.5 = (f32[64,128]{1,0:T(8,128)S(1)}, f32[64,128]{1,0:T(8,128)S(1)}, u32[]{:S(2)}, u32[]{:S(2)}) collective-permute-start(f32[64,128]{1,0:T(8,128)S(1)} %shard_map.62.own_ref), channel_id=1, source_target_pairs={{0,1},{1,0},{2,3},{3,2},{4,5},{5,4},{6,7},{7,6},{8,9},{9,8},{10,11... | collective-permute-start | bytes 98312 | tf_op jit(solution)/shard_map/ppermute | solution.py:29

commit v9 on v8

--- a/solution.py
+++ b/solution.py
@@ -128,9 +128,7 @@
 def second_kernel(high_ref, low_ref, matrix_ref, base_ref, *refs):
     others, (error_ref, out_ref, error, result, rows, error_sem, sems) = refs[:-7], refs[-7:]
     final = base_ref[...] + 0.5 * summed(high_ref, low_ref, [ref[...] for ref in others])
-    error[...] = final.T
-    copies = [pltpu.make_async_copy(error, error_ref, error_sem)]
-    copies[0].start()
+    copies = []
     half = final.astype(BF16).astype(F32)
     crossed = turned(half)
     for h in range(2):
@@ -145,6 +143,10 @@
             copy = pltpu.make_async_copy(result.at[part], out_ref.at[part], sems.at[t, h])
             copy.start()
             copies.append(copy)
+        if h == 0:
+            error[...] = final.T
+            copies.append(pltpu.make_async_copy(error, error_ref, error_sem))
+            copies[-1].start()
     for copy in copies:
         copy.wait()
 

time: 22.8 us -> 22.8 us (level)
  no operation moved by 1% of the time
where the time goes in v9:
time: 22.8 us; the launch traced here: 22.6 us
  starting transfers between devices  12.2 us (54%)
  Pallas kernels  5.88 us (26%)
  waiting for transfers between devices  3.85 us (17%)
  between operations  0.68 us (3%)
    ppermute x10, starting transfers between devices, received(): lax.ppermute(value, axis, [(i, (i + (1 if i % 2 == order else -1)) % size...  12.2 us
    ppermute x10, waiting for transfers between devices, received(): lax.ppermute(value, axis, [(i, (i + (1 if i % 2 == order else -1)) % size...  3.85 us
    pallas_call x1, Pallas kernels, on_device(): pl.pallas_call(restrict_kernel, out_shape=(vector, jax.ShapeDtypeStruct((...  1.94 us
    pallas_call x1, Pallas kernels, on_device(): pl.pallas_call(second_kernel, out_shape=(jax.ShapeDtypeStruct((128, 64),...  1.67 us
    pallas_call x1, Pallas kernels, on_device(): pl.pallas_call(functools.partial(operator_kernel, moves=moves), out_shape...  1.24 us
    pallas_call x2, Pallas kernels, partly(): pl.pallas_call(functools.partial(own_kernel, weight=weight), out_shape=ve...  0.68 us
  transfers between devices with their start and end apart: 10, of which 5 were waited for; matrix products, arithmetic and copies ran while one was open for 0% of the time, Pallas kernels for 9%

profile of v9, /device:TPU:0, one launch (start us, length us, event | category | flops | bytes accessed | tf_op | source)
XLA Modules:
  0.0 22.6 jit_solution(5734970833566412273)
XLA Ops:
  0.6 1.9 %shard_map.60 = (f32[64,128]{1,0:T(8,128)S(1)}, bf16[2,64,3072]{2,1,0:T(8,128)(2,1)S(1)}) custom-call(s32[32]{0:T(128)} %pick_ref.1, bf16[2,48,2,3072]{3,2,1,0:T(2,128)(2,1)} %bitcast.10, bf16[2,2,12,32,256]{4,3,2,1,0:T(8,128)(2,1)} %bitcast.11), custom_call_target="tpu_custom_call" | custom-call | tf_op jit(solution)/shard_map/pallas_call | solution.py:161
  2.6 5.1 %collective-permute-start.4 = (f32[64,128]{1,0:T(8,128)S(1)}, f32[64,128]{1,0:T(8,128)S(1)}, u32[]{:S(2)}, u32[]{:S(2)}) collective-permute-start(f32[64,128]{1,0:T(8,128)S(1)} %get-tuple-element.15.source_ref.own_ref), channel_id=1, source_target_pairs={{0,24},{8,16},{16,8},{24,0},{1,25},{9,17},{17,9},{25,1},{2,26},{10... | collective-permute-start | bytes 98312 | tf_op jit(solution)/shard_map/ppermute | solution.py:29
  7.7 2.4 %collective-permute-start.3 = (f32[64,128]{1,0:T(8,128)S(1)}, f32[64,128]{1,0:T(8,128)S(1)}, u32[]{:S(2)}, u32[]{:S(2)}) collective-permute-start(f32[64,128]{1,0:T(8,128)S(1)} %get-tuple-element.15.source_ref.own_ref), channel_id=1, source_target_pairs={{0,6},{2,4},{4,2},{6,0},{1,7},{3,5},{5,3},{7,1},{8,14},{10,12},{12... | collective-permute-start | bytes 98312 | tf_op jit(solution)/shard_map/ppermute | solution.py:29
  10.1 0.0 collective-permute-start.2
  10.1 0.5 %collective-permute-start.1 = (f32[64,128]{1,0:T(8,128)S(1)}, f32[64,128]{1,0:T(8,128)S(1)}, u32[]{:S(2)}, u32[]{:S(2)}) collective-permute-start(f32[64,128]{1,0:T(8,128)S(1)} %get-tuple-element.15.source_ref.own_ref), channel_id=1, source_target_pairs={{0,2},{2,0},{4,6},{6,4},{1,3},{3,1},{5,7},{7,5},{8,10},{10,8},{12,... | collective-permute-start | bytes 98312 | tf_op jit(solution)/shard_map/ppermute | solution.py:29
  10.7 0.0 collective-permute-start
  10.7 1.2 %shard_map.59 = (bf16[256,128]{1,0:T(8,128)(2,1)S(1)}, bf16[256,128]{1,0:T(8,128)(2,1)S(1)}, bf16[256,320]{1,0:T(8,128)(2,1)S(1)}, bf16[256,320]{1,0:T(8,128)(2,1)S(1)}) custom-call(f32[4,2,9,64,128]{4,3,2,1,0:T(8,128)} %bitcast.9), custom_call_target="tpu_custom_call" | custom-call | tf_op jit(solution)/shard_map/pallas_call | solution.py:181
  11.9 0.3 %shard_map.61.base_ref = f32[64,128]{1,0:T(8,128)S(1)} custom-call(bf16[256,128]{1,0:T(8,128)(2,1)S(1)} %get-tuple-element.13.high_ref, bf16[256,128]{1,0:T(8,128)(2,1)S(1)} %get-tuple-element.14.low_ref, f32[64,128]{1,0:T(8,128)S(1)} %get-tuple-element.15.source_ref.own_ref, f32[64,128]{1,0:T(8,128)S(1)} %get-tuple-element.15.source_ref.own_ref), custom_call_target="tpu_custom_call" | custom-call | tf_op jit(solution)/shard_map/pallas_call | solution.py:192
  12.3 0.0 collective-permute-done.4.refs_4_
  12.3 0.4 %collective-permute-done.3.refs_3_ = f32[64,128]{1,0:T(8,128)S(1)} collective-permute-done((f32[64,128]{1,0:T(8,128)S(1)}, f32[64,128]{1,0:T(8,128)S(1)}, u32[]{:S(2)}, u32[]{:S(2)}) %collective-permute-start.3) | collective-permute-done | bytes 32800 | tf_op jit(solution)/shard_map/ppermute | solution.py:29
  12.7 1.4 %collective-permute-done.2.refs_2_ = f32[64,128]{1,0:T(8,128)S(1)} collective-permute-done((f32[64,128]{1,0:T(8,128)S(1)}, f32[64,128]{1,0:T(8,128)S(1)}, u32[]{:S(2)}, u32[]{:S(2)}) %collective-permute-start.2) | collective-permute-done | bytes 32800 | tf_op jit(solution)/shard_map/ppermute | solution.py:29
  14.1 0.3 %shard_map.62.own_ref = f32[64,128]{1,0:T(8,128)S(1)} custom-call(bf16[256,320]{1,0:T(8,128)(2,1)S(1)} %get-tuple-element.10.high_ref, bf16[256,320]{1,0:T(8,128)(2,1)S(1)} %get-tuple-element.11.low_ref, f32[64,128]{1,0:T(8,128)S(1)} %shard_map.61.base_ref, f32[64,128]{1,0:T(8,128)S(1)} %collective-permute-done.refs_0_, ...), custom_call_target="tpu_custom_call" | custom-call | tf_op jit(solution)/shard_map/pallas_call | solution.py:200
  14.4 1.0 %collective-permute-start.9 = (f32[64,128]{1,0:T(8,128)S(1)}, f32[64,128]{1,0:T(8,128)S(1)}, u32[]{:S(2)}, u32[]{:S(2)}) collective-permute-start(f32[64,128]{1,0:T(8,128)S(1)} %shard_map.62.own_ref), channel_id=1, source_target_pairs={{0,24},{8,16},{16,8},{24,0},{1,25},{9,17},{17,9},{25,1},{2,26},{10... | collective-permute-start | bytes 98312 | tf_op jit(solution)/shard_map/ppermute | solution.py:29
  15.4 0.9 %collective-permute-start.8 = (f32[64,128]{1,0:T(8,128)S(1)}, f32[64,128]{1,0:T(8,128)S(1)}, u32[]{:S(2)}, u32[]{:S(2)}) collective-permute-start(f32[64,128]{1,0:T(8,128)S(1)} %shard_map.62.own_ref), channel_id=1, source_target_pairs={{0,6},{2,4},{4,2},{6,0},{1,7},{3,5},{5,3},{7,1},{8,14},{10,12},{12... | collective-permute-start | bytes 98312 | tf_op jit(solution)/shard_map/ppermute | solution.py:29
  16.3 0.8 %collective-permute-start.7 = (f32[64,128]{1,0:T(8,128)S(1)}, f32[64,128]{1,0:T(8,128)S(1)}, u32[]{:S(2)}, u32[]{:S(2)}) collective-permute-start(f32[64,128]{1,0:T(8,128)S(1)} %shard_map.62.own_ref), channel_id=1, source_target_pairs={{0,8},{8,0},{16,24},{24,16},{1,9},{9,1},{17,25},{25,17},{2,10},{10... | collective-permute-start | bytes 98312 | tf_op jit(solution)/shard_map/ppermute | solution.py:29
  17.1 1.5 %collective-permute-start.6 = (f32[64,128]{1,0:T(8,128)S(1)}, f32[64,128]{1,0:T(8,128)S(1)}, u32[]{:S(2)}, u32[]{:S(2)}) collective-permute-start(f32[64,128]{1,0:T(8,128)S(1)} %shard_map.62.own_ref), channel_id=1, source_target_pairs={{0,2},{2,0},{4,6},{6,4},{1,3},{3,1},{5,7},{7,5},{8,10},{10,8},{12,... | collective-permute-start | bytes 98312 | tf_op jit(solution)/shard_map/ppermute | solution.py:29
  18.5 0.0 collective-permute-start.5
  18.5 0.3 %shard_map.63.base_ref = f32[64,128]{1,0:T(8,128)S(1)} custom-call(bf16[256,128]{1,0:T(8,128)(2,1)S(1)} %get-tuple-element.13.high_ref, bf16[256,128]{1,0:T(8,128)(2,1)S(1)} %get-tuple-element.14.low_ref, f32[64,128]{1,0:T(8,128)S(1)} %get-tuple-element.15.source_ref.own_ref, f32[64,128]{1,0:T(8,128)S(1)} %shard_map.62.own_ref), custom_call_target="tpu_custom_call" | custom-call | tf_op jit(solution)/shard_map/pallas_call | solution.py:192
  18.9 1.6 %collective-permute-done.9.refs_4_ = f32[64,128]{1,0:T(8,128)S(1)} collective-permute-done((f32[64,128]{1,0:T(8,128)S(1)}, f32[64,128]{1,0:T(8,128)S(1)}, u32[]{:S(2)}, u32[]{:S(2)}) %collective-permute-start.9) | collective-permute-done | bytes 32800 | tf_op jit(solution)/shard_map/ppermute | solution.py:29
  20.4 0.0 collective-permute-done.8.refs_3_
  20.5 0.1 collective-permute-done.7.refs_2_
  20.5 0.4 %collective-permute-done.6.refs_1_ = f32[64,128]{1,0:T(8,128)S(1)} collective-permute-done((f32[64,128]{1,0:T(8,128)S(1)}, f32[64,128]{1,0:T(8,128)S(1)}, u32[]{:S(2)}, u32[]{:S(2)}) %collective-permute-start.6) | collective-permute-done | bytes 32800 | tf_op jit(solution)/shard_map/ppermute | solution.py:29
  21.0 0.0 collective-permute-done.5.refs_0_
  21.0 1.7 %shard_map.64 = (f32[128,64]{1,0:T(8,128)}, bf16[2,2,12,32,256]{4,3,2,1,0:T(8,128)(2,1)}) custom-call(bf16[256,320]{1,0:T(8,128)(2,1)S(1)} %get-tuple-element.10.high_ref, bf16[256,320]{1,0:T(8,128)(2,1)S(1)} %get-tuple-element.11.low_ref, bf16[2,64,3072]{2,1,0:T(8,128)(2,1)S(1)} %get-tuple-element.12.matrix_ref, f32[64,128]{1,0:T(8,128)S(1)} %shard_map.63.base_ref, ...), custom_call_target="tpu_custom_call" | custom-call | tf_op jit(solution)/shard_map/pallas_call | solution.py:207
  (2 shorter events, 0.0 us)
Async XLA Ops:
  2.6 9.7 %collective-permute-start.4 = (f32[64,128]{1,0:T(8,128)S(1)}, f32[64,128]{1,0:T(8,128)S(1)}, u32[]{:S(2)}, u32[]{:S(2)}) collective-permute-start(f32[64,128]{1,0:T(8,128)S(1)} %get-tuple-element.15.source_ref.own_ref), channel_id=1, source_target_pairs={{0,24},{8,16},{16,8},{24,0},{1,25},{9,17},{17,9},{25,1},{2,26},{10... | collective-permute-start | bytes 98312 | tf_op jit(solution)/shard_map/ppermute | solution.py:29
  7.7 5.0 %collective-permute-start.3 = (f32[64,128]{1,0:T(8,128)S(1)}, f32[64,128]{1,0:T(8,128)S(1)}, u32[]{:S(2)}, u32[]{:S(2)}) collective-permute-start(f32[64,128]{1,0:T(8,128)S(1)} %get-tuple-element.15.source_ref.own_ref), channel_id=1, source_target_pairs={{0,6},{2,4},{4,2},{6,0},{1,7},{3,5},{5,3},{7,1},{8,14},{10,12},{12... | collective-permute-start | bytes 98312 | tf_op jit(solution)/shard_map/ppermute | solution.py:29
  10.1 3.9 %collective-permute-start.2 = (f32[64,128]{1,0:T(8,128)S(1)}, f32[64,128]{1,0:T(8,128)S(1)}, u32[]{:S(2)}, u32[]{:S(2)}) collective-permute-start(f32[64,128]{1,0:T(8,128)S(1)} %get-tuple-element.15.source_ref.own_ref), channel_id=1, source_target_pairs={{0,8},{8,0},{16,24},{24,16},{1,9},{9,1},{17,25},{25,17},{2,10},{10... | collective-permute-start | bytes 98312 | tf_op jit(solution)/shard_map/ppermute | solution.py:29
  10.1 3.9 %collective-permute-start.1 = (f32[64,128]{1,0:T(8,128)S(1)}, f32[64,128]{1,0:T(8,128)S(1)}, u32[]{:S(2)}, u32[]{:S(2)}) collective-permute-start(f32[64,128]{1,0:T(8,128)S(1)} %get-tuple-element.15.source_ref.own_ref), channel_id=1, source_target_pairs={{0,2},{2,0},{4,6},{6,4},{1,3},{3,1},{5,7},{7,5},{8,10},{10,8},{12,... | collective-permute-start | bytes 98312 | tf_op jit(solution)/shard_map/ppermute | solution.py:29
  10.7 3.4 %collective-permute-start = (f32[64,128]{1,0:T(8,128)S(1)}, f32[64,128]{1,0:T(8,128)S(1)}, u32[]{:S(2)}, u32[]{:S(2)}) collective-permute-start(f32[64,128]{1,0:T(8,128)S(1)} %get-tuple-element.15.source_ref.own_ref), channel_id=1, source_target_pairs={{0,1},{1,0},{2,3},{3,2},{4,5},{5,4},{6,7},{7,6},{8,9},{9,8},{10,11... | collective-permute-start | bytes 98312 | tf_op jit(solution)/shard_map/ppermute | solution.py:29
  14.4 6.0 %collective-permute-start.9 = (f32[64,128]{1,0:T(8,128)S(1)}, f32[64,128]{1,0:T(8,128)S(1)}, u32[]{:S(2)}, u32[]{:S(2)}) collective-permute-start(f32[64,128]{1,0:T(8,128)S(1)} %shard_map.62.own_ref), channel_id=1, source_target_pairs={{0,24},{8,16},{16,8},{24,0},{1,25},{9,17},{17,9},{25,1},{2,26},{10... | collective-permute-start | bytes 98312 | tf_op jit(solution)/shard_map/ppermute | solution.py:29
  15.4 5.1 %collective-permute-start.8 = (f32[64,128]{1,0:T(8,128)S(1)}, f32[64,128]{1,0:T(8,128)S(1)}, u32[]{:S(2)}, u32[]{:S(2)}) collective-permute-start(f32[64,128]{1,0:T(8,128)S(1)} %shard_map.62.own_ref), channel_id=1, source_target_pairs={{0,6},{2,4},{4,2},{6,0},{1,7},{3,5},{5,3},{7,1},{8,14},{10,12},{12... | collective-permute-start | bytes 98312 | tf_op jit(solution)/shard_map/ppermute | solution.py:29
  16.3 4.3 %collective-permute-start.7 = (f32[64,128]{1,0:T(8,128)S(1)}, f32[64,128]{1,0:T(8,128)S(1)}, u32[]{:S(2)}, u32[]{:S(2)}) collective-permute-start(f32[64,128]{1,0:T(8,128)S(1)} %shard_map.62.own_ref), channel_id=1, source_target_pairs={{0,8},{8,0},{16,24},{24,16},{1,9},{9,1},{17,25},{25,17},{2,10},{10... | collective-permute-start | bytes 98312 | tf_op jit(solution)/shard_map/ppermute | solution.py:29
  17.1 3.9 %collective-permute-start.6 = (f32[64,128]{1,0:T(8,128)S(1)}, f32[64,128]{1,0:T(8,128)S(1)}, u32[]{:S(2)}, u32[]{:S(2)}) collective-permute-start(f32[64,128]{1,0:T(8,128)S(1)} %shard_map.62.own_ref), channel_id=1, source_target_pairs={{0,2},{2,0},{4,6},{6,4},{1,3},{3,1},{5,7},{7,5},{8,10},{10,8},{12,... | collective-permute-start | bytes 98312 | tf_op jit(solution)/shard_map/ppermute | solution.py:29
  18.5 2.4 %collective-permute-start.5 = (f32[64,128]{1,0:T(8,128)S(1)}, f32[64,128]{1,0:T(8,128)S(1)}, u32[]{:S(2)}, u32[]{:S(2)}) collective-permute-start(f32[64,128]{1,0:T(8,128)S(1)} %shard_map.62.own_ref), channel_id=1, source_target_pairs={{0,1},{1,0},{2,3},{3,2},{4,5},{5,4},{6,7},{7,6},{8,9},{9,8},{10,11... | collective-permute-start | bytes 98312 | tf_op jit(solution)/shard_map/ppermute | solution.py:29

commit v10 on v9

--- a/solution.py
+++ b/solution.py
@@ -105,9 +105,9 @@
     stacked = jnp.concatenate(values, axis=0)
     high = stacked.astype(BF16)
     low = (stacked - high.astype(F32)).astype(BF16)
-    product = jnp.dot(high_ref[...], jnp.concatenate([high, low], axis=1), preferred_element_type=F32)
-    product = product[:, :128] + product[:, 128:]
-    product = product + jnp.dot(low_ref[...], high, preferred_element_type=F32)
+    rows = jnp.concatenate([high_ref[...], low_ref[...]], axis=0)
+    product = jnp.dot(rows, jnp.concatenate([high, low], axis=1), preferred_element_type=F32)
+    product = product[:256, :128] + product[:256, 128:] + product[256:, :128]
     early = lax.broadcasted_iota(jnp.int32, (64, 128), 1) < 64
     by_real = jnp.where(early, product[:64], product[64:128])
     by_imag = jnp.where(early, product[128:192], product[192:])

time: 22.8 us -> 23 us (level)
  no operation moved by 1% of the time
where the time goes in v10:
time: 23 us; the launch traced here: 22.8 us
  starting transfers between devices  12.2 us (53%)
  Pallas kernels  6.1 us (27%)
  waiting for transfers between devices  3.83 us (17%)
  between operations  0.68 us (3%)
    ppermute x10, starting transfers between devices, received(): lax.ppermute(value, axis, [(i, (i + (1 if i % 2 == order else -1)) % size...  12.2 us
    ppermute x10, waiting for transfers between devices, received(): lax.ppermute(value, axis, [(i, (i + (1 if i % 2 == order else -1)) % size...  3.83 us
    pallas_call x1, Pallas kernels, on_device(): pl.pallas_call(restrict_kernel, out_shape=(vector, jax.ShapeDtypeStruct((...  1.94 us
    pallas_call x1, Pallas kernels, on_device(): pl.pallas_call(second_kernel, out_shape=(jax.ShapeDtypeStruct((128, 64),...  1.85 us
    pallas_call x1, Pallas kernels, on_device(): pl.pallas_call(functools.partial(operator_kernel, moves=moves), out_shape...  1.24 us
    pallas_call x2, Pallas kernels, partly(): pl.pallas_call(functools.partial(own_kernel, weight=weight), out_shape=ve...  0.71 us
  transfers between devices with their start and end apart: 10, of which 5 were waited for; matrix products, arithmetic and copies ran while one was open for 0% of the time, Pallas kernels for 9%

profile of v10, /device:TPU:0, one launch (start us, length us, event | category | flops | bytes accessed | tf_op | source)
XLA Modules:
  0.0 22.8 jit_solution(14609795549930030649)
XLA Ops:
  0.6 1.9 %shard_map.60 = (f32[64,128]{1,0:T(8,128)S(1)}, bf16[2,64,3072]{2,1,0:T(8,128)(2,1)S(1)}) custom-call(s32[32]{0:T(128)} %pick_ref.1, bf16[2,48,2,3072]{3,2,1,0:T(2,128)(2,1)} %bitcast.10, bf16[2,2,12,32,256]{4,3,2,1,0:T(8,128)(2,1)} %bitcast.11), custom_call_target="tpu_custom_call" | custom-call | tf_op jit(solution)/shard_map/pallas_call | solution.py:161
  2.6 5.1 %collective-permute-start.4 = (f32[64,128]{1,0:T(8,128)S(1)}, f32[64,128]{1,0:T(8,128)S(1)}, u32[]{:S(2)}, u32[]{:S(2)}) collective-permute-start(f32[64,128]{1,0:T(8,128)S(1)} %get-tuple-element.15.source_ref.own_ref), channel_id=1, source_target_pairs={{0,24},{8,16},{16,8},{24,0},{1,25},{9,17},{17,9},{25,1},{2,26},{10... | collective-permute-start | bytes 98312 | tf_op jit(solution)/shard_map/ppermute | solution.py:29
  7.7 2.4 %collective-permute-start.3 = (f32[64,128]{1,0:T(8,128)S(1)}, f32[64,128]{1,0:T(8,128)S(1)}, u32[]{:S(2)}, u32[]{:S(2)}) collective-permute-start(f32[64,128]{1,0:T(8,128)S(1)} %get-tuple-element.15.source_ref.own_ref), channel_id=1, source_target_pairs={{0,6},{2,4},{4,2},{6,0},{1,7},{3,5},{5,3},{7,1},{8,14},{10,12},{12... | collective-permute-start | bytes 98312 | tf_op jit(solution)/shard_map/ppermute | solution.py:29
  10.1 0.5 %collective-permute-start.1 = (f32[64,128]{1,0:T(8,128)S(1)}, f32[64,128]{1,0:T(8,128)S(1)}, u32[]{:S(2)}, u32[]{:S(2)}) collective-permute-start(f32[64,128]{1,0:T(8,128)S(1)} %get-tuple-element.15.source_ref.own_ref), channel_id=1, source_target_pairs={{0,2},{2,0},{4,6},{6,4},{1,3},{3,1},{5,7},{7,5},{8,10},{10,8},{12,... | collective-permute-start | bytes 98312 | tf_op jit(solution)/shard_map/ppermute | solution.py:29
  10.7 0.0 collective-permute-start
  10.7 1.2 %shard_map.59 = (bf16[256,128]{1,0:T(8,128)(2,1)S(1)}, bf16[256,128]{1,0:T(8,128)(2,1)S(1)}, bf16[256,320]{1,0:T(8,128)(2,1)S(1)}, bf16[256,320]{1,0:T(8,128)(2,1)S(1)}) custom-call(f32[4,2,9,64,128]{4,3,2,1,0:T(8,128)} %bitcast.9), custom_call_target="tpu_custom_call" | custom-call | tf_op jit(solution)/shard_map/pallas_call | solution.py:181
  11.9 0.4 %shard_map.61.base_ref = f32[64,128]{1,0:T(8,128)S(1)} custom-call(bf16[256,128]{1,0:T(8,128)(2,1)S(1)} %get-tuple-element.13.high_ref, bf16[256,128]{1,0:T(8,128)(2,1)S(1)} %get-tuple-element.14.low_ref, f32[64,128]{1,0:T(8,128)S(1)} %get-tuple-element.15.source_ref.own_ref, f32[64,128]{1,0:T(8,128)S(1)} %get-tuple-element.15.source_ref.own_ref), custom_call_target="tpu_custom_call" | custom-call | tf_op jit(solution)/shard_map/pallas_call | solution.py:192
  12.3 0.0 collective-permute-done.4.refs_4_
  12.3 0.4 %collective-permute-done.3.refs_3_ = f32[64,128]{1,0:T(8,128)S(1)} collective-permute-done((f32[64,128]{1,0:T(8,128)S(1)}, f32[64,128]{1,0:T(8,128)S(1)}, u32[]{:S(2)}, u32[]{:S(2)}) %collective-permute-start.3) | collective-permute-done | bytes 32800 | tf_op jit(solution)/shard_map/ppermute | solution.py:29
  12.7 1.4 %collective-permute-done.2.refs_2_ = f32[64,128]{1,0:T(8,128)S(1)} collective-permute-done((f32[64,128]{1,0:T(8,128)S(1)}, f32[64,128]{1,0:T(8,128)S(1)}, u32[]{:S(2)}, u32[]{:S(2)}) %collective-permute-start.2) | collective-permute-done | bytes 32800 | tf_op jit(solution)/shard_map/ppermute | solution.py:29
  14.1 0.0 collective-permute-done.1.refs_1_
  14.1 0.0 collective-permute-done.refs_0_
  14.1 0.4 %shard_map.62.own_ref = f32[64,128]{1,0:T(8,128)S(1)} custom-call(bf16[256,320]{1,0:T(8,128)(2,1)S(1)} %get-tuple-element.10.high_ref, bf16[256,320]{1,0:T(8,128)(2,1)S(1)} %get-tuple-element.11.low_ref, f32[64,128]{1,0:T(8,128)S(1)} %shard_map.61.base_ref, f32[64,128]{1,0:T(8,128)S(1)} %collective-permute-done.refs_0_, ...), custom_call_target="tpu_custom_call" | custom-call | tf_op jit(solution)/shard_map/pallas_call | solution.py:200
  14.4 1.0 %collective-permute-start.9 = (f32[64,128]{1,0:T(8,128)S(1)}, f32[64,128]{1,0:T(8,128)S(1)}, u32[]{:S(2)}, u32[]{:S(2)}) collective-permute-start(f32[64,128]{1,0:T(8,128)S(1)} %shard_map.62.own_ref), channel_id=1, source_target_pairs={{0,24},{8,16},{16,8},{24,0},{1,25},{9,17},{17,9},{25,1},{2,26},{10... | collective-permute-start | bytes 98312 | tf_op jit(solution)/shard_map/ppermute | solution.py:29
  15.4 0.9 %collective-permute-start.8 = (f32[64,128]{1,0:T(8,128)S(1)}, f32[64,128]{1,0:T(8,128)S(1)}, u32[]{:S(2)}, u32[]{:S(2)}) collective-permute-start(f32[64,128]{1,0:T(8,128)S(1)} %shard_map.62.own_ref), channel_id=1, source_target_pairs={{0,6},{2,4},{4,2},{6,0},{1,7},{3,5},{5,3},{7,1},{8,14},{10,12},{12... | collective-permute-start | bytes 98312 | tf_op jit(solution)/shard_map/ppermute | solution.py:29
  16.3 0.8 %collective-permute-start.7 = (f32[64,128]{1,0:T(8,128)S(1)}, f32[64,128]{1,0:T(8,128)S(1)}, u32[]{:S(2)}, u32[]{:S(2)}) collective-permute-start(f32[64,128]{1,0:T(8,128)S(1)} %shard_map.62.own_ref), channel_id=1, source_target_pairs={{0,8},{8,0},{16,24},{24,16},{1,9},{9,1},{17,25},{25,17},{2,10},{10... | collective-permute-start | bytes 98312 | tf_op jit(solution)/shard_map/ppermute | solution.py:29
  17.1 1.5 %collective-permute-start.6 = (f32[64,128]{1,0:T(8,128)S(1)}, f32[64,128]{1,0:T(8,128)S(1)}, u32[]{:S(2)}, u32[]{:S(2)}) collective-permute-start(f32[64,128]{1,0:T(8,128)S(1)} %shard_map.62.own_ref), channel_id=1, source_target_pairs={{0,2},{2,0},{4,6},{6,4},{1,3},{3,1},{5,7},{7,5},{8,10},{10,8},{12,... | collective-permute-start | bytes 98312 | tf_op jit(solution)/shard_map/ppermute | solution.py:29
  18.6 0.0 collective-permute-start.5
  18.6 0.4 %shard_map.63.base_ref = f32[64,128]{1,0:T(8,128)S(1)} custom-call(bf16[256,128]{1,0:T(8,128)(2,1)S(1)} %get-tuple-element.13.high_ref, bf16[256,128]{1,0:T(8,128)(2,1)S(1)} %get-tuple-element.14.low_ref, f32[64,128]{1,0:T(8,128)S(1)} %get-tuple-element.15.source_ref.own_ref, f32[64,128]{1,0:T(8,128)S(1)} %shard_map.62.own_ref), custom_call_target="tpu_custom_call" | custom-call | tf_op jit(solution)/shard_map/pallas_call | solution.py:192
  18.9 1.5 %collective-permute-done.9.refs_4_ = f32[64,128]{1,0:T(8,128)S(1)} collective-permute-done((f32[64,128]{1,0:T(8,128)S(1)}, f32[64,128]{1,0:T(8,128)S(1)}, u32[]{:S(2)}, u32[]{:S(2)}) %collective-permute-start.9) | collective-permute-done | bytes 32800 | tf_op jit(solution)/shard_map/ppermute | solution.py:29
  20.5 0.0 collective-permute-done.8.refs_3_
  20.5 0.1 collective-permute-done.7.refs_2_
  20.6 0.4 %collective-permute-done.6.refs_1_ = f32[64,128]{1,0:T(8,128)S(1)} collective-permute-done((f32[64,128]{1,0:T(8,128)S(1)}, f32[64,128]{1,0:T(8,128)S(1)}, u32[]{:S(2)}, u32[]{:S(2)}) %collective-permute-start.6) | collective-permute-done | bytes 32800 | tf_op jit(solution)/shard_map/ppermute | solution.py:29
  21.0 1.8 %shard_map.64 = (f32[128,64]{1,0:T(8,128)}, bf16[2,2,12,32,256]{4,3,2,1,0:T(8,128)(2,1)}) custom-call(bf16[256,320]{1,0:T(8,128)(2,1)S(1)} %get-tuple-element.10.high_ref, bf16[256,320]{1,0:T(8,128)(2,1)S(1)} %get-tuple-element.11.low_ref, bf16[2,64,3072]{2,1,0:T(8,128)(2,1)S(1)} %get-tuple-element.12.matrix_ref, f32[64,128]{1,0:T(8,128)S(1)} %shard_map.63.base_ref, ...), custom_call_target="tpu_custom_call" | custom-call | tf_op jit(solution)/shard_map/pallas_call | solution.py:207
  (2 shorter events, 0.0 us)
Async XLA Ops:
  2.6 9.7 %collective-permute-start.4 = (f32[64,128]{1,0:T(8,128)S(1)}, f32[64,128]{1,0:T(8,128)S(1)}, u32[]{:S(2)}, u32[]{:S(2)}) collective-permute-start(f32[64,128]{1,0:T(8,128)S(1)} %get-tuple-element.15.source_ref.own_ref), channel_id=1, source_target_pairs={{0,24},{8,16},{16,8},{24,0},{1,25},{9,17},{17,9},{25,1},{2,26},{10... | collective-permute-start | bytes 98312 | tf_op jit(solution)/shard_map/ppermute | solution.py:29
  7.7 5.0 %collective-permute-start.3 = (f32[64,128]{1,0:T(8,128)S(1)}, f32[64,128]{1,0:T(8,128)S(1)}, u32[]{:S(2)}, u32[]{:S(2)}) collective-permute-start(f32[64,128]{1,0:T(8,128)S(1)} %get-tuple-element.15.source_ref.own_ref), channel_id=1, source_target_pairs={{0,6},{2,4},{4,2},{6,0},{1,7},{3,5},{5,3},{7,1},{8,14},{10,12},{12... | collective-permute-start | bytes 98312 | tf_op jit(solution)/shard_map/ppermute | solution.py:29
  10.1 3.9 %collective-permute-start.2 = (f32[64,128]{1,0:T(8,128)S(1)}, f32[64,128]{1,0:T(8,128)S(1)}, u32[]{:S(2)}, u32[]{:S(2)}) collective-permute-start(f32[64,128]{1,0:T(8,128)S(1)} %get-tuple-element.15.source_ref.own_ref), channel_id=1, source_target_pairs={{0,8},{8,0},{16,24},{24,16},{1,9},{9,1},{17,25},{25,17},{2,10},{10... | collective-permute-start | bytes 98312 | tf_op jit(solution)/shard_map/ppermute | solution.py:29
  10.1 3.9 %collective-permute-start.1 = (f32[64,128]{1,0:T(8,128)S(1)}, f32[64,128]{1,0:T(8,128)S(1)}, u32[]{:S(2)}, u32[]{:S(2)}) collective-permute-start(f32[64,128]{1,0:T(8,128)S(1)} %get-tuple-element.15.source_ref.own_ref), channel_id=1, source_target_pairs={{0,2},{2,0},{4,6},{6,4},{1,3},{3,1},{5,7},{7,5},{8,10},{10,8},{12,... | collective-permute-start | bytes 98312 | tf_op jit(solution)/shard_map/ppermute | solution.py:29
  10.7 3.4 %collective-permute-start = (f32[64,128]{1,0:T(8,128)S(1)}, f32[64,128]{1,0:T(8,128)S(1)}, u32[]{:S(2)}, u32[]{:S(2)}) collective-permute-start(f32[64,128]{1,0:T(8,128)S(1)} %get-tuple-element.15.source_ref.own_ref), channel_id=1, source_target_pairs={{0,1},{1,0},{2,3},{3,2},{4,5},{5,4},{6,7},{7,6},{8,9},{9,8},{10,11... | collective-permute-start | bytes 98312 | tf_op jit(solution)/shard_map/ppermute | solution.py:29
  14.4 6.0 %collective-permute-start.9 = (f32[64,128]{1,0:T(8,128)S(1)}, f32[64,128]{1,0:T(8,128)S(1)}, u32[]{:S(2)}, u32[]{:S(2)}) collective-permute-start(f32[64,128]{1,0:T(8,128)S(1)} %shard_map.62.own_ref), channel_id=1, source_target_pairs={{0,24},{8,16},{16,8},{24,0},{1,25},{9,17},{17,9},{25,1},{2,26},{10... | collective-permute-start | bytes 98312 | tf_op jit(solution)/shard_map/ppermute | solution.py:29
  15.4 5.1 %collective-permute-start.8 = (f32[64,128]{1,0:T(8,128)S(1)}, f32[64,128]{1,0:T(8,128)S(1)}, u32[]{:S(2)}, u32[]{:S(2)}) collective-permute-start(f32[64,128]{1,0:T(8,128)S(1)} %shard_map.62.own_ref), channel_id=1, source_target_pairs={{0,6},{2,4},{4,2},{6,0},{1,7},{3,5},{5,3},{7,1},{8,14},{10,12},{12... | collective-permute-start | bytes 98312 | tf_op jit(solution)/shard_map/ppermute | solution.py:29
  16.3 4.3 %collective-permute-start.7 = (f32[64,128]{1,0:T(8,128)S(1)}, f32[64,128]{1,0:T(8,128)S(1)}, u32[]{:S(2)}, u32[]{:S(2)}) collective-permute-start(f32[64,128]{1,0:T(8,128)S(1)} %shard_map.62.own_ref), channel_id=1, source_target_pairs={{0,8},{8,0},{16,24},{24,16},{1,9},{9,1},{17,25},{25,17},{2,10},{10... | collective-permute-start | bytes 98312 | tf_op jit(solution)/shard_map/ppermute | solution.py:29
  17.1 3.9 %collective-permute-start.6 = (f32[64,128]{1,0:T(8,128)S(1)}, f32[64,128]{1,0:T(8,128)S(1)}, u32[]{:S(2)}, u32[]{:S(2)}) collective-permute-start(f32[64,128]{1,0:T(8,128)S(1)} %shard_map.62.own_ref), channel_id=1, source_target_pairs={{0,2},{2,0},{4,6},{6,4},{1,3},{3,1},{5,7},{7,5},{8,10},{10,8},{12,... | collective-permute-start | bytes 98312 | tf_op jit(solution)/shard_map/ppermute | solution.py:29
  18.6 2.4 %collective-permute-start.5 = (f32[64,128]{1,0:T(8,128)S(1)}, f32[64,128]{1,0:T(8,128)S(1)}, u32[]{:S(2)}, u32[]{:S(2)}) collective-permute-start(f32[64,128]{1,0:T(8,128)S(1)} %shard_map.62.own_ref), channel_id=1, source_target_pairs={{0,1},{1,0},{2,3},{3,2},{4,5},{5,4},{6,7},{7,6},{8,9},{9,8},{10,11... | collective-permute-start | bytes 98312 | tf_op jit(solution)/shard_map/ppermute | solution.py:29
